TPU v7x, 32 devices: a whole 2x2x4 slice. The times are simulated.
32 devices in a mesh: groups: 2 (over y), row: 8 (over z, x), col: 2 (over core).
Axes of the slice: x: 2, y: 2, z: 4, core: 2. Of those that a mesh axis runs over, the one named last changes fastest.
Arguments:
- concentration: float32 [512, 256, 256], P('groups', 'row', 'col'), parts along dimension 0, may hold values from -6 to 6
- species: int32 [2], P('groups'), parts along dimension 0, may hold values from 0 to 63
- reaction_rates: float32 [64], replicated, may hold values from 0.2 to 0.8
- levels: float32 [64], replicated, may hold values from -1 to 1
- sweep_flags: int32 [2, 3], replicated, may hold values from 0 to 1
- explicit_line: float32 [256, 256], replicated, may hold values from -0.5 to 1.2
- inverse_line: float32 [256, 256], replicated, may hold values from -0.5 to 1.2
- explicit_depth: float32 [256, 256], replicated, may hold values from -0.5 to 1.2
- inverse_depth: float32 [256, 256], replicated, may hold values from -0.5 to 1.2
Outputs:
- advanced: float32 [512, 256, 256], P('groups', 'row', 'col'), parts along dimension 0
There are 2 independent parts, one for each index of `groups`. A program takes and returns all parts, laid end to end along the dimension named above; an argument that names none is the same for every part. Nothing has to cross between parts.
All inputs are finite; a program needn't handle non-finite values.
Results may differ from a plain program's by a relative error of at most 0.00011.
Values sent between devices are 32-bit elements; how exact they have to be, the bound alone decides.
No kernel may reach another device: no remote copies, remote signals or barrier semaphores. Data moves between devices by JAX's collectives and lax.ppermute only.
A program may use at most 64 MiB of HBM per device.

v0:
```python
import functools
import jax
import jax.numpy as jnp
from jax import lax
from jax.experimental import pallas as pl
from jax.experimental.pallas import tpu as pltpu
from jax.sharding import PartitionSpec as P

F32 = jnp.float32
BF16 = jnp.bfloat16
CHUNKS = 2
VMEM_LIMIT = 48 * 1024 * 1024


def split(value):
    high = value.astype(BF16)
    return high, (value - high.astype(F32)).astype(BF16)


def product(left, right):
    dot = functools.partial(jnp.dot, preferred_element_type=F32)
    return dot(left[0], right[0]) + (dot(left[0], right[1]) + dot(left[1], right[0]))


def react(value, kinetics):
    rate, level = kinetics
    return value - rate * jnp.tanh(value - level)


def read_kinetics(species_ref, rates_ref, levels_ref):
    index = species_ref[0]
    return rates_ref[index], levels_ref[index]


def reversal(flag, size):
    rows = lax.broadcasted_iota(jnp.int32, (size, size), 0)
    columns = lax.broadcasted_iota(jnp.int32, (size, size), 1)
    target = jnp.where(flag == 1, size - 1 - rows, rows)
    return jnp.where(columns == target, 1.0, 0.0).astype(BF16)


def combined(inverse, explicit):
    return jnp.dot(inverse, explicit, precision=lax.Precision.HIGHEST, preferred_element_type=F32)


def orient(pieces, flag):
    turn = reversal(flag, pieces[0].shape[0])
    dot = functools.partial(jnp.dot, preferred_element_type=F32)
    return tuple(dot(dot(turn, piece).astype(BF16), turn).astype(BF16) for piece in pieces)


def first_sweep(chunk, species, rates, levels, flags, explicit, inverse, field, out, high, low):
    rows = high.shape[0]

    @pl.when(pl.program_id(0) == 0)
    def _():
        pieces = orient(split(combined(inverse[...], explicit[...])), flags[0, 0])
        high[...] = pieces[0][chunk * rows : (chunk + 1) * rows]
        low[...] = pieces[1][chunk * rows : (chunk + 1) * rows]

    kinetics = read_kinetics(species, rates, levels)
    matrix = (high[...], low[...])
    ranks, each, depth, width = out.shape
    for cell in range(0, depth, 2):
        value = jnp.concatenate([field[:, cell, :], field[:, cell + 1, :]], axis=1)
        result = product(matrix, split(react(value, kinetics)))
        for half in range(2):
            out[:, :, cell + half, :] = result[:, half * width : (half + 1) * width].reshape(
                ranks, each, width
            )


def last_sweep(chunk, species, rates, levels, flags, explicit, inverse, *refs):
    if chunk == 0:
        field, out, high, low = refs
    else:
        field, total, out, high, low = refs
    columns = high.shape[1]

    @pl.when(pl.program_id(0) == 0)
    def _():
        last = flags.shape[0] - 1
        pieces = orient(split(combined(inverse[...], explicit[...])), flags[last, 0])
        high[...] = pieces[0][:, chunk * columns : (chunk + 1) * columns]
        low[...] = pieces[1][:, chunk * columns : (chunk + 1) * columns]

    kinetics = read_kinetics(species, rates, levels)
    matrix = (high[...], low[...])
    ranks, each, depth, width = field.shape
    for cell in range(0, depth, 2):
        value = jnp.concatenate(
            [field[:, :, cell + half, :].reshape(ranks * each, width) for half in range(2)], axis=1
        )
        result = product(matrix, split(react(value, kinetics)))
        for half in range(2):
            part = result[:, half * width : (half + 1) * width]
            if chunk > 0:
                part = part + total[:, cell + half, :]
            out[:, cell + half, :] = part


def prepare(flags, explicit_line, inverse_line, explicit_depth, inverse_depth, high, low):
    line = split(combined(inverse_line[...], explicit_line[...]))
    depth = split(combined(inverse_depth[...], explicit_depth[...]).T)
    for place, (pieces, step, axis_dim) in enumerate(
        [(line, 0, 1), (depth, 0, 2), (depth, 1, 2), (line, 1, 1)]
    ):
        high[place], low[place] = orient(pieces, flags[step, axis_dim])


def plane_sweeps(rows, columns, species, rates, levels, high, low, field, out):
    kinetics = read_kinetics(species, rates, levels)
    each, depth, width = field.shape[1:]
    for cell in range(each):
        value = jnp.concatenate(
            [
                jnp.concatenate([field[r * columns + c, cell] for c in range(columns)], axis=1)
                for r in range(rows)
            ],
            axis=0,
        )
        for place in range(4):
            pieces = split(react(value, kinetics))
            matrix = (high[place], low[place])
            value = product(matrix, pieces) if place in (0, 3) else product(pieces, matrix)
        for r in range(rows):
            for c in range(columns):
                out[r * columns + c, cell] = value[
                    r * depth : (r + 1) * depth, c * width : (c + 1) * width
                ]


SMEM = pl.BlockSpec(memory_space=pltpu.SMEM)
WHOLE = pl.BlockSpec(memory_space=pltpu.VMEM)
PARAMS = pltpu.CompilerParams(vmem_limit_bytes=VMEM_LIMIT)


def cost(cells, length, sweeps, bytes_accessed):
    return pl.CostEstimate(
        flops=6 * cells * length * sweeps, bytes_accessed=bytes_accessed, transcendentals=cells * sweeps
    )


def fast(rows, columns, concentration, species, reaction_rates, levels, sweep_flags,
         explicit_line, inverse_line, explicit_depth, inverse_depth):
    lines, depth, width = concentration.shape
    ranks = rows * columns
    each = lines // ranks // CHUNKS
    block = 8
    kinetic = (species, reaction_rates, levels)
    size = lines * depth * width
    chunk_shape = jax.ShapeDtypeStruct((ranks, each, depth, width), F32)
    share = lines // CHUNKS

    def exchange(value):
        return lax.all_to_all(value, ("row", "col"), split_axis=0, concat_axis=0, tiled=True)

    chunk_spec = pl.BlockSpec((ranks, each, block, width), lambda i: (0, 0, i, 0))
    home_spec = pl.BlockSpec((lines, block, width), lambda i: (0, i, 0))

    def first(chunk):
        return pl.pallas_call(
            functools.partial(first_sweep, chunk),
            grid=(depth // block,),
            in_specs=[SMEM] * 4 + [WHOLE] * 2 + [home_spec],
            out_specs=chunk_spec,
            out_shape=chunk_shape,
            scratch_shapes=[pltpu.VMEM((share, lines), BF16)] * 2,
            compiler_params=PARAMS,
            cost_estimate=cost(size // CHUNKS, lines, 1, 4 * (size + size // CHUNKS)),
            name=f"first_sweep_{chunk}",
        )(*kinetic, sweep_flags, explicit_line, inverse_line, concentration)

    def planes(value, chunk):
        spec = pl.BlockSpec((ranks, 2, depth, width), lambda i: (0, i, 0, 0))
        return pl.pallas_call(
            functools.partial(plane_sweeps, rows, columns),
            grid=(each // 2,),
            in_specs=[SMEM] * 3 + [WHOLE] * 2 + [spec],
            out_specs=spec,
            out_shape=chunk_shape,
            compiler_params=PARAMS,
            cost_estimate=cost(size // CHUNKS, lines, 4, 8 * size // CHUNKS),
            name=f"plane_sweeps_{chunk}",
        )(*kinetic, high, low, value)

    def last(value, total, chunk):
        more = [] if chunk == 0 else [total]
        return pl.pallas_call(
            functools.partial(last_sweep, chunk),
            grid=(depth // block,),
            in_specs=[SMEM] * 4 + [WHOLE] * 2 + [chunk_spec] + [home_spec] * len(more),
            out_specs=home_spec,
            out_shape=jax.ShapeDtypeStruct((lines, depth, width), F32),
            scratch_shapes=[pltpu.VMEM((lines, share), BF16)] * 2,
            compiler_params=PARAMS,
            cost_estimate=cost(size // CHUNKS, lines, 1, 4 * (size + size // CHUNKS)),
            name=f"last_sweep_{chunk}",
        )(*kinetic, sweep_flags, explicit_line, inverse_line, value, *more)

    pieces_shape = jax.ShapeDtypeStruct((4, lines, lines), BF16)
    high, low = pl.pallas_call(
        prepare,
        in_specs=[SMEM] + [WHOLE] * 4,
        out_specs=[WHOLE] * 2,
        out_shape=[pieces_shape] * 2,
        compiler_params=PARAMS,
        cost_estimate=cost(lines * lines, lines, 8, 8 * 4 * lines * lines),
        name="prepare",
    )(sweep_flags, explicit_line, inverse_line, explicit_depth, inverse_depth)

    there = [exchange(first(chunk)) for chunk in range(CHUNKS)]
    back = [exchange(planes(there[chunk], chunk)) for chunk in range(CHUNKS)]
    total = None
    for chunk in range(CHUNKS):
        total = last(back[chunk], total, chunk)
    return total


def oriented(matrix, reflect):
    return jnp.where(reflect == 1, matrix[::-1, ::-1], matrix)


def plain(concentration, species, reaction_rates, levels, sweep_flags,
          explicit_line, inverse_line, explicit_depth, inverse_depth):
    kinetics = (reaction_rates[species[0]], levels[species[0]])
    matmul = functools.partial(jnp.einsum, precision=lax.Precision.HIGHEST)
    line = matmul("ij,jk->ik", inverse_line, explicit_line)
    deep = matmul("ij,jk->ik", inverse_depth, explicit_depth)
    letters = ["ij,jbc->ibc", "ij,ajc->aic", "ij,abj->abi"]

    def sweep(value, step, axis_dim):
        matrix = oriented(deep if axis_dim == 2 else line, sweep_flags[step, axis_dim])
        return matmul(letters[axis_dim], matrix, react(value, kinetics))

    def regroup(value):
        value = lax.all_to_all(value, "row", split_axis=0, concat_axis=1, tiled=True)
        return lax.all_to_all(value, "col", split_axis=0, concat_axis=2, tiled=True)

    def restore(value):
        value = lax.all_to_all(value, "col", split_axis=2, concat_axis=0, tiled=True)
        return lax.all_to_all(value, "row", split_axis=1, concat_axis=0, tiled=True)

    value, home = concentration, True
    for step in range(sweep_flags.shape[0]):
        for axis_dim in [0, 1, 2] if step % 2 == 0 else [2, 1, 0]:
            if home != (axis_dim == 0):
                value = restore(value) if axis_dim == 0 else regroup(value)
                home = axis_dim == 0
            value = sweep(value, step, axis_dim)
    return value if home else restore(value)


def solution(mesh):
    rows, columns = mesh.shape["row"], mesh.shape["col"]

    def on_device(*args):
        lines, depth, width = args[0].shape
        fits = (
            args[4].shape[0] == 2
            and lines % (rows * columns * CHUNKS * 8) == 0
            and depth % 8 == 0
            and width % 128 == 0
            and depth * rows == lines
            and width * columns == args[7].shape[0] == lines
        )
        if fits:
            return fast(rows, columns, *args)
        return plain(*args)

    in_specs = (P("groups", "row", "col"), P("groups"), P(), P(), P(), P(), P(), P(), P())
    return jax.shard_map(
        on_device, mesh=mesh, in_specs=in_specs, out_specs=P("groups", "row", "col"), check_vma=False
    )
```

profile of v0, /device:TPU:17, one launch (start us, length us, event | category | flops | bytes accessed | tf_op | source)
XLA Modules:
  0.0 236.1 jit_solution(18075037492657489476)
XLA Ops:
  0.7 0.0 copy-start
  0.7 0.9 copy-done
  1.6 0.0 copy-start.2
  1.6 0.9 copy-done.2
  2.6 0.0 copy-start.10
  2.6 0.7 copy-done.10
  3.2 0.0 copy-start.12
  3.2 0.7 copy-done.12
  3.9 0.0 copy-start.14
  3.9 0.7 copy-done.14
  4.5 7.8 %first_sweep_0.1 = f32[16,8,32,128]{3,2,1,0:T(8,128)} custom-call(s32[1]{0:T(128)S(6)} %copy.10.species, f32[64]{0:T(128)S(1)} %copy-done.12, f32[64]{0:T(128)S(1)} %copy-done.14, s32[2,3]{1,0:T(2,128)S(1)} %copy-done.10, f32[256,256]{1,0:T(8,128)S(1)} %copy-done, f32[256,256]{1,0:T(8,128)S(1)} %copy-done.2, f32[256,32,128]{2,1,0:T(8,128)} %field.3), custom_call_target="tpu_custom_call" | custom-call | flops 805306368 | bytes 6291456 | tf_op jit(solution)/shard_map/first_sweep_0/pallas_call | solution.py:162
  12.4 0.0 copy-start.13
  12.4 0.0 copy-start.15
  12.4 6.6 %all-to-all-start.2 = ((f32[16,8,32,128]{3,2,1,0:T(8,128)}), f32[16,8,32,128]{3,2,1,0:T(8,128)S(1)}, u32[]{:S(2)}, u32[]{:S(2)}) async-start(f32[16,8,32,128]{3,2,1,0:T(8,128)} %first_sweep_0.1), calls=%async_computation.2 | async-start | bytes 4194304 | tf_op jit(solution)/shard_map/all_to_all | solution.py:156
  19.0 0.0 copy-done.1
  19.0 0.0 copy-done.3
  19.1 0.0 copy-done.11
  19.1 0.0 copy-done.13
  19.1 0.0 copy-done.15
  19.1 7.8 %first_sweep_1.1 = f32[16,8,32,128]{3,2,1,0:T(8,128)} custom-call(s32[1]{0:T(128)S(6)} %copy.10.species, f32[64]{0:T(128)S(1)} %copy-done.13, f32[64]{0:T(128)S(1)} %copy-done.15, s32[2,3]{1,0:T(2,128)S(1)} %copy-done.11, f32[256,256]{1,0:T(8,128)S(1)} %copy-done.1, f32[256,256]{1,0:T(8,128)S(1)} %copy-done.3, f32[256,32,128]{2,1,0:T(8,128)} %field.3), custom_call_target="tpu_custom_call" | custom-call | flops 805306368 | bytes 6291456 | tf_op jit(solution)/shard_map/first_sweep_1/pallas_call | solution.py:162
  26.9 39.3 %all-to-all-done.2.field = f32[16,8,32,128]{3,2,1,0:T(8,128)S(1)} async-done(((f32[16,8,32,128]{3,2,1,0:T(8,128)}), f32[16,8,32,128]{3,2,1,0:T(8,128)S(1)}, u32[]{:S(2)}, u32[]{:S(2)}) %all-to-all-start.2) | async-done | bytes 2097184 | tf_op jit(solution)/shard_map/all_to_all | solution.py:156
  66.2 1.4 copy-done.6
  67.5 5.2 %all-to-all-start = ((f32[16,8,32,128]{3,2,1,0:T(8,128)}), f32[16,8,32,128]{3,2,1,0:T(8,128)S(1)}, u32[]{:S(2)}, u32[]{:S(2)}) async-start(f32[16,8,32,128]{3,2,1,0:T(8,128)} %first_sweep_1.1), calls=%async_computation | async-start | bytes 4194304 | tf_op jit(solution)/shard_map/all_to_all | solution.py:156
  72.7 0.0 copy-done.16
  72.7 0.0 copy-done.17
  72.7 0.0 copy-start.7
  72.7 2.0 prepare.1
  74.8 0.0 copy-done.7
  74.8 9.0 %plane_sweeps_0.1 = f32[16,8,32,128]{3,2,1,0:T(8,128)S(1)} custom-call(s32[1]{0:T(128)S(6)} %copy.10.species, f32[64]{0:T(128)S(1)} %copy-done.13, f32[64]{0:T(128)S(1)} %copy-done.15, bf16[4,256,256]{2,1,0:T(8,128)(2,1)S(1)} %get-tuple-element.7.high, bf16[4,256,256]{2,1,0:T(8,128)(2,1)S(1)} %get-tuple-element.8.low, f32[16,8,32,128]{3,2,1,0:T(8,128)S(1)} %copy-done.7), custom_call_target="tpu_custom_call" | custom-call | flops 3221225472 | bytes 4194304 | tf_op jit(solution)/shard_map/plane_sweeps_0/pallas_call | solution.py:176
  83.7 0.0 copy-start.8
  83.8 1.3 copy-done.8
  85.1 0.8 copy-done.18
  85.9 0.8 copy-done.20
  86.7 33.2 %all-to-all-done.field = f32[16,8,32,128]{3,2,1,0:T(8,128)S(1)} async-done(((f32[16,8,32,128]{3,2,1,0:T(8,128)}), f32[16,8,32,128]{3,2,1,0:T(8,128)S(1)}, u32[]{:S(2)}, u32[]{:S(2)}) %all-to-all-start) | async-done | bytes 2097184 | tf_op jit(solution)/shard_map/all_to_all | solution.py:156
  119.9 1.3 copy-done.4
  121.2 5.3 %all-to-all-start.3 = ((f32[16,8,32,128]{3,2,1,0:T(8,128)}), f32[16,8,32,128]{3,2,1,0:T(8,128)S(1)}, u32[]{:S(2)}, u32[]{:S(2)}) async-start(f32[16,8,32,128]{3,2,1,0:T(8,128)} %copy-done.8), calls=%async_computation.3 | async-start | bytes 4194304 | tf_op jit(solution)/shard_map/all_to_all | solution.py:156
  126.5 0.0 copy-done.19
  126.5 0.0 copy-start.5
  126.5 1.6 copy-done.5
  128.1 1.0 copy-done.21
  129.1 9.0 %plane_sweeps_1.1 = f32[16,8,32,128]{3,2,1,0:T(8,128)S(1)} custom-call(s32[1]{0:T(128)S(6)} %copy.10.species, f32[64]{0:T(128)S(1)} %copy-done.13, f32[64]{0:T(128)S(1)} %copy-done.15, bf16[4,256,256]{2,1,0:T(8,128)(2,1)S(1)} %copy-done.19, bf16[4,256,256]{2,1,0:T(8,128)(2,1)S(1)} %copy-done.21, f32[16,8,32,128]{3,2,1,0:T(8,128)S(1)} %copy-done.5), custom_call_target="tpu_custom_call" | custom-call | flops 3221225472 | bytes 4194304 | tf_op jit(solution)/shard_map/plane_sweeps_1/pallas_call | solution.py:176
  138.1 0.0 copy-start.9
  138.1 1.3 copy-done.9
  139.4 34.2 %all-to-all-done.3.refs_0_ = f32[16,8,32,128]{3,2,1,0:T(8,128)S(1)} async-done(((f32[16,8,32,128]{3,2,1,0:T(8,128)}), f32[16,8,32,128]{3,2,1,0:T(8,128)S(1)}, u32[]{:S(2)}, u32[]{:S(2)}) %all-to-all-start.3) | async-done | bytes 2097184 | tf_op jit(solution)/shard_map/all_to_all | solution.py:156
  173.6 5.2 %all-to-all-start.1 = ((f32[16,8,32,128]{3,2,1,0:T(8,128)}), f32[16,8,32,128]{3,2,1,0:T(8,128)}, u32[]{:S(2)}, u32[]{:S(2)}) async-start(f32[16,8,32,128]{3,2,1,0:T(8,128)} %copy-done.9), calls=%async_computation.1 | async-start | bytes 4194304 | tf_op jit(solution)/shard_map/all_to_all | solution.py:156
  178.8 7.1 %last_sweep_0.1.refs_1_ = f32[256,32,128]{2,1,0:T(8,128)} custom-call(s32[1]{0:T(128)S(6)} %copy.10.species, f32[64]{0:T(128)S(1)} %copy-done.13, f32[64]{0:T(128)S(1)} %copy-done.15, s32[2,3]{1,0:T(2,128)S(1)} %copy-done.11, f32[256,256]{1,0:T(8,128)S(1)} %copy-done.1, f32[256,256]{1,0:T(8,128)S(1)} %copy-done.3, f32[16,8,32,128]{3,2,1,0:T(8,128)S(1)} %all-to-all-done.3.refs_0_), custom_call_target="tpu_custom_call" | custom-call | flops 805306368 | bytes 6291456 | tf_op jit(solution)/shard_map/last_sweep_0/pallas_call | solution.py:189
  186.0 40.1 %all-to-all-done.1.refs_0_ = f32[16,8,32,128]{3,2,1,0:T(8,128)} async-done(((f32[16,8,32,128]{3,2,1,0:T(8,128)}), f32[16,8,32,128]{3,2,1,0:T(8,128)}, u32[]{:S(2)}, u32[]{:S(2)}) %all-to-all-start.1) | async-done | bytes 2097184 | tf_op jit(solution)/shard_map/all_to_all | solution.py:156
  226.1 10.0 %last_sweep_1.1 = f32[256,32,128]{2,1,0:T(8,128)} custom-call(s32[1]{0:T(128)S(6)} %copy.10.species, f32[64]{0:T(128)S(1)} %copy-done.13, f32[64]{0:T(128)S(1)} %copy-done.15, s32[2,3]{1,0:T(2,128)S(1)} %copy-done.11, f32[256,256]{1,0:T(8,128)S(1)} %copy-done.1, f32[256,256]{1,0:T(8,128)S(1)} %copy-done.3, f32[16,8,32,128]{3,2,1,0:T(8,128)} %all-to-all-done.1.refs_0_, ...), custom_call_target="tpu_custom_call" | custom-call | flops 805306368 | bytes 6291456 | tf_op jit(solution)/shard_map/last_sweep_1/pallas_call | solution.py:189
  (11 shorter events, 0.0 us)
Async XLA Ops:
  0.7 1.0 copy-start
  1.6 0.9 copy-start.2
  2.6 0.7 copy-start.10
  3.2 0.7 copy-start.12
  3.9 0.7 copy-start.14
  12.4 6.6 %copy-start.1 = (f32[256,256]{1,0:T(8,128)S(1)}, f32[256,256]{1,0:T(8,128)}, u32[]{:S(2)}) copy-start(f32[256,256]{1,0:T(8,128)} %explicit.7) | copy-start | bytes 786436
  12.4 6.7 %copy-start.3 = (f32[256,256]{1,0:T(8,128)S(1)}, f32[256,256]{1,0:T(8,128)}, u32[]{:S(2)}) copy-start(f32[256,256]{1,0:T(8,128)} %inverse.7) | copy-start | bytes 786436
  12.4 6.7 %copy-start.11 = (s32[2,3]{1,0:T(2,128)S(1)}, s32[2,3]{1,0:T(2,128)}, u32[]{:S(2)}) copy-start(s32[2,3]{1,0:T(2,128)} %flags.9) | copy-start | bytes 76
  12.4 6.7 %copy-start.13 = (f32[64]{0:T(128)S(1)}, f32[64]{0:T(128)}, u32[]{:S(2)}) copy-start(f32[64]{0:T(128)} %rates.11) | copy-start | bytes 772
  12.4 6.7 %copy-start.15 = (f32[64]{0:T(128)S(1)}, f32[64]{0:T(128)}, u32[]{:S(2)}) copy-start(f32[64]{0:T(128)} %levels.11) | copy-start | bytes 772
  12.4 53.8 %all-to-all-start.2 = ((f32[16,8,32,128]{3,2,1,0:T(8,128)}), f32[16,8,32,128]{3,2,1,0:T(8,128)S(1)}, u32[]{:S(2)}, u32[]{:S(2)}) async-start(f32[16,8,32,128]{3,2,1,0:T(8,128)} %first_sweep_0.1), calls=%async_computation.2 | async-start | bytes 4194304 | tf_op jit(solution)/shard_map/all_to_all | solution.py:156
  26.9 45.8 %copy-start.16 = (f32[256,256]{1,0:T(8,128)S(1)}, f32[256,256]{1,0:T(8,128)}, u32[]{:S(2)}) copy-start(f32[256,256]{1,0:T(8,128)} %explicit_depth.1) | copy-start | bytes 786436
  26.9 45.8 %copy-start.17 = (f32[256,256]{1,0:T(8,128)S(1)}, f32[256,256]{1,0:T(8,128)}, u32[]{:S(2)}) copy-start(f32[256,256]{1,0:T(8,128)} %inverse_depth.1) | copy-start | bytes 786436
  66.2 1.4 copy-start.6
  67.5 52.3 %all-to-all-start = ((f32[16,8,32,128]{3,2,1,0:T(8,128)}), f32[16,8,32,128]{3,2,1,0:T(8,128)S(1)}, u32[]{:S(2)}, u32[]{:S(2)}) async-start(f32[16,8,32,128]{3,2,1,0:T(8,128)} %first_sweep_1.1), calls=%async_computation | async-start | bytes 4194304 | tf_op jit(solution)/shard_map/all_to_all | solution.py:156
  72.7 2.0 copy-start.7
  83.7 1.4 copy-start.8
  85.1 0.8 copy-start.18
  85.9 0.8 copy-start.20
  119.9 1.3 copy-start.4
  121.2 5.3 %copy-start.19 = (bf16[4,256,256]{2,1,0:T(8,128)(2,1)S(1)}, bf16[4,256,256]{2,1,0:T(8,128)(2,1)}, u32[]{:S(2)}) copy-start(bf16[4,256,256]{2,1,0:T(8,128)(2,1)} %copy-done.18) | copy-start | bytes 1572868
  121.2 52.5 %all-to-all-start.3 = ((f32[16,8,32,128]{3,2,1,0:T(8,128)}), f32[16,8,32,128]{3,2,1,0:T(8,128)S(1)}, u32[]{:S(2)}, u32[]{:S(2)}) async-start(f32[16,8,32,128]{3,2,1,0:T(8,128)} %copy-done.8), calls=%async_computation.3 | async-start | bytes 4194304 | tf_op jit(solution)/shard_map/all_to_all | solution.py:156
  126.5 1.6 copy-start.5
  128.1 1.0 copy-start.21
  138.1 1.3 copy-start.9
  173.6 52.4 %all-to-all-start.1 = ((f32[16,8,32,128]{3,2,1,0:T(8,128)}), f32[16,8,32,128]{3,2,1,0:T(8,128)}, u32[]{:S(2)}, u32[]{:S(2)}) async-start(f32[16,8,32,128]{3,2,1,0:T(8,128)} %copy-done.9), calls=%async_computation.1 | async-start | bytes 4194304 | tf_op jit(solution)/shard_map/all_to_all | solution.py:156
where the time goes:
time: 237 us; the launch traced here: 236 us
  waiting for transfers between devices  147 us (62%)
  Pallas kernels  52.7 us (22%)
  starting transfers between devices  22.3 us (9%)
  local copies, waits for them, and re-layouts  13.5 us (6%)
    all_to_all x4, waiting for transfers between devices, exchange(): lax.all_to_all(value, ('row', 'col'), split_axis=0, concat_axis=0, tiled=...  147 us
    all_to_all x4, starting transfers between devices, exchange(): lax.all_to_all(value, ('row', 'col'), split_axis=0, concat_axis=0, tiled=...  22.3 us
    pallas_call x2, Pallas kernels, planes(): pl.pallas_call(functools.partial(plane_sweeps, rows, columns), grid=(each...  17.9 us
    pallas_call x2, Pallas kernels, last(): pl.pallas_call(functools.partial(last_sweep, chunk), grid=(depth // block...  17.1 us
    pallas_call x2, Pallas kernels, first(): pl.pallas_call(functools.partial(first_sweep, chunk), grid=(depth // bloc...  15.7 us
    unnamed x44, local copies, waits for them, and re-layouts  13.5 us
  transfers between devices with their start and end apart: 4, of which 4 were waited for; matrix products, arithmetic and copies ran while one was open for 0% of the time, Pallas kernels for 15%

commit v1 on v0

v1 whole, which is shorter than its diff:
```python
import functools
import jax
import jax.numpy as jnp
from jax import lax
from jax.experimental import pallas as pl
from jax.experimental.pallas import tpu as pltpu
from jax.sharding import PartitionSpec as P

F32 = jnp.float32
BF16 = jnp.bfloat16
CHUNKS = 2
BLOCK = 8
VMEM_LIMIT = 32 * 1024 * 1024
FIRST_LIMIT = 60 * 1024 * 1024


def split(value):
    high = value.astype(BF16)
    return high, (value - high.astype(F32)).astype(BF16)


def product(left, right):
    dot = functools.partial(jnp.dot, preferred_element_type=F32)
    return dot(left[0], right[0]) + (dot(left[0], right[1]) + dot(left[1], right[0]))


def react(value, kinetics):
    rate, level = kinetics
    return value - rate * jnp.tanh(value - level)


def read_kinetics(species_ref, rates_ref, levels_ref):
    index = species_ref[0]
    return rates_ref[index], levels_ref[index]


def relative(index, block, own):
    return ((index // block) ^ own) * block + index % block


def picker(shape, along, source, flag, length):
    wanted = source(lax.broadcasted_iota(jnp.int32, shape, along))
    wanted = jnp.where(flag == 1, length - 1 - wanted, wanted)
    return jnp.where(lax.broadcasted_iota(jnp.int32, shape, 1 - along) == wanted, 1.0, 0.0).astype(BF16)


def combined(inverse, explicit):
    return jnp.dot(inverse, explicit, precision=lax.Precision.HIGHEST, preferred_element_type=F32)


def rearrange(pieces, rows, columns):
    dot = functools.partial(jnp.dot, preferred_element_type=F32)
    return tuple(dot(dot(rows, piece).astype(BF16), columns).astype(BF16) for piece in pieces)


def sending_order(ranks):
    half = ranks // 2
    order = []
    for index in range(half):
        order.append(half + index)
        order += [half - 1 - near for near in range(half - 1) if near - near // 5 == index]
    return order + [0]


def by_place(refs):
    order = sending_order(len(refs))
    return [refs[order.index(place)] for place in range(len(refs))]


def position():
    return lax.axis_index("row"), lax.axis_index("col")


def first_sweep(chunk, columns, species, rates, levels, flags, explicit, inverse, field, *refs):
    blocks = by_place(refs[:-5])
    held, matrices, high, low, done = refs[-5:]
    ranks = len(blocks)
    depth, each, width = blocks[0].shape
    row, column = position()
    own = row * columns + column

    step, steps = pl.program_id(0), held.shape[0]

    def arrival(index):
        part = field.at[:, pl.ds(index * depth, depth), :]
        return pltpu.make_async_copy(part, held.at[index], done.at[index])

    @pl.when(step == 0)
    def _():
        copies = [
            pltpu.make_async_copy(source, matrices.at[index], done.at[steps + index])
            for index, source in enumerate((inverse, explicit))
        ]
        for copy in copies:
            copy.start()
        for index in range(steps):
            arrival(index).start()
        for copy in copies:
            copy.wait()
        share, length = high.shape
        pieces = split(combined(matrices[0], matrices[1]))
        flag = flags[0, 0]
        high[...], low[...] = rearrange(
            pieces,
            picker((share, length), 0, lambda i: chunk * share + relative(i, each, own), flag, length),
            picker((length, length), 1, lambda i: i, flag, length),
        )

    arrival(step).wait()
    kinetics = read_kinetics(species, rates, levels)
    matrix = (high[...], low[...])
    for cell in range(0, depth, 2):
        value = jnp.concatenate([held[step, :, cell, :], held[step, :, cell + 1, :]], axis=1)
        result = product(matrix, split(react(value, kinetics)))
        for half in range(2):
            part = result[:, half * width : (half + 1) * width].reshape(ranks, each, width)
            for place in range(ranks):
                blocks[place][cell + half] = part[place]


def last_sweep(chunk, columns, ranks, species, rates, levels, flags, explicit, inverse, *refs):
    blocks, refs = by_place(refs[:ranks]), refs[ranks:]
    total = refs[0] if chunk > 0 else None
    out, high, low = refs[-3:]
    each, width = blocks[0].shape[1:]
    depth = out.shape[1] if chunk > 0 else out.shape[0]
    first = pl.program_id(0) * depth
    row, column = position()
    own = row * columns + column

    @pl.when(pl.program_id(0) == 0)
    def _():
        length, share = high.shape
        flag = flags[flags.shape[0] - 1, 0]
        pieces = split(combined(inverse[...], explicit[...]))
        high[...], low[...] = rearrange(
            pieces,
            picker((length, length), 0, lambda i: i, flag, length),
            picker((length, share), 1, lambda i: chunk * share + relative(i, each, own), flag, length),
        )

    kinetics = read_kinetics(species, rates, levels)
    matrix = (high[...], low[...])
    for cell in range(0, depth, 2):
        value = jnp.concatenate(
            [
                jnp.concatenate([block[first + cell + half] for block in blocks], axis=0)
                for half in range(2)
            ],
            axis=1,
        )
        result = product(matrix, split(react(value, kinetics)))
        for half in range(2):
            part = result[:, half * width : (half + 1) * width]
            if chunk > 0:
                out[:, cell + half, :] = part + total[first + cell + half]
            else:
                out[cell + half] = part


def prepare(depth, width, flags, explicit_line, inverse_line, explicit_depth, inverse_depth, high, low):
    row, column = position()
    line = split(combined(inverse_line[...], explicit_line[...]))
    deep = split(combined(inverse_depth[...], explicit_depth[...]).T)
    for place, (pieces, step, axis_dim) in enumerate(
        [(line, 0, 1), (deep, 0, 2), (deep, 1, 2), (line, 1, 1)]
    ):
        own, block = (row, depth) if axis_dim == 1 else (column, width)
        shape = pieces[0].shape
        flag = flags[step, axis_dim]
        high[place], low[place] = rearrange(
            pieces,
            *[picker(shape, along, lambda i: relative(i, block, own), flag, shape[0]) for along in range(2)],
        )


def plane_sweeps(columns, species, rates, levels, high, low, *refs):
    ranks = len(refs) // 2
    blocks, outs = by_place(refs[:ranks]), by_place(refs[ranks:])
    depth, each, width = blocks[0].shape
    rows = ranks // columns
    kinetics = read_kinetics(species, rates, levels)
    for cell in range(each):
        value = jnp.concatenate(
            [
                jnp.concatenate([blocks[r * columns + c][:, cell, :] for c in range(columns)], axis=1)
                for r in range(rows)
            ],
            axis=0,
        )
        for place in range(4):
            pieces = split(react(value, kinetics))
            matrix = (high[place], low[place])
            value = product(matrix, pieces) if place in (0, 3) else product(pieces, matrix)
        for place in range(ranks):
            r, c = place // columns, place % columns
            outs[place][:, cell, :] = value[r * depth : (r + 1) * depth, c * width : (c + 1) * width]


PARAMS = pltpu.CompilerParams(vmem_limit_bytes=VMEM_LIMIT)
VMEM = pl.BlockSpec(memory_space=pltpu.VMEM)


def scalars(shape):
    return pl.BlockSpec(shape, lambda i: (0,) * len(shape), memory_space=pltpu.SMEM)


def whole(shape):
    return pl.BlockSpec(shape, lambda i: (0,) * len(shape))


def cost(cells, length, sweeps, bytes_accessed):
    return pl.CostEstimate(
        flops=6 * cells * length * sweeps, bytes_accessed=bytes_accessed, transcendentals=cells * sweeps
    )


def fast(rows, columns, concentration, species, reaction_rates, levels, sweep_flags,
         explicit_line, inverse_line, explicit_depth, inverse_depth):
    lines, depth, width = concentration.shape
    ranks = rows * columns
    share = lines // CHUNKS
    each = share // ranks
    size = lines * depth * width
    kinetic = (species, reaction_rates, levels)
    kinetic_specs = [scalars(array.shape) for array in kinetic]
    flags_spec = scalars(sweep_flags.shape)
    matrix_spec = whole((lines, lines))
    home_spec = pl.BlockSpec((lines, BLOCK, width), lambda i: (0, i, 0))
    chunk_shapes = [jax.ShapeDtypeStruct((depth, each, width), F32)] * ranks
    depth_specs = [pl.BlockSpec((BLOCK, each, width), lambda i: (i, 0, 0))] * ranks
    plane_specs = [VMEM] * ranks

    def exchange(blocks):
        return [
            lax.ppermute(block, ("row", "col"), [(i, i ^ place) for i in range(ranks)]) if place else block
            for place, block in zip(sending_order(ranks), blocks)
        ]

    def first(chunk):
        return pl.pallas_call(
            functools.partial(first_sweep, chunk, columns),
            grid=(depth // BLOCK,),
            in_specs=kinetic_specs + [flags_spec] + [pl.BlockSpec(memory_space=pl.ANY)] * 3,
            out_specs=depth_specs,
            out_shape=chunk_shapes,
            scratch_shapes=[
                pltpu.VMEM((depth // BLOCK, lines, BLOCK, width), F32),
                pltpu.VMEM((2, lines, lines), F32),
                pltpu.VMEM((share, lines), BF16),
                pltpu.VMEM((share, lines), BF16),
                pltpu.SemaphoreType.DMA((depth // BLOCK + 2,)),
            ],
            compiler_params=pltpu.CompilerParams(vmem_limit_bytes=FIRST_LIMIT),
            cost_estimate=cost(size // CHUNKS, lines, 1, 4 * (size + size // CHUNKS)),
            name=f"first_sweep_{chunk}",
        )(*kinetic, sweep_flags, explicit_line, inverse_line, concentration)

    def planes(blocks, chunk):
        return pl.pallas_call(
            functools.partial(plane_sweeps, columns),
            grid=(1,),
            in_specs=kinetic_specs + [whole((4, lines, lines))] * 2 + plane_specs,
            out_specs=plane_specs,
            out_shape=chunk_shapes,
            compiler_params=PARAMS,
            cost_estimate=cost(size // CHUNKS, lines, 4, 8 * size // CHUNKS),
            name=f"plane_sweeps_{chunk}",
        )(*kinetic, high, low, *blocks)

    def last(blocks, total, chunk):
        more = [] if chunk == 0 else [total]
        return pl.pallas_call(
            functools.partial(last_sweep, chunk, columns, ranks),
            grid=(depth // BLOCK,),
            in_specs=kinetic_specs + [flags_spec] + [matrix_spec] * 2 + [VMEM] * ranks + [VMEM] * len(more),
            out_specs=home_spec if more else pl.BlockSpec((BLOCK, lines, width), lambda i: (i, 0, 0)),
            out_shape=jax.ShapeDtypeStruct((lines, depth, width) if more else (depth, lines, width), F32),
            scratch_shapes=[pltpu.VMEM((lines, share), BF16)] * 2,
            compiler_params=PARAMS,
            cost_estimate=cost(size // CHUNKS, lines, 1, 4 * (size + size // CHUNKS)),
            name=f"last_sweep_{chunk}",
        )(*kinetic, sweep_flags, explicit_line, inverse_line, *blocks, *more)

    pieces_shape = jax.ShapeDtypeStruct((4, lines, lines), BF16)
    high, low = pl.pallas_call(
        functools.partial(prepare, depth, width),
        grid=(1,),
        in_specs=[flags_spec] + [matrix_spec] * 4,
        out_specs=[whole((4, lines, lines))] * 2,
        out_shape=[pieces_shape] * 2,
        compiler_params=PARAMS,
        cost_estimate=cost(lines * lines, lines, 8, 8 * 4 * lines * lines),
        name="prepare",
    )(sweep_flags, explicit_line, inverse_line, explicit_depth, inverse_depth)

    there = [exchange(first(chunk)) for chunk in range(CHUNKS)]
    back = [exchange(planes(there[chunk], chunk)) for chunk in range(CHUNKS)]
    total = None
    for chunk in range(CHUNKS):
        total = last(back[chunk], total, chunk)
    return total


def oriented(matrix, reflect):
    return jnp.where(reflect == 1, matrix[::-1, ::-1], matrix)


def plain(concentration, species, reaction_rates, levels, sweep_flags,
          explicit_line, inverse_line, explicit_depth, inverse_depth):
    kinetics = (reaction_rates[species[0]], levels[species[0]])
    matmul = functools.partial(jnp.einsum, precision=lax.Precision.HIGHEST)
    line = matmul("ij,jk->ik", inverse_line, explicit_line)
    deep = matmul("ij,jk->ik", inverse_depth, explicit_depth)
    letters = ["ij,jbc->ibc", "ij,ajc->aic", "ij,abj->abi"]

    def sweep(value, step, axis_dim):
        matrix = oriented(deep if axis_dim == 2 else line, sweep_flags[step, axis_dim])
        return matmul(letters[axis_dim], matrix, react(value, kinetics))

    def regroup(value):
        value = lax.all_to_all(value, "row", split_axis=0, concat_axis=1, tiled=True)
        return lax.all_to_all(value, "col", split_axis=0, concat_axis=2, tiled=True)

    def restore(value):
        value = lax.all_to_all(value, "col", split_axis=2, concat_axis=0, tiled=True)
        return lax.all_to_all(value, "row", split_axis=1, concat_axis=0, tiled=True)

    value, home = concentration, True
    for step in range(sweep_flags.shape[0]):
        for axis_dim in [0, 1, 2] if step % 2 == 0 else [2, 1, 0]:
            if home != (axis_dim == 0):
                value = restore(value) if axis_dim == 0 else regroup(value)
                home = axis_dim == 0
            value = sweep(value, step, axis_dim)
    return value if home else restore(value)


def solution(mesh):
    rows, columns = mesh.shape["row"], mesh.shape["col"]
    ranks = rows * columns

    def on_device(*args):
        lines, depth, width = args[0].shape
        fits = (
            args[4].shape[0] == 2
            and ranks & (ranks - 1) == 0
            and ranks >= 2
            and lines % (ranks * CHUNKS * 8) == 0
            and depth % BLOCK == 0
            and width % 128 == 0
            and depth * rows == lines
            and width * columns == args[7].shape[0] == lines
        )
        if fits:
            return fast(rows, columns, *args)
        return plain(*args)

    in_specs = (P("groups", "row", "col"), P("groups"), P(), P(), P(), P(), P(), P(), P())
    return jax.shard_map(
        on_device, mesh=mesh, in_specs=in_specs, out_specs=P("groups", "row", "col"), check_vma=False
    )
```

time: 237 us -> 204 us (0.86)
  waiting for transfers between devices: 147 us -> 47 us
  starting transfers between devices: 22.3 us -> 112 us
  local copies, waits for them, and re-layouts: 13.5 us -> 0.05 us
  Pallas kernels: 52.7 us -> 44.4 us
    all_to_all x4 -> x0, waiting for transfers between devices: 147 us -> none  [exchange(): lax.all_to_all(value, ('row', 'col'), split_axis=0, concat_axis=0, tiled=...]
    ppermute x0 -> x60, starting transfers between devices: none -> 112 us  [exchange(): lax.ppermute(block, ('row', 'col'), [(i, i ^ place) for i in range(ranks)])]
    ppermute x0 -> x60, waiting for transfers between devices: none -> 47 us  [exchange(): lax.ppermute(block, ('row', 'col'), [(i, i ^ place) for i in range(ranks)])]
    all_to_all x4 -> x0, starting transfers between devices: 22.3 us -> none  [exchange(): lax.all_to_all(value, ('row', 'col'), split_axis=0, concat_axis=0, tiled=...]
    unnamed x44 -> x18, local copies, waits for them, and re-layouts: 13.5 us -> 0.05 us
    pallas_call x7, Pallas kernels: 52.7 us -> 44.4 us  [the longest x2 16.5 us: planes(): pl.pallas_call(functools.partial(plane_sweeps, columns), grid=(1,), in_sp...]
  transfers between devices with their start and end apart: 4 -> 60, of which waited for: 4 -> 22; matrix products, arithmetic and copies ran while one was open for 0% -> 0% of each run, Pallas kernels for 15% -> 15%
where the time goes in v1:
time: 204 us
  starting transfers between devices  112 us (55%)
  waiting for transfers between devices  47 us (23%)
  Pallas kernels  44.4 us (22%)
    ppermute x60, starting transfers between devices, exchange(): lax.ppermute(block, ('row', 'col'), [(i, i ^ place) for i in range(ranks)])  112 us
    ppermute x60, waiting for transfers between devices, exchange(): lax.ppermute(block, ('row', 'col'), [(i, i ^ place) for i in range(ranks)])  47 us
    pallas_call x2, Pallas kernels, planes(): pl.pallas_call(functools.partial(plane_sweeps, columns), grid=(1,), in_sp...  16.5 us
    pallas_call x2, Pallas kernels, first(): pl.pallas_call(functools.partial(first_sweep, chunk, columns), grid=(dept...  15.3 us
    pallas_call x2, Pallas kernels, last(): pl.pallas_call(functools.partial(last_sweep, chunk, columns, ranks), grid...  10.5 us
  transfers between devices with their start and end apart: 60, of which 22 were waited for; matrix products, arithmetic and copies ran while one was open for 0% of the time, Pallas kernels for 15%

profile of v1, /device:TPU:17, one launch (start us, length us, event | category | flops | bytes accessed | tf_op | source)
XLA Modules:
  0.0 204.2 jit_solution(18177902491267785329)
XLA Ops:
  0.7 7.7 %first_sweep_0.1 = (f32[32,8,128]{2,1,0:T(8,128)}, f32[32,8,128]{2,1,0:T(8,128)}, f32[32,8,128]{2,1,0:T(8,128)}, f32[32,8,128]{2,1,0:T(8,128)}, f32[32,8,128]{2,...) custom-call(s32[1]{0:T(128)S(6)} %copy.10.species, ...), custom_call_target="tpu_custom_call" | custom-call | flops 805306368 | bytes 6291456 | tf_op jit(solution)/shard_map/first_sweep_0/pallas_call | solution.py:241
  8.5 3.1 %collective-permute-start.31 = (f32[32,8,128]{2,1,0:T(8,128)}, f32[32,8,128]{2,1,0:T(8,128)S(1)}, u32[]{:S(2)}, u32[]{:S(2)}) collective-permute-start(f32[32,8,128]{2,1,0:T(8,128)} %get-tuple-element.106), channel_id=1, source_target_pairs={{0,7},{1,6},{2,5},{3,4},{4,3},{5,2},{6,1},{7,0},{8,15},{9,14},{10,... | collective-permute-start | bytes 393224 | tf_op jit(solution)/shard_map/ppermute | solution.py:236
  11.6 1.7 collective-permute-start.32
  15.0 4.8 %collective-permute-start.35 = (f32[32,8,128]{2,1,0:T(8,128)}, f32[32,8,128]{2,1,0:T(8,128)S(1)}, u32[]{:S(2)}, u32[]{:S(2)}) collective-permute-start(f32[32,8,128]{2,1,0:T(8,128)} %get-tuple-element.110), channel_id=1, source_target_pairs={{0,5},{1,4},{2,7},{3,6},{4,1},{5,0},{6,3},{7,2},{8,13},{9,12},{10,... | collective-permute-start | bytes 393224 | tf_op jit(solution)/shard_map/ppermute | solution.py:236
  19.8 2.5 %collective-permute-start.36 = (f32[32,8,128]{2,1,0:T(8,128)}, f32[32,8,128]{2,1,0:T(8,128)S(1)}, u32[]{:S(2)}, u32[]{:S(2)}) collective-permute-start(f32[32,8,128]{2,1,0:T(8,128)} %get-tuple-element.111), channel_id=1, source_target_pairs={{0,11},{1,10},{2,9},{3,8},{4,15},{5,14},{6,13},{7,12},{8,3},{9,2},... | collective-permute-start | bytes 393224 | tf_op jit(solution)/shard_map/ppermute | solution.py:236
  22.3 2.6 %collective-permute-start.37 = (f32[32,8,128]{2,1,0:T(8,128)}, f32[32,8,128]{2,1,0:T(8,128)S(1)}, u32[]{:S(2)}, u32[]{:S(2)}) collective-permute-start(f32[32,8,128]{2,1,0:T(8,128)} %get-tuple-element.112), channel_id=1, source_target_pairs={{0,4},{1,5},{2,6},{3,7},{4,0},{5,1},{6,2},{7,3},{8,12},{9,13},{10,... | collective-permute-start | bytes 393224 | tf_op jit(solution)/shard_map/ppermute | solution.py:236
  25.1 1.6 collective-permute-done.34.refs_4_
  26.6 2.9 %collective-permute-start.39 = (f32[32,8,128]{2,1,0:T(8,128)}, f32[32,8,128]{2,1,0:T(8,128)S(1)}, u32[]{:S(2)}, u32[]{:S(2)}) collective-permute-start(f32[32,8,128]{2,1,0:T(8,128)} %get-tuple-element.114), channel_id=1, source_target_pairs={{0,3},{1,2},{2,1},{3,0},{4,7},{5,6},{6,5},{7,4},{8,11},{9,10},{10,... | collective-permute-start | bytes 393224 | tf_op jit(solution)/shard_map/ppermute | solution.py:236
  30.2 3.3 %collective-permute-done.36.refs_6_ = f32[32,8,128]{2,1,0:T(8,128)S(1)} collective-permute-done((f32[32,8,128]{2,1,0:T(8,128)}, f32[32,8,128]{2,1,0:T(8,128)S(1)}, u32[]{:S(2)}, u32[]{:S(2)}) %collective-permute-start.36) | collective-permute-done | bytes 131104 | tf_op jit(solution)/shard_map/ppermute | solution.py:236
  34.6 2.9 %collective-permute-done.37.refs_7_ = f32[32,8,128]{2,1,0:T(8,128)S(1)} collective-permute-done((f32[32,8,128]{2,1,0:T(8,128)}, f32[32,8,128]{2,1,0:T(8,128)S(1)}, u32[]{:S(2)}, u32[]{:S(2)}) %collective-permute-start.37) | collective-permute-done | bytes 131104 | tf_op jit(solution)/shard_map/ppermute | solution.py:236
  37.4 3.0 %collective-permute-done.38.refs_8_ = f32[32,8,128]{2,1,0:T(8,128)S(1)} collective-permute-done((f32[32,8,128]{2,1,0:T(8,128)}, f32[32,8,128]{2,1,0:T(8,128)S(1)}, u32[]{:S(2)}, u32[]{:S(2)}) %collective-permute-start.38) | collective-permute-done | bytes 131104 | tf_op jit(solution)/shard_map/ppermute | solution.py:236
  40.6 4.1 %collective-permute-start.44 = (f32[32,8,128]{2,1,0:T(8,128)}, f32[32,8,128]{2,1,0:T(8,128)S(1)}, u32[]{:S(2)}, u32[]{:S(2)}) collective-permute-start(f32[32,8,128]{2,1,0:T(8,128)} %get-tuple-element.119), channel_id=1, source_target_pairs={{0,15},{1,14},{2,13},{3,12},{4,11},{5,10},{6,9},{7,8},{8,7},{9,6},... | collective-permute-start | bytes 393224 | tf_op jit(solution)/shard_map/ppermute | solution.py:236
  44.7 7.6 %first_sweep_1.1 = (f32[32,8,128]{2,1,0:T(8,128)}, f32[32,8,128]{2,1,0:T(8,128)}, f32[32,8,128]{2,1,0:T(8,128)}, f32[32,8,128]{2,1,0:T(8,128)}, f32[32,8,128]{2,...) custom-call(s32[1]{0:T(128)S(6)} %copy.10.species, ...), custom_call_target="tpu_custom_call" | custom-call | flops 805306368 | bytes 6291456 | tf_op jit(solution)/shard_map/first_sweep_1/pallas_call | solution.py:241
  53.9 2.7 %collective-permute-start.2 = (f32[32,8,128]{2,1,0:T(8,128)}, f32[32,8,128]{2,1,0:T(8,128)S(1)}, u32[]{:S(2)}, u32[]{:S(2)}) collective-permute-start(f32[32,8,128]{2,1,0:T(8,128)} %get-tuple-element.75), channel_id=1, source_target_pairs={{0,9},{1,8},{2,11},{3,10},{4,13},{5,12},{6,15},{7,14},{8,1},{9,0},... | collective-permute-start | bytes 393224 | tf_op jit(solution)/shard_map/ppermute | solution.py:236
  58.9 6.8 %collective-permute-start.4 = (f32[32,8,128]{2,1,0:T(8,128)}, f32[32,8,128]{2,1,0:T(8,128)S(1)}, u32[]{:S(2)}, u32[]{:S(2)}) collective-permute-start(f32[32,8,128]{2,1,0:T(8,128)} %get-tuple-element.77), channel_id=1, source_target_pairs={{0,10},{1,11},{2,8},{3,9},{4,14},{5,15},{6,12},{7,13},{8,2},{9,3},... | collective-permute-start | bytes 393224 | tf_op jit(solution)/shard_map/ppermute | solution.py:236
  65.7 2.6 %collective-permute-start.5 = (f32[32,8,128]{2,1,0:T(8,128)}, f32[32,8,128]{2,1,0:T(8,128)S(1)}, u32[]{:S(2)}, u32[]{:S(2)}) collective-permute-start(f32[32,8,128]{2,1,0:T(8,128)} %get-tuple-element.78), channel_id=1, source_target_pairs={{0,5},{1,4},{2,7},{3,6},{4,1},{5,0},{6,3},{7,2},{8,13},{9,12},{10,... | collective-permute-start | bytes 393224 | tf_op jit(solution)/shard_map/ppermute | solution.py:236
  68.3 5.3 %collective-permute-start.7 = (f32[32,8,128]{2,1,0:T(8,128)}, f32[32,8,128]{2,1,0:T(8,128)S(1)}, u32[]{:S(2)}, u32[]{:S(2)}) collective-permute-start(f32[32,8,128]{2,1,0:T(8,128)} %get-tuple-element.80), channel_id=1, source_target_pairs={{0,4},{1,5},{2,6},{3,7},{4,0},{5,1},{6,2},{7,3},{8,12},{9,13},{10,... | collective-permute-start | bytes 393224 | tf_op jit(solution)/shard_map/ppermute | solution.py:236
  73.6 1.8 collective-permute-start.8
  75.4 2.2 %collective-permute-done.4.refs_4_ = f32[32,8,128]{2,1,0:T(8,128)S(1)} collective-permute-done((f32[32,8,128]{2,1,0:T(8,128)}, f32[32,8,128]{2,1,0:T(8,128)S(1)}, u32[]{:S(2)}, u32[]{:S(2)}) %collective-permute-start.4) | collective-permute-done | bytes 131104 | tf_op jit(solution)/shard_map/ppermute | solution.py:236
  77.7 2.1 %prepare.1 = (bf16[4,256,256]{2,1,0:T(8,128)(2,1)S(1)}, bf16[4,256,256]{2,1,0:T(8,128)(2,1)S(1)}) custom-call(s32[2,3]{1,0:T(2,128)S(1)} %copy-done.2, f32[256,256]{1,0:T(8,128)S(1)} %copy-done, f32[256,256]{1,0:T(8,128)S(1)} %copy-done.1, f32[256,256]{1,0:T(8,128)S(1)} %copy-done.5, f32[256,256]{1,0:T(8,128)S(1)} %copy-done.6), custom_call_target="tpu_custom_call" | custom-call | flops 805306368 | bytes 2097152 | tf_op jit(solution)/shard_map/prepare/pallas_call | solution.py:286
  80.3 3.2 %collective-permute-start.11 = (f32[32,8,128]{2,1,0:T(8,128)}, f32[32,8,128]{2,1,0:T(8,128)S(1)}, u32[]{:S(2)}, u32[]{:S(2)}) collective-permute-start(f32[32,8,128]{2,1,0:T(8,128)} %get-tuple-element.84), channel_id=1, source_target_pairs={{0,13},{1,12},{2,15},{3,14},{4,9},{5,8},{6,11},{7,10},{8,5},{9,4},... | collective-permute-start | bytes 393224 | tf_op jit(solution)/shard_map/ppermute | solution.py:236
  84.0 2.0 collective-permute-start.12
  86.6 2.6 %collective-permute-start.14 = (f32[32,8,128]{2,1,0:T(8,128)}, f32[32,8,128]{2,1,0:T(8,128)S(1)}, u32[]{:S(2)}, u32[]{:S(2)}) collective-permute-start(f32[32,8,128]{2,1,0:T(8,128)} %get-tuple-element.87), channel_id=1, source_target_pairs={{0,15},{1,14},{2,13},{3,12},{4,11},{5,10},{6,9},{7,8},{8,7},{9,6},... | collective-permute-start | bytes 393224 | tf_op jit(solution)/shard_map/ppermute | solution.py:236
  89.2 8.2 %plane_sweeps_0.1 = (f32[32,8,128]{2,1,0:T(8,128)S(1)}, f32[32,8,128]{2,1,0:T(8,128)S(1)}, f32[32,8,128]{2,1,0:T(8,128)S(1)}, f32[32,8,128]{2,1,0:T(8,128)S(1)},...) custom-call(s32[1]{0:T(128)S(6)} %copy.10.species, ...), custom_call_target="tpu_custom_call" | custom-call | flops 3221225472 | bytes 4194304 | tf_op jit(solution)/shard_map/plane_sweeps_0/pallas_call | solution.py:260
  97.4 5.6 %collective-permute-start.45 = (f32[32,8,128]{2,1,0:T(8,128)S(1)}, f32[32,8,128]{2,1,0:T(8,128)S(1)}, u32[]{:S(2)}, u32[]{:S(2)}) collective-permute-start(f32[32,8,128]{2,1,0:T(8,128)S(1)} %get-tuple-element.121), channel_id=1, source_target_pairs={{0,8},{1,9},{2,10},{3,11},{4,12},{5,13},{6,14},{7,15},{8,0},{9,1},... | collective-permute-start | bytes 393224 | tf_op jit(solution)/shard_map/ppermute | solution.py:236
  103.3 2.4 %collective-permute-start.48 = (f32[32,8,128]{2,1,0:T(8,128)S(1)}, f32[32,8,128]{2,1,0:T(8,128)S(1)}, u32[]{:S(2)}, u32[]{:S(2)}) collective-permute-start(f32[32,8,128]{2,1,0:T(8,128)S(1)} %get-tuple-element.124), channel_id=1, source_target_pairs={{0,6},{1,7},{2,4},{3,5},{4,2},{5,3},{6,0},{7,1},{8,14},{9,15},{10,... | collective-permute-start | bytes 393224 | tf_op jit(solution)/shard_map/ppermute | solution.py:236
  107.2 4.5 %collective-permute-done.45.refs_0_ = f32[32,8,128]{2,1,0:T(8,128)S(1)} collective-permute-done((f32[32,8,128]{2,1,0:T(8,128)S(1)}, f32[32,8,128]{2,1,0:T(8,128)S(1)}, u32[]{:S(2)}, u32[]{:S(2)}) %collective-permute-start.45) | collective-permute-done | bytes 131104 | tf_op jit(solution)/shard_map/ppermute | solution.py:236
  111.8 2.0 collective-permute-start.50
  114.9 6.5 %collective-permute-start.53 = (f32[32,8,128]{2,1,0:T(8,128)S(1)}, f32[32,8,128]{2,1,0:T(8,128)S(1)}, u32[]{:S(2)}, u32[]{:S(2)}) collective-permute-start(f32[32,8,128]{2,1,0:T(8,128)S(1)} %get-tuple-element.129), channel_id=1, source_target_pairs={{0,12},{1,13},{2,14},{3,15},{4,8},{5,9},{6,10},{7,11},{8,4},{9,5},... | collective-permute-start | bytes 393224 | tf_op jit(solution)/shard_map/ppermute | solution.py:236
  121.5 4.0 %collective-permute-start.55 = (f32[32,8,128]{2,1,0:T(8,128)S(1)}, f32[32,8,128]{2,1,0:T(8,128)S(1)}, u32[]{:S(2)}, u32[]{:S(2)}) collective-permute-start(f32[32,8,128]{2,1,0:T(8,128)S(1)} %get-tuple-element.131), channel_id=1, source_target_pairs={{0,2},{1,3},{2,0},{3,1},{4,6},{5,7},{6,4},{7,5},{8,10},{9,11},{10,... | collective-permute-start | bytes 393224 | tf_op jit(solution)/shard_map/ppermute | solution.py:236
  126.4 3.5 %collective-permute-start.57 = (f32[32,8,128]{2,1,0:T(8,128)S(1)}, f32[32,8,128]{2,1,0:T(8,128)S(1)}, u32[]{:S(2)}, u32[]{:S(2)}) collective-permute-start(f32[32,8,128]{2,1,0:T(8,128)S(1)} %get-tuple-element.133), channel_id=1, source_target_pairs={{0,1},{1,0},{2,3},{3,2},{4,5},{5,4},{6,7},{7,6},{8,9},{9,8},{10,11... | collective-permute-start | bytes 393224 | tf_op jit(solution)/shard_map/ppermute | solution.py:236
  129.8 4.5 %collective-permute-done.53.refs_8_ = f32[32,8,128]{2,1,0:T(8,128)S(1)} collective-permute-done((f32[32,8,128]{2,1,0:T(8,128)S(1)}, f32[32,8,128]{2,1,0:T(8,128)S(1)}, u32[]{:S(2)}, u32[]{:S(2)}) %collective-permute-start.53) | collective-permute-done | bytes 131104 | tf_op jit(solution)/shard_map/ppermute | solution.py:236
  134.4 3.5 %collective-permute-start.59 = (f32[32,8,128]{2,1,0:T(8,128)S(1)}, f32[32,8,128]{2,1,0:T(8,128)S(1)}, u32[]{:S(2)}, u32[]{:S(2)}) collective-permute-start(f32[32,8,128]{2,1,0:T(8,128)S(1)} %get-tuple-element.135), channel_id=1, source_target_pairs={{0,15},{1,14},{2,13},{3,12},{4,11},{5,10},{6,9},{7,8},{8,7},{9,6},... | collective-permute-start | bytes 393224 | tf_op jit(solution)/shard_map/ppermute | solution.py:236
  137.9 8.3 %plane_sweeps_1.1 = (f32[32,8,128]{2,1,0:T(8,128)S(1)}, f32[32,8,128]{2,1,0:T(8,128)S(1)}, f32[32,8,128]{2,1,0:T(8,128)S(1)}, f32[32,8,128]{2,1,0:T(8,128)S(1)},...) custom-call(s32[1]{0:T(128)S(6)} %copy.10.species, ...), custom_call_target="tpu_custom_call" | custom-call | flops 3221225472 | bytes 4194304 | tf_op jit(solution)/shard_map/plane_sweeps_1/pallas_call | solution.py:260
  147.8 2.5 %collective-permute-start.17 = (f32[32,8,128]{2,1,0:T(8,128)S(1)}, f32[32,8,128]{2,1,0:T(8,128)S(1)}, u32[]{:S(2)}, u32[]{:S(2)}) collective-permute-start(f32[32,8,128]{2,1,0:T(8,128)S(1)} %get-tuple-element.91), channel_id=1, source_target_pairs={{0,9},{1,8},{2,11},{3,10},{4,13},{5,12},{6,15},{7,14},{8,1},{9,0},... | collective-permute-start | bytes 393224 | tf_op jit(solution)/shard_map/ppermute | solution.py:236
  151.3 7.7 %collective-permute-start.19 = (f32[32,8,128]{2,1,0:T(8,128)S(1)}, f32[32,8,128]{2,1,0:T(8,128)S(1)}, u32[]{:S(2)}, u32[]{:S(2)}) collective-permute-start(f32[32,8,128]{2,1,0:T(8,128)S(1)} %get-tuple-element.93), channel_id=1, source_target_pairs={{0,10},{1,11},{2,8},{3,9},{4,14},{5,15},{6,12},{7,13},{8,2},{9,3},... | collective-permute-start | bytes 393224 | tf_op jit(solution)/shard_map/ppermute | solution.py:236
  159.0 3.8 %collective-permute-start.21 = (f32[32,8,128]{2,1,0:T(8,128)S(1)}, f32[32,8,128]{2,1,0:T(8,128)S(1)}, u32[]{:S(2)}, u32[]{:S(2)}) collective-permute-start(f32[32,8,128]{2,1,0:T(8,128)S(1)} %get-tuple-element.95), channel_id=1, source_target_pairs={{0,11},{1,10},{2,9},{3,8},{4,15},{5,14},{6,13},{7,12},{8,3},{9,2},... | collective-permute-start | bytes 393224 | tf_op jit(solution)/shard_map/ppermute | solution.py:236
  163.9 3.3 %collective-permute-start.23 = (f32[32,8,128]{2,1,0:T(8,128)S(1)}, f32[32,8,128]{2,1,0:T(8,128)S(1)}, u32[]{:S(2)}, u32[]{:S(2)}) collective-permute-start(f32[32,8,128]{2,1,0:T(8,128)S(1)} %get-tuple-element.97), channel_id=1, source_target_pairs={{0,12},{1,13},{2,14},{3,15},{4,8},{5,9},{6,10},{7,11},{8,4},{9,5},... | collective-permute-start | bytes 393224 | tf_op jit(solution)/shard_map/ppermute | solution.py:236
  167.1 2.4 %collective-permute-done.19.refs_4_ = f32[32,8,128]{2,1,0:T(8,128)S(1)} collective-permute-done((f32[32,8,128]{2,1,0:T(8,128)S(1)}, f32[32,8,128]{2,1,0:T(8,128)S(1)}, u32[]{:S(2)}, u32[]{:S(2)}) %collective-permute-start.19) | collective-permute-done | bytes 131104 | tf_op jit(solution)/shard_map/ppermute | solution.py:236
  170.8 2.2 %collective-permute-start.25 = (f32[32,8,128]{2,1,0:T(8,128)S(1)}, f32[32,8,128]{2,1,0:T(8,128)S(1)}, u32[]{:S(2)}, u32[]{:S(2)}) collective-permute-start(f32[32,8,128]{2,1,0:T(8,128)S(1)} %get-tuple-element.99), channel_id=1, source_target_pairs={{0,2},{1,3},{2,0},{3,1},{4,6},{5,7},{6,4},{7,5},{8,10},{9,11},{10,... | collective-permute-start | bytes 393224 | tf_op jit(solution)/shard_map/ppermute | solution.py:236
  173.0 3.6 %collective-permute-done.21.refs_6_ = f32[32,8,128]{2,1,0:T(8,128)S(1)} collective-permute-done((f32[32,8,128]{2,1,0:T(8,128)S(1)}, f32[32,8,128]{2,1,0:T(8,128)S(1)}, u32[]{:S(2)}, u32[]{:S(2)}) %collective-permute-start.21) | collective-permute-done | bytes 131104 | tf_op jit(solution)/shard_map/ppermute | solution.py:236
  176.7 1.9 collective-permute-done.22.refs_7_
  179.2 2.5 %collective-permute-start.28 = (f32[32,8,128]{2,1,0:T(8,128)S(1)}, f32[32,8,128]{2,1,0:T(8,128)S(1)}, u32[]{:S(2)}, u32[]{:S(2)}) collective-permute-start(f32[32,8,128]{2,1,0:T(8,128)S(1)} %get-tuple-element.102), channel_id=1, source_target_pairs={{0,14},{1,15},{2,12},{3,13},{4,10},{5,11},{6,8},{7,9},{8,6},{9,7},... | collective-permute-start | bytes 393224 | tf_op jit(solution)/shard_map/ppermute | solution.py:236
  182.6 4.1 %last_sweep_0.1.refs_16_ = f32[32,256,128]{2,1,0:T(8,128)S(1)} custom-call(s32[1]{0:T(128)S(6)} %copy.10.species, f32[64]{0:T(128)S(1)} %copy-done.3, f32[64]{0:T(128)S(1)} %copy-done.4, s32[2,3]{1,0:T(2,128)S(1)} %copy-done.2, f32[256,256]{1,0:T(8,128)S(1)} %copy-done, f32[256,256]{1,0:T(8,128)S(1)} %copy-done.1, ...), custom_call_target="tpu_custom_call" | custom-call | flops 805306368 | bytes 6291456 | tf_op jit(solution)/shard_map/last_sweep_0/pallas_call | solution.py:273
  186.7 4.2 %collective-permute-done.26.refs_11_ = f32[32,8,128]{2,1,0:T(8,128)S(1)} collective-permute-done((f32[32,8,128]{2,1,0:T(8,128)S(1)}, f32[32,8,128]{2,1,0:T(8,128)S(1)}, u32[]{:S(2)}, u32[]{:S(2)}) %collective-permute-start.26) | collective-permute-done | bytes 131104 | tf_op jit(solution)/shard_map/ppermute | solution.py:236
  190.9 3.9 %collective-permute-done.28.refs_13_ = f32[32,8,128]{2,1,0:T(8,128)S(1)} collective-permute-done((f32[32,8,128]{2,1,0:T(8,128)S(1)}, f32[32,8,128]{2,1,0:T(8,128)S(1)}, u32[]{:S(2)}, u32[]{:S(2)}) %collective-permute-start.28) | collective-permute-done | bytes 131104 | tf_op jit(solution)/shard_map/ppermute | solution.py:236
  194.9 2.9 %collective-permute-done.29.refs_14_ = f32[32,8,128]{2,1,0:T(8,128)S(1)} collective-permute-done((f32[32,8,128]{2,1,0:T(8,128)S(1)}, f32[32,8,128]{2,1,0:T(8,128)S(1)}, u32[]{:S(2)}, u32[]{:S(2)}) %collective-permute-start.29) | collective-permute-done | bytes 131104 | tf_op jit(solution)/shard_map/ppermute | solution.py:236
  197.8 6.4 %last_sweep_1.1 = f32[256,32,128]{2,1,0:T(8,128)} custom-call(s32[1]{0:T(128)S(6)} %copy.10.species, f32[64]{0:T(128)S(1)} %copy-done.3, f32[64]{0:T(128)S(1)} %copy-done.4, s32[2,3]{1,0:T(2,128)S(1)} %copy-done.2, f32[256,256]{1,0:T(8,128)S(1)} %copy-done, f32[256,256]{1,0:T(8,128)S(1)} %copy-done.1, f32[32,8,128]{2,1,0:T(8,128)S(1)} %collective-permute-done.15.refs_0_, ...), custom_call_target="tpu_custom_call" | custom-call | flops 805306368 | bytes 6291456 | tf_op jit(solution)/shard_map/last_sweep_1/pallas_call | solution.py:273
  (97 shorter events, 19.6 us)
Async XLA Ops:
  13.9 12.7 %collective-permute-start.34 = (f32[32,8,128]{2,1,0:T(8,128)}, f32[32,8,128]{2,1,0:T(8,128)S(1)}, u32[]{:S(2)}, u32[]{:S(2)}) collective-permute-start(f32[32,8,128]{2,1,0:T(8,128)} %get-tuple-element.109), channel_id=1, source_target_pairs={{0,10},{1,11},{2,8},{3,9},{4,14},{5,15},{6,12},{7,13},{8,2},{9,3},... | collective-permute-start | bytes 393224 | tf_op jit(solution)/shard_map/ppermute | solution.py:236
  15.0 14.5 %collective-permute-start.35 = (f32[32,8,128]{2,1,0:T(8,128)}, f32[32,8,128]{2,1,0:T(8,128)S(1)}, u32[]{:S(2)}, u32[]{:S(2)}) collective-permute-start(f32[32,8,128]{2,1,0:T(8,128)} %get-tuple-element.110), channel_id=1, source_target_pairs={{0,5},{1,4},{2,7},{3,6},{4,1},{5,0},{6,3},{7,2},{8,13},{9,12},{10,... | collective-permute-start | bytes 393224 | tf_op jit(solution)/shard_map/ppermute | solution.py:236
  19.8 13.7 %collective-permute-start.36 = (f32[32,8,128]{2,1,0:T(8,128)}, f32[32,8,128]{2,1,0:T(8,128)S(1)}, u32[]{:S(2)}, u32[]{:S(2)}) collective-permute-start(f32[32,8,128]{2,1,0:T(8,128)} %get-tuple-element.111), channel_id=1, source_target_pairs={{0,11},{1,10},{2,9},{3,8},{4,15},{5,14},{6,13},{7,12},{8,3},{9,2},... | collective-permute-start | bytes 393224 | tf_op jit(solution)/shard_map/ppermute | solution.py:236
  22.3 15.1 %collective-permute-start.37 = (f32[32,8,128]{2,1,0:T(8,128)}, f32[32,8,128]{2,1,0:T(8,128)S(1)}, u32[]{:S(2)}, u32[]{:S(2)}) collective-permute-start(f32[32,8,128]{2,1,0:T(8,128)} %get-tuple-element.112), channel_id=1, source_target_pairs={{0,4},{1,5},{2,6},{3,7},{4,0},{5,1},{6,2},{7,3},{8,12},{9,13},{10,... | collective-permute-start | bytes 393224 | tf_op jit(solution)/shard_map/ppermute | solution.py:236
  24.9 15.6 %collective-permute-start.38 = (f32[32,8,128]{2,1,0:T(8,128)}, f32[32,8,128]{2,1,0:T(8,128)S(1)}, u32[]{:S(2)}, u32[]{:S(2)}) collective-permute-start(f32[32,8,128]{2,1,0:T(8,128)} %get-tuple-element.113), channel_id=1, source_target_pairs={{0,12},{1,13},{2,14},{3,15},{4,8},{5,9},{6,10},{7,11},{8,4},{9,5},... | collective-permute-start | bytes 393224 | tf_op jit(solution)/shard_map/ppermute | solution.py:236
  26.6 14.0 %collective-permute-start.39 = (f32[32,8,128]{2,1,0:T(8,128)}, f32[32,8,128]{2,1,0:T(8,128)S(1)}, u32[]{:S(2)}, u32[]{:S(2)}) collective-permute-start(f32[32,8,128]{2,1,0:T(8,128)} %get-tuple-element.114), channel_id=1, source_target_pairs={{0,3},{1,2},{2,1},{3,0},{4,7},{5,6},{6,5},{7,4},{8,11},{9,10},{10,... | collective-permute-start | bytes 393224 | tf_op jit(solution)/shard_map/ppermute | solution.py:236
  29.5 22.9 %collective-permute-start.40 = (f32[32,8,128]{2,1,0:T(8,128)}, f32[32,8,128]{2,1,0:T(8,128)S(1)}, u32[]{:S(2)}, u32[]{:S(2)}) collective-permute-start(f32[32,8,128]{2,1,0:T(8,128)} %get-tuple-element.115), channel_id=1, source_target_pairs={{0,2},{1,3},{2,0},{3,1},{4,6},{5,7},{6,4},{7,5},{8,10},{9,11},{10,... | collective-permute-start | bytes 393224 | tf_op jit(solution)/shard_map/ppermute | solution.py:236
  33.5 19.0 %collective-permute-start.41 = (f32[32,8,128]{2,1,0:T(8,128)}, f32[32,8,128]{2,1,0:T(8,128)S(1)}, u32[]{:S(2)}, u32[]{:S(2)}) collective-permute-start(f32[32,8,128]{2,1,0:T(8,128)} %get-tuple-element.116), channel_id=1, source_target_pairs={{0,13},{1,12},{2,15},{3,14},{4,9},{5,8},{6,11},{7,10},{8,5},{9,4},... | collective-permute-start | bytes 393224 | tf_op jit(solution)/shard_map/ppermute | solution.py:236
  37.4 16.5 %collective-permute-start.42 = (f32[32,8,128]{2,1,0:T(8,128)}, f32[32,8,128]{2,1,0:T(8,128)S(1)}, u32[]{:S(2)}, u32[]{:S(2)}) collective-permute-start(f32[32,8,128]{2,1,0:T(8,128)} %get-tuple-element.117), channel_id=1, source_target_pairs={{0,1},{1,0},{2,3},{3,2},{4,5},{5,4},{6,7},{7,6},{8,9},{9,8},{10,11... | collective-permute-start | bytes 393224 | tf_op jit(solution)/shard_map/ppermute | solution.py:236
  40.5 16.1 %collective-permute-start.43 = (f32[32,8,128]{2,1,0:T(8,128)}, f32[32,8,128]{2,1,0:T(8,128)S(1)}, u32[]{:S(2)}, u32[]{:S(2)}) collective-permute-start(f32[32,8,128]{2,1,0:T(8,128)} %get-tuple-element.118), channel_id=1, source_target_pairs={{0,14},{1,15},{2,12},{3,13},{4,10},{5,11},{6,8},{7,9},{8,6},{9,7},... | collective-permute-start | bytes 393224 | tf_op jit(solution)/shard_map/ppermute | solution.py:236
  40.6 18.3 %collective-permute-start.44 = (f32[32,8,128]{2,1,0:T(8,128)}, f32[32,8,128]{2,1,0:T(8,128)S(1)}, u32[]{:S(2)}, u32[]{:S(2)}) collective-permute-start(f32[32,8,128]{2,1,0:T(8,128)} %get-tuple-element.119), channel_id=1, source_target_pairs={{0,15},{1,14},{2,13},{3,12},{4,11},{5,10},{6,9},{7,8},{8,7},{9,6},... | collective-permute-start | bytes 393224 | tf_op jit(solution)/shard_map/ppermute | solution.py:236
  52.4 13.3 %collective-permute-start = (f32[32,8,128]{2,1,0:T(8,128)}, f32[32,8,128]{2,1,0:T(8,128)S(1)}, u32[]{:S(2)}, u32[]{:S(2)}) collective-permute-start(f32[32,8,128]{2,1,0:T(8,128)} %get-tuple-element.73), channel_id=1, source_target_pairs={{0,8},{1,9},{2,10},{3,11},{4,12},{5,13},{6,14},{7,15},{8,0},{9,1},... | collective-permute-start | bytes 393224 | tf_op jit(solution)/shard_map/ppermute | solution.py:236
  52.5 15.8 %collective-permute-start.1 = (f32[32,8,128]{2,1,0:T(8,128)}, f32[32,8,128]{2,1,0:T(8,128)S(1)}, u32[]{:S(2)}, u32[]{:S(2)}) collective-permute-start(f32[32,8,128]{2,1,0:T(8,128)} %get-tuple-element.74), channel_id=1, source_target_pairs={{0,7},{1,6},{2,5},{3,4},{4,3},{5,2},{6,1},{7,0},{8,15},{9,14},{10,... | collective-permute-start | bytes 393224 | tf_op jit(solution)/shard_map/ppermute | solution.py:236
  53.9 14.4 %collective-permute-start.2 = (f32[32,8,128]{2,1,0:T(8,128)}, f32[32,8,128]{2,1,0:T(8,128)S(1)}, u32[]{:S(2)}, u32[]{:S(2)}) collective-permute-start(f32[32,8,128]{2,1,0:T(8,128)} %get-tuple-element.75), channel_id=1, source_target_pairs={{0,9},{1,8},{2,11},{3,10},{4,13},{5,12},{6,15},{7,14},{8,1},{9,0},... | collective-permute-start | bytes 393224 | tf_op jit(solution)/shard_map/ppermute | solution.py:236
  56.6 17.0 %collective-permute-start.3 = (f32[32,8,128]{2,1,0:T(8,128)}, f32[32,8,128]{2,1,0:T(8,128)S(1)}, u32[]{:S(2)}, u32[]{:S(2)}) collective-permute-start(f32[32,8,128]{2,1,0:T(8,128)} %get-tuple-element.76), channel_id=1, source_target_pairs={{0,6},{1,7},{2,4},{3,5},{4,2},{5,3},{6,0},{7,1},{8,14},{9,15},{10,... | collective-permute-start | bytes 393224 | tf_op jit(solution)/shard_map/ppermute | solution.py:236
  58.9 18.7 %collective-permute-start.4 = (f32[32,8,128]{2,1,0:T(8,128)}, f32[32,8,128]{2,1,0:T(8,128)S(1)}, u32[]{:S(2)}, u32[]{:S(2)}) collective-permute-start(f32[32,8,128]{2,1,0:T(8,128)} %get-tuple-element.77), channel_id=1, source_target_pairs={{0,10},{1,11},{2,8},{3,9},{4,14},{5,15},{6,12},{7,13},{8,2},{9,3},... | collective-permute-start | bytes 393224 | tf_op jit(solution)/shard_map/ppermute | solution.py:236
  65.7 14.3 %collective-permute-start.5 = (f32[32,8,128]{2,1,0:T(8,128)}, f32[32,8,128]{2,1,0:T(8,128)S(1)}, u32[]{:S(2)}, u32[]{:S(2)}) collective-permute-start(f32[32,8,128]{2,1,0:T(8,128)} %get-tuple-element.78), channel_id=1, source_target_pairs={{0,5},{1,4},{2,7},{3,6},{4,1},{5,0},{6,3},{7,2},{8,13},{9,12},{10,... | collective-permute-start | bytes 393224 | tf_op jit(solution)/shard_map/ppermute | solution.py:236
  68.3 15.7 %collective-permute-start.7 = (f32[32,8,128]{2,1,0:T(8,128)}, f32[32,8,128]{2,1,0:T(8,128)S(1)}, u32[]{:S(2)}, u32[]{:S(2)}) collective-permute-start(f32[32,8,128]{2,1,0:T(8,128)} %get-tuple-element.80), channel_id=1, source_target_pairs={{0,4},{1,5},{2,6},{3,7},{4,0},{5,1},{6,2},{7,3},{8,12},{9,13},{10,... | collective-permute-start | bytes 393224 | tf_op jit(solution)/shard_map/ppermute | solution.py:236
  73.6 12.4 %collective-permute-start.8 = (f32[32,8,128]{2,1,0:T(8,128)}, f32[32,8,128]{2,1,0:T(8,128)S(1)}, u32[]{:S(2)}, u32[]{:S(2)}) collective-permute-start(f32[32,8,128]{2,1,0:T(8,128)} %get-tuple-element.81), channel_id=1, source_target_pairs={{0,12},{1,13},{2,14},{3,15},{4,8},{5,9},{6,10},{7,11},{8,4},{9,5},... | collective-permute-start | bytes 393224 | tf_op jit(solution)/shard_map/ppermute | solution.py:236
  80.0 17.4 %collective-permute-start.10 = (f32[32,8,128]{2,1,0:T(8,128)}, f32[32,8,128]{2,1,0:T(8,128)S(1)}, u32[]{:S(2)}, u32[]{:S(2)}) collective-permute-start(f32[32,8,128]{2,1,0:T(8,128)} %get-tuple-element.83), channel_id=1, source_target_pairs={{0,2},{1,3},{2,0},{3,1},{4,6},{5,7},{6,4},{7,5},{8,10},{9,11},{10,... | collective-permute-start | bytes 393224 | tf_op jit(solution)/shard_map/ppermute | solution.py:236
  80.3 22.7 %collective-permute-start.11 = (f32[32,8,128]{2,1,0:T(8,128)}, f32[32,8,128]{2,1,0:T(8,128)S(1)}, u32[]{:S(2)}, u32[]{:S(2)}) collective-permute-start(f32[32,8,128]{2,1,0:T(8,128)} %get-tuple-element.84), channel_id=1, source_target_pairs={{0,13},{1,12},{2,15},{3,14},{4,9},{5,8},{6,11},{7,10},{8,5},{9,4},... | collective-permute-start | bytes 393224 | tf_op jit(solution)/shard_map/ppermute | solution.py:236
  84.0 19.0 %collective-permute-start.12 = (f32[32,8,128]{2,1,0:T(8,128)}, f32[32,8,128]{2,1,0:T(8,128)S(1)}, u32[]{:S(2)}, u32[]{:S(2)}) collective-permute-start(f32[32,8,128]{2,1,0:T(8,128)} %get-tuple-element.85), channel_id=1, source_target_pairs={{0,1},{1,0},{2,3},{3,2},{4,5},{5,4},{6,7},{7,6},{8,9},{9,8},{10,11... | collective-permute-start | bytes 393224 | tf_op jit(solution)/shard_map/ppermute | solution.py:236
  86.1 17.3 %collective-permute-start.13 = (f32[32,8,128]{2,1,0:T(8,128)}, f32[32,8,128]{2,1,0:T(8,128)S(1)}, u32[]{:S(2)}, u32[]{:S(2)}) collective-permute-start(f32[32,8,128]{2,1,0:T(8,128)} %get-tuple-element.86), channel_id=1, source_target_pairs={{0,14},{1,15},{2,12},{3,13},{4,10},{5,11},{6,8},{7,9},{8,6},{9,7},... | collective-permute-start | bytes 393224 | tf_op jit(solution)/shard_map/ppermute | solution.py:236
  86.6 20.7 %collective-permute-start.14 = (f32[32,8,128]{2,1,0:T(8,128)}, f32[32,8,128]{2,1,0:T(8,128)S(1)}, u32[]{:S(2)}, u32[]{:S(2)}) collective-permute-start(f32[32,8,128]{2,1,0:T(8,128)} %get-tuple-element.87), channel_id=1, source_target_pairs={{0,15},{1,14},{2,13},{3,12},{4,11},{5,10},{6,9},{7,8},{8,7},{9,6},... | collective-permute-start | bytes 393224 | tf_op jit(solution)/shard_map/ppermute | solution.py:236
  97.4 14.4 %collective-permute-start.45 = (f32[32,8,128]{2,1,0:T(8,128)S(1)}, f32[32,8,128]{2,1,0:T(8,128)S(1)}, u32[]{:S(2)}, u32[]{:S(2)}) collective-permute-start(f32[32,8,128]{2,1,0:T(8,128)S(1)} %get-tuple-element.121), channel_id=1, source_target_pairs={{0,8},{1,9},{2,10},{3,11},{4,12},{5,13},{6,14},{7,15},{8,0},{9,1},... | collective-permute-start | bytes 393224 | tf_op jit(solution)/shard_map/ppermute | solution.py:236
  107.2 14.3 %collective-permute-start.49 = (f32[32,8,128]{2,1,0:T(8,128)S(1)}, f32[32,8,128]{2,1,0:T(8,128)S(1)}, u32[]{:S(2)}, u32[]{:S(2)}) collective-permute-start(f32[32,8,128]{2,1,0:T(8,128)S(1)} %get-tuple-element.125), channel_id=1, source_target_pairs={{0,10},{1,11},{2,8},{3,9},{4,14},{5,15},{6,12},{7,13},{8,2},{9,3},... | collective-permute-start | bytes 393224 | tf_op jit(solution)/shard_map/ppermute | solution.py:236
  113.8 12.1 %collective-permute-start.51 = (f32[32,8,128]{2,1,0:T(8,128)S(1)}, f32[32,8,128]{2,1,0:T(8,128)S(1)}, u32[]{:S(2)}, u32[]{:S(2)}) collective-permute-start(f32[32,8,128]{2,1,0:T(8,128)S(1)} %get-tuple-element.127), channel_id=1, source_target_pairs={{0,11},{1,10},{2,9},{3,8},{4,15},{5,14},{6,13},{7,12},{8,3},{9,2},... | collective-permute-start | bytes 393224 | tf_op jit(solution)/shard_map/ppermute | solution.py:236
  114.9 19.4 %collective-permute-start.53 = (f32[32,8,128]{2,1,0:T(8,128)S(1)}, f32[32,8,128]{2,1,0:T(8,128)S(1)}, u32[]{:S(2)}, u32[]{:S(2)}) collective-permute-start(f32[32,8,128]{2,1,0:T(8,128)S(1)} %get-tuple-element.129), channel_id=1, source_target_pairs={{0,12},{1,13},{2,14},{3,15},{4,8},{5,9},{6,10},{7,11},{8,4},{9,5},... | collective-permute-start | bytes 393224 | tf_op jit(solution)/shard_map/ppermute | solution.py:236
  121.5 12.9 %collective-permute-start.54 = (f32[32,8,128]{2,1,0:T(8,128)S(1)}, f32[32,8,128]{2,1,0:T(8,128)S(1)}, u32[]{:S(2)}, u32[]{:S(2)}) collective-permute-start(f32[32,8,128]{2,1,0:T(8,128)S(1)} %get-tuple-element.130), channel_id=1, source_target_pairs={{0,3},{1,2},{2,1},{3,0},{4,7},{5,6},{6,5},{7,4},{8,11},{9,10},{10,... | collective-permute-start | bytes 393224 | tf_op jit(solution)/shard_map/ppermute | solution.py:236
  121.5 24.7 %collective-permute-start.55 = (f32[32,8,128]{2,1,0:T(8,128)S(1)}, f32[32,8,128]{2,1,0:T(8,128)S(1)}, u32[]{:S(2)}, u32[]{:S(2)}) collective-permute-start(f32[32,8,128]{2,1,0:T(8,128)S(1)} %get-tuple-element.131), channel_id=1, source_target_pairs={{0,2},{1,3},{2,0},{3,1},{4,6},{5,7},{6,4},{7,5},{8,10},{9,11},{10,... | collective-permute-start | bytes 393224 | tf_op jit(solution)/shard_map/ppermute | solution.py:236
  126.0 20.6 %collective-permute-start.56 = (f32[32,8,128]{2,1,0:T(8,128)S(1)}, f32[32,8,128]{2,1,0:T(8,128)S(1)}, u32[]{:S(2)}, u32[]{:S(2)}) collective-permute-start(f32[32,8,128]{2,1,0:T(8,128)S(1)} %get-tuple-element.132), channel_id=1, source_target_pairs={{0,13},{1,12},{2,15},{3,14},{4,9},{5,8},{6,11},{7,10},{8,5},{9,4},... | collective-permute-start | bytes 393224 | tf_op jit(solution)/shard_map/ppermute | solution.py:236
  126.4 21.4 %collective-permute-start.57 = (f32[32,8,128]{2,1,0:T(8,128)S(1)}, f32[32,8,128]{2,1,0:T(8,128)S(1)}, u32[]{:S(2)}, u32[]{:S(2)}) collective-permute-start(f32[32,8,128]{2,1,0:T(8,128)S(1)} %get-tuple-element.133), channel_id=1, source_target_pairs={{0,1},{1,0},{2,3},{3,2},{4,5},{5,4},{6,7},{7,6},{8,9},{9,8},{10,11... | collective-permute-start | bytes 393224 | tf_op jit(solution)/shard_map/ppermute | solution.py:236
  134.4 15.9 %collective-permute-start.58 = (f32[32,8,128]{2,1,0:T(8,128)S(1)}, f32[32,8,128]{2,1,0:T(8,128)S(1)}, u32[]{:S(2)}, u32[]{:S(2)}) collective-permute-start(f32[32,8,128]{2,1,0:T(8,128)S(1)} %get-tuple-element.134), channel_id=1, source_target_pairs={{0,14},{1,15},{2,12},{3,13},{4,10},{5,11},{6,8},{7,9},{8,6},{9,7},... | collective-permute-start | bytes 393224 | tf_op jit(solution)/shard_map/ppermute | solution.py:236
  134.4 16.9 %collective-permute-start.59 = (f32[32,8,128]{2,1,0:T(8,128)S(1)}, f32[32,8,128]{2,1,0:T(8,128)S(1)}, u32[]{:S(2)}, u32[]{:S(2)}) collective-permute-start(f32[32,8,128]{2,1,0:T(8,128)S(1)} %get-tuple-element.135), channel_id=1, source_target_pairs={{0,15},{1,14},{2,13},{3,12},{4,11},{5,10},{6,9},{7,8},{8,7},{9,6},... | collective-permute-start | bytes 393224 | tf_op jit(solution)/shard_map/ppermute | solution.py:236
  146.2 12.8 %collective-permute-start.15 = (f32[32,8,128]{2,1,0:T(8,128)S(1)}, f32[32,8,128]{2,1,0:T(8,128)S(1)}, u32[]{:S(2)}, u32[]{:S(2)}) collective-permute-start(f32[32,8,128]{2,1,0:T(8,128)S(1)} %get-tuple-element.89), channel_id=1, source_target_pairs={{0,8},{1,9},{2,10},{3,11},{4,12},{5,13},{6,14},{7,15},{8,0},{9,1},... | collective-permute-start | bytes 393224 | tf_op jit(solution)/shard_map/ppermute | solution.py:236
  146.5 12.5 %collective-permute-start.16 = (f32[32,8,128]{2,1,0:T(8,128)S(1)}, f32[32,8,128]{2,1,0:T(8,128)S(1)}, u32[]{:S(2)}, u32[]{:S(2)}) collective-permute-start(f32[32,8,128]{2,1,0:T(8,128)S(1)} %get-tuple-element.90), channel_id=1, source_target_pairs={{0,7},{1,6},{2,5},{3,4},{4,3},{5,2},{6,1},{7,0},{8,15},{9,14},{10,... | collective-permute-start | bytes 393224 | tf_op jit(solution)/shard_map/ppermute | solution.py:236
  147.8 15.0 %collective-permute-start.17 = (f32[32,8,128]{2,1,0:T(8,128)S(1)}, f32[32,8,128]{2,1,0:T(8,128)S(1)}, u32[]{:S(2)}, u32[]{:S(2)}) collective-permute-start(f32[32,8,128]{2,1,0:T(8,128)S(1)} %get-tuple-element.91), channel_id=1, source_target_pairs={{0,9},{1,8},{2,11},{3,10},{4,13},{5,12},{6,15},{7,14},{8,1},{9,0},... | collective-permute-start | bytes 393224 | tf_op jit(solution)/shard_map/ppermute | solution.py:236
  150.3 13.6 %collective-permute-start.18 = (f32[32,8,128]{2,1,0:T(8,128)S(1)}, f32[32,8,128]{2,1,0:T(8,128)S(1)}, u32[]{:S(2)}, u32[]{:S(2)}) collective-permute-start(f32[32,8,128]{2,1,0:T(8,128)S(1)} %get-tuple-element.92), channel_id=1, source_target_pairs={{0,6},{1,7},{2,4},{3,5},{4,2},{5,3},{6,0},{7,1},{8,14},{9,15},{10,... | collective-permute-start | bytes 393224 | tf_op jit(solution)/shard_map/ppermute | solution.py:236
  151.3 18.3 %collective-permute-start.19 = (f32[32,8,128]{2,1,0:T(8,128)S(1)}, f32[32,8,128]{2,1,0:T(8,128)S(1)}, u32[]{:S(2)}, u32[]{:S(2)}) collective-permute-start(f32[32,8,128]{2,1,0:T(8,128)S(1)} %get-tuple-element.93), channel_id=1, source_target_pairs={{0,10},{1,11},{2,8},{3,9},{4,14},{5,15},{6,12},{7,13},{8,2},{9,3},... | collective-permute-start | bytes 393224 | tf_op jit(solution)/shard_map/ppermute | solution.py:236
  159.0 17.6 %collective-permute-start.21 = (f32[32,8,128]{2,1,0:T(8,128)S(1)}, f32[32,8,128]{2,1,0:T(8,128)S(1)}, u32[]{:S(2)}, u32[]{:S(2)}) collective-permute-start(f32[32,8,128]{2,1,0:T(8,128)S(1)} %get-tuple-element.95), channel_id=1, source_target_pairs={{0,11},{1,10},{2,9},{3,8},{4,15},{5,14},{6,13},{7,12},{8,3},{9,2},... | collective-permute-start | bytes 393224 | tf_op jit(solution)/shard_map/ppermute | solution.py:236
  162.8 15.8 %collective-permute-start.22 = (f32[32,8,128]{2,1,0:T(8,128)S(1)}, f32[32,8,128]{2,1,0:T(8,128)S(1)}, u32[]{:S(2)}, u32[]{:S(2)}) collective-permute-start(f32[32,8,128]{2,1,0:T(8,128)S(1)} %get-tuple-element.96), channel_id=1, source_target_pairs={{0,4},{1,5},{2,6},{3,7},{4,0},{5,1},{6,2},{7,3},{8,12},{9,13},{10,... | collective-permute-start | bytes 393224 | tf_op jit(solution)/shard_map/ppermute | solution.py:236
  163.9 15.3 %collective-permute-start.23 = (f32[32,8,128]{2,1,0:T(8,128)S(1)}, f32[32,8,128]{2,1,0:T(8,128)S(1)}, u32[]{:S(2)}, u32[]{:S(2)}) collective-permute-start(f32[32,8,128]{2,1,0:T(8,128)S(1)} %get-tuple-element.97), channel_id=1, source_target_pairs={{0,12},{1,13},{2,14},{3,15},{4,8},{5,9},{6,10},{7,11},{8,4},{9,5},... | collective-permute-start | bytes 393224 | tf_op jit(solution)/shard_map/ppermute | solution.py:236
  169.6 12.1 %collective-permute-start.24 = (f32[32,8,128]{2,1,0:T(8,128)S(1)}, f32[32,8,128]{2,1,0:T(8,128)S(1)}, u32[]{:S(2)}, u32[]{:S(2)}) collective-permute-start(f32[32,8,128]{2,1,0:T(8,128)S(1)} %get-tuple-element.98), channel_id=1, source_target_pairs={{0,3},{1,2},{2,1},{3,0},{4,7},{5,6},{6,5},{7,4},{8,11},{9,10},{10,... | collective-permute-start | bytes 393224 | tf_op jit(solution)/shard_map/ppermute | solution.py:236
  170.8 15.9 %collective-permute-start.25 = (f32[32,8,128]{2,1,0:T(8,128)S(1)}, f32[32,8,128]{2,1,0:T(8,128)S(1)}, u32[]{:S(2)}, u32[]{:S(2)}) collective-permute-start(f32[32,8,128]{2,1,0:T(8,128)S(1)} %get-tuple-element.99), channel_id=1, source_target_pairs={{0,2},{1,3},{2,0},{3,1},{4,6},{5,7},{6,4},{7,5},{8,10},{9,11},{10,... | collective-permute-start | bytes 393224 | tf_op jit(solution)/shard_map/ppermute | solution.py:236
  176.7 14.3 %collective-permute-start.26 = (f32[32,8,128]{2,1,0:T(8,128)S(1)}, f32[32,8,128]{2,1,0:T(8,128)S(1)}, u32[]{:S(2)}, u32[]{:S(2)}) collective-permute-start(f32[32,8,128]{2,1,0:T(8,128)S(1)} %get-tuple-element.100), channel_id=1, source_target_pairs={{0,13},{1,12},{2,15},{3,14},{4,9},{5,8},{6,11},{7,10},{8,5},{9,4},... | collective-permute-start | bytes 393224 | tf_op jit(solution)/shard_map/ppermute | solution.py:236
  178.6 12.4 %collective-permute-start.27 = (f32[32,8,128]{2,1,0:T(8,128)S(1)}, f32[32,8,128]{2,1,0:T(8,128)S(1)}, u32[]{:S(2)}, u32[]{:S(2)}) collective-permute-start(f32[32,8,128]{2,1,0:T(8,128)S(1)} %get-tuple-element.101), channel_id=1, source_target_pairs={{0,1},{1,0},{2,3},{3,2},{4,5},{5,4},{6,7},{7,6},{8,9},{9,8},{10,11... | collective-permute-start | bytes 393224 | tf_op jit(solution)/shard_map/ppermute | solution.py:236
  179.2 15.7 %collective-permute-start.28 = (f32[32,8,128]{2,1,0:T(8,128)S(1)}, f32[32,8,128]{2,1,0:T(8,128)S(1)}, u32[]{:S(2)}, u32[]{:S(2)}) collective-permute-start(f32[32,8,128]{2,1,0:T(8,128)S(1)} %get-tuple-element.102), channel_id=1, source_target_pairs={{0,14},{1,15},{2,12},{3,13},{4,10},{5,11},{6,8},{7,9},{8,6},{9,7},... | collective-permute-start | bytes 393224 | tf_op jit(solution)/shard_map/ppermute | solution.py:236
  181.7 16.1 %collective-permute-start.29 = (f32[32,8,128]{2,1,0:T(8,128)S(1)}, f32[32,8,128]{2,1,0:T(8,128)S(1)}, u32[]{:S(2)}, u32[]{:S(2)}) collective-permute-start(f32[32,8,128]{2,1,0:T(8,128)S(1)} %get-tuple-element.103), channel_id=1, source_target_pairs={{0,15},{1,14},{2,13},{3,12},{4,11},{5,10},{6,9},{7,8},{8,7},{9,6},... | collective-permute-start | bytes 393224 | tf_op jit(solution)/shard_map/ppermute | solution.py:236
  (21 other events, 804.4 us)

commit v2 on v1

v2 whole, which is shorter than its diff:
```python
import functools
import jax
import jax.numpy as jnp
from jax import lax
from jax.experimental import pallas as pl
from jax.experimental.pallas import tpu as pltpu
from jax.sharding import PartitionSpec as P

F32 = jnp.float32
BF16 = jnp.bfloat16
CHUNKS = 2
BLOCK = 8
VMEM_LIMIT = 24 * 1024 * 1024
FIRST_LIMIT = 60 * 1024 * 1024
GRAIN = 16
OUT_GRAIN = 4
LATE = 5


def split(value):
    high = value.astype(BF16)
    return high, (value - high.astype(F32)).astype(BF16)


def product(left, right):
    dot = functools.partial(jnp.dot, preferred_element_type=F32)
    rows = left[0].shape[0]
    both = dot(jnp.concatenate(left, axis=0), right[0])
    return both[:rows] + (both[rows:] + dot(left[0], right[1]))


def react(value, kinetics):
    rate, level = kinetics
    return value - rate * jnp.tanh(value - level)


def read_kinetics(species_ref, rates_ref, levels_ref):
    index = species_ref[0]
    return rates_ref[index], levels_ref[index]


def relative(index, block, own):
    return ((index // block) ^ own) * block + index % block


def picker(shape, along, source, flag, length):
    wanted = source(lax.broadcasted_iota(jnp.int32, shape, along))
    wanted = jnp.where(flag == 1, length - 1 - wanted, wanted)
    return jnp.where(lax.broadcasted_iota(jnp.int32, shape, 1 - along) == wanted, 1.0, 0.0).astype(BF16)


def combined(inverse, explicit):
    return jnp.dot(inverse, explicit, precision=lax.Precision.HIGHEST, preferred_element_type=F32)


def rearrange(pieces, rows, columns):
    dot = functools.partial(jnp.dot, preferred_element_type=F32)
    return tuple(dot(dot(rows, piece).astype(BF16), columns).astype(BF16) for piece in pieces)


def sending_order(ranks):
    half = ranks // 2
    order = []
    for index in range(half):
        order.append(half + index)
        order += [half - 1 - near for near in range(half - 1) if near - near // 5 == index]
    return order + [0]


def arrivals(ranks):
    order = sending_order(ranks)
    late = order[-1 - LATE : -1]
    early = [(chunk, place) for chunk in range(CHUNKS - 1) for place in order]
    early += [(CHUNKS - 1, place) for place in order if place not in late]
    return early, [(CHUNKS - 1, place) for place in late]


def by_place(refs):
    order = sending_order(len(refs))
    return [refs[order.index(place)] for place in range(len(refs))]


def position():
    return lax.axis_index("row"), lax.axis_index("col")


def first_sweep(chunk, columns, species, rates, levels, flags, explicit, inverse, field, *refs):
    blocks = by_place(refs[:-7])
    held, matrices, done, *small = refs[-7:]
    ranks = len(blocks)
    depth, each, width = blocks[0].shape
    length = field.shape[0]
    row, column = position()
    own = row * columns + column
    targets = [*small, matrices.at[0], matrices.at[1]] + [held.at[cell] for cell in range(depth)]
    sources = [species, rates, levels, flags, inverse, explicit]
    sources += [field.at[:, cell, :] for cell in range(depth)]
    copies = [
        pltpu.make_async_copy(source, target, done.at[index])
        for index, (source, target) in enumerate(zip(sources, targets))
    ]
    for copy in copies:
        copy.start()
    for copy in copies[:-depth]:
        copy.wait()
    species, rates, levels, flags = small
    share = ranks * each
    flag = flags[0, 0]
    matrix = rearrange(
        split(combined(matrices[0], matrices[1])),
        picker((share, length), 0, lambda i: chunk * share + relative(i, each, own), flag, length),
        picker((length, length), 1, lambda i: i, flag, length),
    )
    kinetics = read_kinetics(species, rates, levels)
    for cell in range(0, depth, 2):
        if cell % GRAIN == 0:
            for copy in copies[len(copies) - depth + cell :][:GRAIN]:
                copy.wait()
        value = jnp.concatenate([held[cell], held[cell + 1]], axis=1)
        result = product(matrix, split(react(value, kinetics)))
        for half in range(2):
            piece = result[:, half * width : (half + 1) * width].reshape(ranks, each, width)
            for place in range(ranks):
                blocks[place][cell + half] = piece[place]


def block_sums(blocks, cell, matrix, kinetics):
    value = jnp.concatenate(
        [jnp.concatenate([block[cell + half] for block in blocks], axis=0) for half in range(2)], axis=1
    )
    return product(matrix, split(react(value, kinetics)))


def partial_sums(kinetics, high, low, *refs):
    blocks, out = refs[:-1], refs[-1]
    depth, _, width = out.shape
    for cell in range(0, depth, 2):
        index = pl.program_id(0) * depth + cell
        result = block_sums(blocks, index, (high[...], low[...]), (kinetics[0:1, :], kinetics[1:2, :]))
        out[cell] = result[:, :width]
        out[cell + 1] = result[:, width:]


def last_sweep(kinetics, high, low, *refs):
    blocks, (total, out, held, done) = refs[:-4], refs[-4:]
    depth, _, width = held.shape
    copies = [
        pltpu.make_async_copy(held.at[cell], out.at[:, cell, :], done.at[cell]) for cell in range(depth)
    ]
    for cell in range(0, depth, 2):
        result = block_sums(blocks, cell, (high[...], low[...]), (kinetics[0:1, :], kinetics[1:2, :]))
        held[cell] = result[:, :width] + total[cell]
        held[cell + 1] = result[:, width:] + total[cell + 1]
        if (cell + 2) % OUT_GRAIN == 0:
            for copy in copies[cell + 2 - OUT_GRAIN : cell + 2]:
                copy.start()
    for copy in copies:
        copy.wait()


def prepare(columns, depth, width, each, species, rates, levels, flags, explicit_line, inverse_line,
            explicit_depth, inverse_depth, kinetics, high, low, *last):
    row, column = position()
    rate, level = read_kinetics(species, rates, levels)
    kinetics[0:1, :] = jnp.full((1, kinetics.shape[1]), rate, F32)
    kinetics[1:2, :] = jnp.full((1, kinetics.shape[1]), level, F32)
    line = split(combined(inverse_line[...], explicit_line[...]))
    deep = split(combined(inverse_depth[...], explicit_depth[...]).T)
    shape = line[0].shape
    for place, (pieces, step, axis_dim) in enumerate(
        [(line, 0, 1), (deep, 0, 2), (deep, 1, 2), (line, 1, 1)]
    ):
        own, block = (row, depth) if axis_dim == 1 else (column, width)
        flag = flags[step, axis_dim]
        high[place], low[place] = rearrange(
            pieces,
            *[picker(shape, along, lambda i: relative(i, block, own), flag, shape[0]) for along in range(2)],
        )
    own = row * columns + column
    rows = picker(shape, 0, lambda i: i, flags[1, 0], shape[0])
    for blocks, high, low in zip(arrivals(shape[0] // CHUNKS // each), last[0::2], last[1::2]):

        def source(index):
            cell = index % each
            for number, (chunk, place) in enumerate(blocks):
                start = chunk * (shape[0] // CHUNKS) + (place ^ own) * each
                cell = jnp.where(index // each == number, start + index % each, cell)
            return cell

        selected = (shape[0], len(blocks) * each)
        high[...], low[...] = rearrange(line, rows, picker(selected, 1, source, flags[1, 0], shape[0]))


def plane_sweeps(columns, ranks, kinetics, high, low, *refs):
    refs, field = refs[:-1], refs[-1]
    groups = [by_place(refs[i : i + ranks]) for i in range(0, len(refs), ranks)]
    depths = [group[0].shape[0] for group in groups]
    _, each, width = groups[0][0].shape
    rows = ranks // columns
    depth = high.shape[1] // rows
    splits = next(i for i in range(len(groups)) if sum(depths[:i]) == depth)
    ins, outs = groups[:splits], groups[splits:]
    rate_level = (kinetics[0:1, :], kinetics[1:2, :])
    for place in range(ranks):
        start = place // columns * depth
        lanes = slice(place % columns * width, (place % columns + 1) * width)
        for group in ins:
            for line in range(0, group[place].shape[0], BLOCK):
                field[:, start + line : start + line + BLOCK, lanes] = jnp.swapaxes(
                    group[place][line : line + BLOCK], 0, 1
                )
            start += group[place].shape[0]
    for cell in range(each):
        value = field[cell]
        for place in range(4):
            pieces = split(react(value, rate_level))
            matrix = (high[place], low[place])
            value = product(matrix, pieces) if place in (0, 3) else product(pieces, matrix)
        field[cell] = value
    for place in range(ranks):
        start = place // columns * depth
        lanes = slice(place % columns * width, (place % columns + 1) * width)
        for group in outs:
            for line in range(0, group[place].shape[0], BLOCK):
                group[place][line : line + BLOCK] = jnp.swapaxes(
                    field[:, start + line : start + line + BLOCK, lanes], 0, 1
                )
            start += group[place].shape[0]


PARAMS = pltpu.CompilerParams(vmem_limit_bytes=VMEM_LIMIT)
VMEM = pl.BlockSpec(memory_space=pltpu.VMEM)
HBM = pl.BlockSpec(memory_space=pltpu.HBM)


def scalars(shape):
    return pl.BlockSpec(shape, lambda i: (0,) * len(shape), memory_space=pltpu.SMEM)


def whole(shape):
    return pl.BlockSpec(shape, lambda i: (0,) * len(shape))


def cost(cells, length, sweeps, bytes_accessed):
    return pl.CostEstimate(
        flops=6 * cells * length * sweeps, bytes_accessed=bytes_accessed, transcendentals=cells * sweeps
    )


def fast(rows, columns, concentration, species, reaction_rates, levels, sweep_flags,
         explicit_line, inverse_line, explicit_depth, inverse_depth):
    lines, depth, width = concentration.shape
    ranks = rows * columns
    share = lines // CHUNKS
    each = share // ranks
    size = lines * depth * width
    scalar_arrays = (species, reaction_rates, levels, sweep_flags)
    scalar_specs = [scalars(array.shape) for array in scalar_arrays]
    order = sending_order(ranks)

    def exchange(blocks):
        return [
            lax.ppermute(block, ("row", "col"), [(i, i ^ place) for i in range(ranks)]) if place else block
            for place, block in zip(order, blocks)
        ]

    def block_shapes(count):
        return [jax.ShapeDtypeStruct((count, each, width), F32)] * ranks

    def first(chunk):
        return pl.pallas_call(
            functools.partial(first_sweep, chunk, columns),
            grid=(1,),
            in_specs=[HBM] * 7,
            out_specs=[VMEM] * ranks,
            out_shape=block_shapes(depth),
            scratch_shapes=[
                pltpu.VMEM((depth, lines, width), F32),
                pltpu.VMEM((2, lines, lines), F32),
                pltpu.SemaphoreType.DMA((depth + 2 + len(scalar_arrays),)),
                *[pltpu.SMEM(array.shape, array.dtype) for array in scalar_arrays],
            ],
            compiler_params=PARAMS if chunk else pltpu.CompilerParams(vmem_limit_bytes=FIRST_LIMIT),
            cost_estimate=cost(size // CHUNKS, lines, 1, 4 * (size + size // CHUNKS)),
            name=f"first_sweep_{chunk}",
        )(*scalar_arrays, explicit_line, inverse_line, concentration)

    def planes(pieces, chunk, parts):
        outs = pl.pallas_call(
            functools.partial(plane_sweeps, columns, ranks),
            grid=(1,),
            in_specs=[VMEM] * (3 + ranks * len(pieces)),
            out_specs=[VMEM] * (ranks * len(parts)),
            out_shape=[shape for _, count in parts for shape in block_shapes(count)],
            scratch_shapes=[pltpu.VMEM((each, lines, lines), F32)],
            compiler_params=PARAMS,
            cost_estimate=cost(size // CHUNKS, lines, 4, 8 * size // CHUNKS),
            name=f"plane_sweeps_{chunk}",
        )(kinetics, high, low, *[block for blocks in pieces for block in blocks])
        return [outs[i * ranks : (i + 1) * ranks] for i in range(len(parts))]

    def early_sums(blocks, matrix):
        return pl.pallas_call(
            partial_sums,
            grid=(depth // BLOCK,),
            in_specs=[VMEM] * (3 + len(blocks)),
            out_specs=pl.BlockSpec((BLOCK, lines, width), lambda i: (i, 0, 0)),
            out_shape=jax.ShapeDtypeStruct((depth, lines, width), F32),
            compiler_params=PARAMS,
            cost_estimate=cost(size // CHUNKS, lines, 1, 4 * (size + size // CHUNKS)),
            name="partial_sums",
        )(kinetics, *matrix, *blocks)

    def last(blocks, matrix, total):
        return pl.pallas_call(
            last_sweep,
            grid=(1,),
            in_specs=[VMEM] * (4 + len(blocks)),
            out_specs=HBM,
            out_shape=jax.ShapeDtypeStruct((lines, depth, width), F32),
            scratch_shapes=[pltpu.VMEM((depth, lines, width), F32), pltpu.SemaphoreType.DMA((depth,))],
            compiler_params=PARAMS,
            cost_estimate=cost(size // CHUNKS, lines, 1, 4 * (size + size // CHUNKS)),
            name="last_sweep",
        )(kinetics, *matrix, *blocks, total)

    matrix_spec = whole((lines, lines))
    outputs = [
        jax.ShapeDtypeStruct((2, 2 * width), F32),
        *[jax.ShapeDtypeStruct((4, lines, lines), BF16)] * 2,
        *[
            jax.ShapeDtypeStruct((lines, len(blocks) * each), BF16)
            for blocks in arrivals(ranks)
            for _ in range(2)
        ],
    ]
    kinetics, high, low, *last_matrices = pl.pallas_call(
        functools.partial(prepare, columns, depth, width, each),
        grid=(1,),
        in_specs=scalar_specs + [matrix_spec] * 4,
        out_specs=[whole(output.shape) for output in outputs],
        out_shape=outputs,
        compiler_params=PARAMS,
        cost_estimate=cost(lines * lines, lines, 8, 8 * 4 * lines * lines),
        name="prepare",
    )(*scalar_arrays, explicit_line, inverse_line, explicit_depth, inverse_depth)

    there = [exchange(first(chunk)) for chunk in range(CHUNKS)]
    back = [exchange(planes([there[chunk]], chunk, [(0, depth)])[0]) for chunk in range(CHUNKS)]
    early, late = [
        [back[chunk][order.index(place)] for chunk, place in blocks] for blocks in arrivals(ranks)
    ]
    return last(late, last_matrices[2:], early_sums(early, last_matrices[:2]))


def oriented(matrix, reflect):
    return jnp.where(reflect == 1, matrix[::-1, ::-1], matrix)


def plain(concentration, species, reaction_rates, levels, sweep_flags,
          explicit_line, inverse_line, explicit_depth, inverse_depth):
    kinetics = (reaction_rates[species[0]], levels[species[0]])
    matmul = functools.partial(jnp.einsum, precision=lax.Precision.HIGHEST)
    line = matmul("ij,jk->ik", inverse_line, explicit_line)
    deep = matmul("ij,jk->ik", inverse_depth, explicit_depth)
    letters = ["ij,jbc->ibc", "ij,ajc->aic", "ij,abj->abi"]

    def sweep(value, step, axis_dim):
        matrix = oriented(deep if axis_dim == 2 else line, sweep_flags[step, axis_dim])
        return matmul(letters[axis_dim], matrix, react(value, kinetics))

    def regroup(value):
        value = lax.all_to_all(value, "row", split_axis=0, concat_axis=1, tiled=True)
        return lax.all_to_all(value, "col", split_axis=0, concat_axis=2, tiled=True)

    def restore(value):
        value = lax.all_to_all(value, "col", split_axis=2, concat_axis=0, tiled=True)
        return lax.all_to_all(value, "row", split_axis=1, concat_axis=0, tiled=True)

    value, home = concentration, True
    for step in range(sweep_flags.shape[0]):
        for axis_dim in [0, 1, 2] if step % 2 == 0 else [2, 1, 0]:
            if home != (axis_dim == 0):
                value = restore(value) if axis_dim == 0 else regroup(value)
                home = axis_dim == 0
            value = sweep(value, step, axis_dim)
    return value if home else restore(value)


def solution(mesh):
    rows, columns = mesh.shape["row"], mesh.shape["col"]
    ranks = rows * columns

    def on_device(*args):
        lines, depth, width = args[0].shape
        fits = (
            args[4].shape[0] == 2
            and ranks & (ranks - 1) == 0
            and ranks >= 2
            and lines % (ranks * CHUNKS * 8) == 0
            and depth % BLOCK == 0
            and width % 128 == 0
            and depth * rows == lines
            and width * columns == args[7].shape[0] == lines
            and 2 * width == lines
        )
        if fits:
            return fast(rows, columns, *args)
        return plain(*args)

    in_specs = (P("groups", "row", "col"), P("groups"), P(), P(), P(), P(), P(), P(), P())
    return jax.shard_map(
        on_device, mesh=mesh, in_specs=in_specs, out_specs=P("groups", "row", "col"), check_vma=False
    )
```

time: 204 us -> 199 us (0.975)
  Pallas kernels: 44.4 us -> 35.3 us
  starting transfers between devices: 112 us -> 118 us
  waiting for transfers between devices: 47 us -> 42.4 us
  local copies, waits for them, and re-layouts: 0.05 us -> 2.21 us
    pallas_call x7, Pallas kernels: 44.4 us -> 35.3 us  [the longest x2 14.8 us: planes(): pl.pallas_call(functools.partial(plane_sweeps, columns, ranks), grid=(1,)...]
    ppermute x60, starting transfers between devices: 112 us -> 118 us  [exchange(): lax.ppermute(block, ('row', 'col'), [(i, i ^ place) for i in range(ranks)])]
    ppermute x60, waiting for transfers between devices: 47 us -> 42.4 us  [exchange(): lax.ppermute(block, ('row', 'col'), [(i, i ^ place) for i in range(ranks)])]
    unnamed x18, local copies, waits for them, and re-layouts: 0.05 us -> 2.21 us
  transfers between devices with their start and end apart: 60 -> 60, of which waited for: 22 -> 19; matrix products, arithmetic and copies ran while one was open for 0% -> 0% of each run, Pallas kernels for 15% -> 14%
where the time goes in v2:
time: 199 us
  starting transfers between devices  118 us (59%)
  waiting for transfers between devices  42.4 us (21%)
  Pallas kernels  35.3 us (18%)
  local copies, waits for them, and re-layouts  2.21 us (1%)
    ppermute x60, starting transfers between devices, exchange(): lax.ppermute(block, ('row', 'col'), [(i, i ^ place) for i in range(ranks)])  118 us
    ppermute x60, waiting for transfers between devices, exchange(): lax.ppermute(block, ('row', 'col'), [(i, i ^ place) for i in range(ranks)])  42.4 us
    pallas_call x2, Pallas kernels, planes(): pl.pallas_call(functools.partial(plane_sweeps, columns, ranks), grid=(1,)...  14.8 us
    pallas_call x2, Pallas kernels, first(): pl.pallas_call(functools.partial(first_sweep, chunk, columns), grid=(1,),...  12.7 us
  transfers between devices with their start and end apart: 60, of which 19 were waited for; matrix products, arithmetic and copies ran while one was open for 0% of the time, Pallas kernels for 14%

profile of v2, /device:TPU:17, one launch (start us, length us, event | category | flops | bytes accessed | tf_op | source)
XLA Modules:
  0.0 199.1 jit_solution(16742633971229041694)
XLA Ops:
  0.7 5.2 %first_sweep_0.1 = (f32[32,8,128]{2,1,0:T(8,128)}, f32[32,8,128]{2,1,0:T(8,128)}, f32[32,8,128]{2,1,0:T(8,128)}, f32[32,8,128]{2,1,0:T(8,128)}, f32[32,8,128]{2,...) custom-call(s32[1]{0:T(128)S(6)} %copy.10.species, ...), custom_call_target="tpu_custom_call" | custom-call | flops 805306368 | bytes 6291456 | tf_op jit(solution)/shard_map/first_sweep_0/pallas_call | solution.py:271
  6.1 3.1 %collective-permute-start.21 = (f32[32,8,128]{2,1,0:T(8,128)}, f32[32,8,128]{2,1,0:T(8,128)S(1)}, u32[]{:S(2)}, u32[]{:S(2)}) collective-permute-start(f32[32,8,128]{2,1,0:T(8,128)} %get-tuple-element.105), channel_id=1, source_target_pairs={{0,7},{1,6},{2,5},{3,4},{4,3},{5,2},{6,1},{7,0},{8,15},{9,14},{10,... | collective-permute-start | bytes 393224 | tf_op jit(solution)/shard_map/ppermute | solution.py:263
  9.2 1.7 collective-permute-start.22
  12.6 4.8 %collective-permute-start.25 = (f32[32,8,128]{2,1,0:T(8,128)}, f32[32,8,128]{2,1,0:T(8,128)S(1)}, u32[]{:S(2)}, u32[]{:S(2)}) collective-permute-start(f32[32,8,128]{2,1,0:T(8,128)} %get-tuple-element.109), channel_id=1, source_target_pairs={{0,5},{1,4},{2,7},{3,6},{4,1},{5,0},{6,3},{7,2},{8,13},{9,12},{10,... | collective-permute-start | bytes 393224 | tf_op jit(solution)/shard_map/ppermute | solution.py:263
  17.4 2.5 %collective-permute-start.26 = (f32[32,8,128]{2,1,0:T(8,128)}, f32[32,8,128]{2,1,0:T(8,128)S(1)}, u32[]{:S(2)}, u32[]{:S(2)}) collective-permute-start(f32[32,8,128]{2,1,0:T(8,128)} %get-tuple-element.110), channel_id=1, source_target_pairs={{0,11},{1,10},{2,9},{3,8},{4,15},{5,14},{6,13},{7,12},{8,3},{9,2},... | collective-permute-start | bytes 393224 | tf_op jit(solution)/shard_map/ppermute | solution.py:263
  19.9 2.6 %collective-permute-start.27 = (f32[32,8,128]{2,1,0:T(8,128)}, f32[32,8,128]{2,1,0:T(8,128)S(1)}, u32[]{:S(2)}, u32[]{:S(2)}) collective-permute-start(f32[32,8,128]{2,1,0:T(8,128)} %get-tuple-element.111), channel_id=1, source_target_pairs={{0,4},{1,5},{2,6},{3,7},{4,0},{5,1},{6,2},{7,3},{8,12},{9,13},{10,... | collective-permute-start | bytes 393224 | tf_op jit(solution)/shard_map/ppermute | solution.py:263
  24.2 2.9 %collective-permute-start.29 = (f32[32,8,128]{2,1,0:T(8,128)}, f32[32,8,128]{2,1,0:T(8,128)S(1)}, u32[]{:S(2)}, u32[]{:S(2)}) collective-permute-start(f32[32,8,128]{2,1,0:T(8,128)} %get-tuple-element.113), channel_id=1, source_target_pairs={{0,3},{1,2},{2,1},{3,0},{4,7},{5,6},{6,5},{7,4},{8,11},{9,10},{10,... | collective-permute-start | bytes 393224 | tf_op jit(solution)/shard_map/ppermute | solution.py:263
  27.8 3.3 %collective-permute-done.26.refs_6_ = f32[32,8,128]{2,1,0:T(8,128)S(1)} collective-permute-done((f32[32,8,128]{2,1,0:T(8,128)}, f32[32,8,128]{2,1,0:T(8,128)S(1)}, u32[]{:S(2)}, u32[]{:S(2)}) %collective-permute-start.26) | collective-permute-done | bytes 131104 | tf_op jit(solution)/shard_map/ppermute | solution.py:263
  32.2 2.9 %collective-permute-done.27.refs_7_ = f32[32,8,128]{2,1,0:T(8,128)S(1)} collective-permute-done((f32[32,8,128]{2,1,0:T(8,128)}, f32[32,8,128]{2,1,0:T(8,128)S(1)}, u32[]{:S(2)}, u32[]{:S(2)}) %collective-permute-start.27) | collective-permute-done | bytes 131104 | tf_op jit(solution)/shard_map/ppermute | solution.py:263
  35.0 3.0 %collective-permute-done.28.refs_8_ = f32[32,8,128]{2,1,0:T(8,128)S(1)} collective-permute-done((f32[32,8,128]{2,1,0:T(8,128)}, f32[32,8,128]{2,1,0:T(8,128)S(1)}, u32[]{:S(2)}, u32[]{:S(2)}) %collective-permute-start.28) | collective-permute-done | bytes 131104 | tf_op jit(solution)/shard_map/ppermute | solution.py:263
  38.2 4.1 %collective-permute-start.34 = (f32[32,8,128]{2,1,0:T(8,128)}, f32[32,8,128]{2,1,0:T(8,128)S(1)}, u32[]{:S(2)}, u32[]{:S(2)}) collective-permute-start(f32[32,8,128]{2,1,0:T(8,128)} %get-tuple-element.118), channel_id=1, source_target_pairs={{0,15},{1,14},{2,13},{3,12},{4,11},{5,10},{6,9},{7,8},{8,7},{9,6},... | collective-permute-start | bytes 393224 | tf_op jit(solution)/shard_map/ppermute | solution.py:263
  42.3 2.2 %copy-done = f32[256,32,128]{2,1,0:T(8,128)S(1)} copy-done((f32[256,32,128]{2,1,0:T(8,128)S(1)}, f32[256,32,128]{2,1,0:T(8,128)}, u32[]{:S(2)}) %copy-start) | copy-done | bytes 4194328
  44.5 7.4 %first_sweep_1.1 = (f32[32,8,128]{2,1,0:T(8,128)S(1)}, f32[32,8,128]{2,1,0:T(8,128)S(1)}, f32[32,8,128]{2,1,0:T(8,128)S(1)}, f32[32,8,128]{2,1,0:T(8,128)S(1)}, ...) custom-call(s32[1]{0:T(128)S(6)} %copy.10.species, ...), custom_call_target="tpu_custom_call" | custom-call | flops 805306368 | bytes 6291456 | tf_op jit(solution)/shard_map/first_sweep_1/pallas_call | solution.py:271
  53.5 2.7 %collective-permute-start.2 = (f32[32,8,128]{2,1,0:T(8,128)S(1)}, f32[32,8,128]{2,1,0:T(8,128)S(1)}, u32[]{:S(2)}, u32[]{:S(2)}) collective-permute-start(f32[32,8,128]{2,1,0:T(8,128)S(1)} %get-tuple-element.83), channel_id=1, source_target_pairs={{0,9},{1,8},{2,11},{3,10},{4,13},{5,12},{6,15},{7,14},{8,1},{9,0},... | collective-permute-start | bytes 393224 | tf_op jit(solution)/shard_map/ppermute | solution.py:263
  57.1 8.2 %collective-permute-start.4 = (f32[32,8,128]{2,1,0:T(8,128)S(1)}, f32[32,8,128]{2,1,0:T(8,128)S(1)}, u32[]{:S(2)}, u32[]{:S(2)}) collective-permute-start(f32[32,8,128]{2,1,0:T(8,128)S(1)} %get-tuple-element.85), channel_id=1, source_target_pairs={{0,10},{1,11},{2,8},{3,9},{4,14},{5,15},{6,12},{7,13},{8,2},{9,3},... | collective-permute-start | bytes 393224 | tf_op jit(solution)/shard_map/ppermute | solution.py:263
  65.3 2.4 %collective-permute-start.5 = (f32[32,8,128]{2,1,0:T(8,128)S(1)}, f32[32,8,128]{2,1,0:T(8,128)S(1)}, u32[]{:S(2)}, u32[]{:S(2)}) collective-permute-start(f32[32,8,128]{2,1,0:T(8,128)S(1)} %get-tuple-element.86), channel_id=1, source_target_pairs={{0,5},{1,4},{2,7},{3,6},{4,1},{5,0},{6,3},{7,2},{8,13},{9,12},{10,... | collective-permute-start | bytes 393224 | tf_op jit(solution)/shard_map/ppermute | solution.py:263
  67.9 5.1 %collective-permute-start.7 = (f32[32,8,128]{2,1,0:T(8,128)S(1)}, f32[32,8,128]{2,1,0:T(8,128)S(1)}, u32[]{:S(2)}, u32[]{:S(2)}) collective-permute-start(f32[32,8,128]{2,1,0:T(8,128)S(1)} %get-tuple-element.88), channel_id=1, source_target_pairs={{0,4},{1,5},{2,6},{3,7},{4,0},{5,1},{6,2},{7,3},{8,12},{9,13},{10,... | collective-permute-start | bytes 393224 | tf_op jit(solution)/shard_map/ppermute | solution.py:263
  73.0 1.7 collective-permute-start.8
  74.7 2.2 %collective-permute-done.4.refs_4_ = f32[32,8,128]{2,1,0:T(8,128)S(1)} collective-permute-done((f32[32,8,128]{2,1,0:T(8,128)S(1)}, f32[32,8,128]{2,1,0:T(8,128)S(1)}, u32[]{:S(2)}, u32[]{:S(2)}) %collective-permute-start.4) | collective-permute-done | bytes 131104 | tf_op jit(solution)/shard_map/ppermute | solution.py:263
  76.9 2.3 %prepare.1 = (f32[2,256]{1,0:T(2,128)S(1)}, bf16[4,256,256]{2,1,0:T(8,128)(2,1)S(1)}, bf16[4,256,256]{2,1,0:T(8,128)(2,1)S(1)}, bf16[256,216]{1,0:T(8,128)(2,1)S...) custom-call(s32[1]{0:T(128)S(6)} %copy.10.species, f32[64]{0:T(128)S(1)} %copy-done.4, ...), custom_call_target="tpu_custom_call" | custom-call | flops 805306368 | bytes 2097152 | tf_op jit(solution)/shard_map/prepare/pallas_call | solution.py:337
  79.7 3.0 %collective-permute-start.11 = (f32[32,8,128]{2,1,0:T(8,128)S(1)}, f32[32,8,128]{2,1,0:T(8,128)S(1)}, u32[]{:S(2)}, u32[]{:S(2)}) collective-permute-start(f32[32,8,128]{2,1,0:T(8,128)S(1)} %get-tuple-element.92), channel_id=1, source_target_pairs={{0,13},{1,12},{2,15},{3,14},{4,9},{5,8},{6,11},{7,10},{8,5},{9,4},... | collective-permute-start | bytes 393224 | tf_op jit(solution)/shard_map/ppermute | solution.py:263
  83.4 2.1 %collective-permute-start.12 = (f32[32,8,128]{2,1,0:T(8,128)S(1)}, f32[32,8,128]{2,1,0:T(8,128)S(1)}, u32[]{:S(2)}, u32[]{:S(2)}) collective-permute-start(f32[32,8,128]{2,1,0:T(8,128)S(1)} %get-tuple-element.93), channel_id=1, source_target_pairs={{0,1},{1,0},{2,3},{3,2},{4,5},{5,4},{6,7},{7,6},{8,9},{9,8},{10,11... | collective-permute-start | bytes 393224 | tf_op jit(solution)/shard_map/ppermute | solution.py:263
  85.9 2.7 %collective-permute-start.14 = (f32[32,8,128]{2,1,0:T(8,128)S(1)}, f32[32,8,128]{2,1,0:T(8,128)S(1)}, u32[]{:S(2)}, u32[]{:S(2)}) collective-permute-start(f32[32,8,128]{2,1,0:T(8,128)S(1)} %get-tuple-element.95), channel_id=1, source_target_pairs={{0,15},{1,14},{2,13},{3,12},{4,11},{5,10},{6,9},{7,8},{8,7},{9,6},... | collective-permute-start | bytes 393224 | tf_op jit(solution)/shard_map/ppermute | solution.py:263
  88.6 7.5 %plane_sweeps_0.1 = (f32[32,8,128]{2,1,0:T(8,128)S(1)}, f32[32,8,128]{2,1,0:T(8,128)S(1)}, f32[32,8,128]{2,1,0:T(8,128)S(1)}, f32[32,8,128]{2,1,0:T(8,128)S(1)},...) custom-call(f32[2,256]{1,0:T(2,128)S(1)} %get-tuple-element.76.kinet, ...), custom_call_target="tpu_custom_call" | custom-call | flops 3221225472 | bytes 4194304 | tf_op jit(solution)/shard_map/plane_sweeps_0/pallas_call | solution.py:289
  96.1 5.8 %collective-permute-start.35 = (f32[32,8,128]{2,1,0:T(8,128)S(1)}, f32[32,8,128]{2,1,0:T(8,128)S(1)}, u32[]{:S(2)}, u32[]{:S(2)}) collective-permute-start(f32[32,8,128]{2,1,0:T(8,128)S(1)} %get-tuple-element.120), channel_id=1, source_target_pairs={{0,8},{1,9},{2,10},{3,11},{4,12},{5,13},{6,14},{7,15},{8,0},{9,1},... | collective-permute-start | bytes 393224 | tf_op jit(solution)/shard_map/ppermute | solution.py:263
  102.3 2.4 %collective-permute-start.38 = (f32[32,8,128]{2,1,0:T(8,128)S(1)}, f32[32,8,128]{2,1,0:T(8,128)S(1)}, u32[]{:S(2)}, u32[]{:S(2)}) collective-permute-start(f32[32,8,128]{2,1,0:T(8,128)S(1)} %get-tuple-element.123), channel_id=1, source_target_pairs={{0,6},{1,7},{2,4},{3,5},{4,2},{5,3},{6,0},{7,1},{8,14},{9,15},{10,... | collective-permute-start | bytes 393224 | tf_op jit(solution)/shard_map/ppermute | solution.py:263
  104.7 3.4 %collective-permute-done.14.refs_14_ = f32[32,8,128]{2,1,0:T(8,128)S(1)} collective-permute-done((f32[32,8,128]{2,1,0:T(8,128)S(1)}, f32[32,8,128]{2,1,0:T(8,128)S(1)}, u32[]{:S(2)}, u32[]{:S(2)}) %collective-permute-start.14) | collective-permute-done | bytes 131104 | tf_op jit(solution)/shard_map/ppermute | solution.py:263
  108.1 2.9 %collective-permute-done.35.refs_0_ = f32[32,8,128]{2,1,0:T(8,128)S(1)} collective-permute-done((f32[32,8,128]{2,1,0:T(8,128)S(1)}, f32[32,8,128]{2,1,0:T(8,128)S(1)}, u32[]{:S(2)}, u32[]{:S(2)}) %collective-permute-start.35) | collective-permute-done | bytes 131104 | tf_op jit(solution)/shard_map/ppermute | solution.py:263
  111.1 2.2 %collective-permute-start.40 = (f32[32,8,128]{2,1,0:T(8,128)S(1)}, f32[32,8,128]{2,1,0:T(8,128)S(1)}, u32[]{:S(2)}, u32[]{:S(2)}) collective-permute-start(f32[32,8,128]{2,1,0:T(8,128)S(1)} %get-tuple-element.125), channel_id=1, source_target_pairs={{0,5},{1,4},{2,7},{3,6},{4,1},{5,0},{6,3},{7,2},{8,13},{9,12},{10,... | collective-permute-start | bytes 393224 | tf_op jit(solution)/shard_map/ppermute | solution.py:263
  115.4 5.3 %collective-permute-start.43 = (f32[32,8,128]{2,1,0:T(8,128)S(1)}, f32[32,8,128]{2,1,0:T(8,128)S(1)}, u32[]{:S(2)}, u32[]{:S(2)}) collective-permute-start(f32[32,8,128]{2,1,0:T(8,128)S(1)} %get-tuple-element.128), channel_id=1, source_target_pairs={{0,12},{1,13},{2,14},{3,15},{4,8},{5,9},{6,10},{7,11},{8,4},{9,5},... | collective-permute-start | bytes 393224 | tf_op jit(solution)/shard_map/ppermute | solution.py:263
  120.8 3.9 %collective-permute-start.45 = (f32[32,8,128]{2,1,0:T(8,128)S(1)}, f32[32,8,128]{2,1,0:T(8,128)S(1)}, u32[]{:S(2)}, u32[]{:S(2)}) collective-permute-start(f32[32,8,128]{2,1,0:T(8,128)S(1)} %get-tuple-element.130), channel_id=1, source_target_pairs={{0,2},{1,3},{2,0},{3,1},{4,6},{5,7},{6,4},{7,5},{8,10},{9,11},{10,... | collective-permute-start | bytes 393224 | tf_op jit(solution)/shard_map/ppermute | solution.py:263
  125.4 3.6 %collective-permute-start.47 = (f32[32,8,128]{2,1,0:T(8,128)S(1)}, f32[32,8,128]{2,1,0:T(8,128)S(1)}, u32[]{:S(2)}, u32[]{:S(2)}) collective-permute-start(f32[32,8,128]{2,1,0:T(8,128)S(1)} %get-tuple-element.132), channel_id=1, source_target_pairs={{0,1},{1,0},{2,3},{3,2},{4,5},{5,4},{6,7},{7,6},{8,9},{9,8},{10,11... | collective-permute-start | bytes 393224 | tf_op jit(solution)/shard_map/ppermute | solution.py:263
  131.7 5.5 %collective-permute-start.49 = (f32[32,8,128]{2,1,0:T(8,128)S(1)}, f32[32,8,128]{2,1,0:T(8,128)S(1)}, u32[]{:S(2)}, u32[]{:S(2)}) collective-permute-start(f32[32,8,128]{2,1,0:T(8,128)S(1)} %get-tuple-element.134), channel_id=1, source_target_pairs={{0,15},{1,14},{2,13},{3,12},{4,11},{5,10},{6,9},{7,8},{8,7},{9,6},... | collective-permute-start | bytes 393224 | tf_op jit(solution)/shard_map/ppermute | solution.py:263
  137.2 7.3 %plane_sweeps_1.1 = (f32[32,8,128]{2,1,0:T(8,128)S(1)}, f32[32,8,128]{2,1,0:T(8,128)S(1)}, f32[32,8,128]{2,1,0:T(8,128)S(1)}, f32[32,8,128]{2,1,0:T(8,128)S(1)},...) custom-call(f32[2,256]{1,0:T(2,128)S(1)} %get-tuple-element.76.kinet, ...), custom_call_target="tpu_custom_call" | custom-call | flops 3221225472 | bytes 4194304 | tf_op jit(solution)/shard_map/plane_sweeps_1/pallas_call | solution.py:289
  146.1 2.4 %collective-permute-start.52 = (f32[32,8,128]{2,1,0:T(8,128)S(1)}, f32[32,8,128]{2,1,0:T(8,128)S(1)}, u32[]{:S(2)}, u32[]{:S(2)}) collective-permute-start(f32[32,8,128]{2,1,0:T(8,128)S(1)} %get-tuple-element.138), channel_id=1, source_target_pairs={{0,9},{1,8},{2,11},{3,10},{4,13},{5,12},{6,15},{7,14},{8,1},{9,0},... | collective-permute-start | bytes 393224 | tf_op jit(solution)/shard_map/ppermute | solution.py:263
  149.6 7.6 %collective-permute-start.54 = (f32[32,8,128]{2,1,0:T(8,128)S(1)}, f32[32,8,128]{2,1,0:T(8,128)S(1)}, u32[]{:S(2)}, u32[]{:S(2)}) collective-permute-start(f32[32,8,128]{2,1,0:T(8,128)S(1)} %get-tuple-element.140), channel_id=1, source_target_pairs={{0,10},{1,11},{2,8},{3,9},{4,14},{5,15},{6,12},{7,13},{8,2},{9,3},... | collective-permute-start | bytes 393224 | tf_op jit(solution)/shard_map/ppermute | solution.py:263
  157.2 4.8 %collective-permute-start.56 = (f32[32,8,128]{2,1,0:T(8,128)S(1)}, f32[32,8,128]{2,1,0:T(8,128)S(1)}, u32[]{:S(2)}, u32[]{:S(2)}) collective-permute-start(f32[32,8,128]{2,1,0:T(8,128)S(1)} %get-tuple-element.142), channel_id=1, source_target_pairs={{0,11},{1,10},{2,9},{3,8},{4,15},{5,14},{6,13},{7,12},{8,3},{9,2},... | collective-permute-start | bytes 393224 | tf_op jit(solution)/shard_map/ppermute | solution.py:263
  162.1 3.3 %collective-permute-start.58 = (f32[32,8,128]{2,1,0:T(8,128)S(1)}, f32[32,8,128]{2,1,0:T(8,128)S(1)}, u32[]{:S(2)}, u32[]{:S(2)}) collective-permute-start(f32[32,8,128]{2,1,0:T(8,128)S(1)} %get-tuple-element.144), channel_id=1, source_target_pairs={{0,12},{1,13},{2,14},{3,15},{4,8},{5,9},{6,10},{7,11},{8,4},{9,5},... | collective-permute-start | bytes 393224 | tf_op jit(solution)/shard_map/ppermute | solution.py:263
  165.4 2.5 %collective-permute-done.54.refs_20_ = f32[32,8,128]{2,1,0:T(8,128)S(1)} collective-permute-done((f32[32,8,128]{2,1,0:T(8,128)S(1)}, f32[32,8,128]{2,1,0:T(8,128)S(1)}, u32[]{:S(2)}, u32[]{:S(2)}) %collective-permute-start.54) | collective-permute-done | bytes 131104 | tf_op jit(solution)/shard_map/ppermute | solution.py:263
  169.0 2.2 %collective-permute-start.15 = (f32[32,8,128]{2,1,0:T(8,128)S(1)}, f32[32,8,128]{2,1,0:T(8,128)S(1)}, u32[]{:S(2)}, u32[]{:S(2)}) collective-permute-start(f32[32,8,128]{2,1,0:T(8,128)S(1)} %get-tuple-element.97), channel_id=1, source_target_pairs={{0,2},{1,3},{2,0},{3,1},{4,6},{5,7},{6,4},{7,5},{8,10},{9,11},{10,... | collective-permute-start | bytes 393224 | tf_op jit(solution)/shard_map/ppermute | solution.py:263
  171.2 3.6 %collective-permute-done.56.refs_22_ = f32[32,8,128]{2,1,0:T(8,128)S(1)} collective-permute-done((f32[32,8,128]{2,1,0:T(8,128)S(1)}, f32[32,8,128]{2,1,0:T(8,128)S(1)}, u32[]{:S(2)}, u32[]{:S(2)}) %collective-permute-start.56) | collective-permute-done | bytes 131104 | tf_op jit(solution)/shard_map/ppermute | solution.py:263
  174.8 1.9 collective-permute-done.57.refs_23_
  176.7 4.6 %collective-permute-start.18 = (f32[32,8,128]{2,1,0:T(8,128)S(1)}, f32[32,8,128]{2,1,0:T(8,128)S(1)}, u32[]{:S(2)}, u32[]{:S(2)}) collective-permute-start(f32[32,8,128]{2,1,0:T(8,128)S(1)} %get-tuple-element.100), channel_id=1, source_target_pairs={{0,14},{1,15},{2,12},{3,13},{4,10},{5,11},{6,8},{7,9},{8,6},{9,7},... | collective-permute-start | bytes 393224 | tf_op jit(solution)/shard_map/ppermute | solution.py:263
  182.2 2.7 %partial_sums.1.refs_5_ = f32[32,256,128]{2,1,0:T(8,128)S(1)} custom-call(f32[2,256]{1,0:T(2,128)S(1)} %get-tuple-element.76.kinetics, bf16[256,216]{1,0:T(8,128)(2,1)S(1)} %get-tuple-element.102.high, bf16[256,216]{1,0:T(8,128)(2,1)S(1)} %get-tuple-element.103.low, f32[32,8,128]{2,1,0:T(8,128)S(1)} %collective-permute-done.35.refs_0_, ...), custom_call_target="tpu_custom_call" | custom-call | flops 805306368 | bytes 6291456 | tf_op jit(solution)/shard_map/partial_sums/pallas_call | solution.py:303
  184.9 3.2 %collective-permute-done.16.refs_1_ = f32[32,8,128]{2,1,0:T(8,128)S(1)} collective-permute-done((f32[32,8,128]{2,1,0:T(8,128)S(1)}, f32[32,8,128]{2,1,0:T(8,128)S(1)}, u32[]{:S(2)}, u32[]{:S(2)}) %collective-permute-start.16) | collective-permute-done | bytes 131104 | tf_op jit(solution)/shard_map/ppermute | solution.py:263
  188.1 5.0 %collective-permute-done.18.refs_3_ = f32[32,8,128]{2,1,0:T(8,128)S(1)} collective-permute-done((f32[32,8,128]{2,1,0:T(8,128)S(1)}, f32[32,8,128]{2,1,0:T(8,128)S(1)}, u32[]{:S(2)}, u32[]{:S(2)}) %collective-permute-start.18) | collective-permute-done | bytes 131104 | tf_op jit(solution)/shard_map/ppermute | solution.py:263
  193.1 2.9 %collective-permute-done.19.refs_4_ = f32[32,8,128]{2,1,0:T(8,128)S(1)} collective-permute-done((f32[32,8,128]{2,1,0:T(8,128)S(1)}, f32[32,8,128]{2,1,0:T(8,128)S(1)}, u32[]{:S(2)}, u32[]{:S(2)}) %collective-permute-start.19) | collective-permute-done | bytes 131104 | tf_op jit(solution)/shard_map/ppermute | solution.py:263
  196.1 2.8 %last_sweep.1 = f32[256,32,128]{2,1,0:T(8,128)} custom-call(f32[2,256]{1,0:T(2,128)S(1)} %get-tuple-element.76.kinetics, bf16[256,40]{1,0:T(8,128)(2,1)S(1)} %get-tuple-element.77.high, bf16[256,40]{1,0:T(8,128)(2,1)S(1)} %get-tuple-element.78.low, f32[32,8,128]{2,1,0:T(8,128)S(1)} %collective-permute-done.15.refs_0_, ...), custom_call_target="tpu_custom_call" | custom-call | flops 805306368 | bytes 6291456 | tf_op jit(solution)/shard_map/last_sweep/pallas_call | solution.py:315
  (97 shorter events, 20.4 us)
Async XLA Ops:
  11.5 12.7 %collective-permute-start.24 = (f32[32,8,128]{2,1,0:T(8,128)}, f32[32,8,128]{2,1,0:T(8,128)S(1)}, u32[]{:S(2)}, u32[]{:S(2)}) collective-permute-start(f32[32,8,128]{2,1,0:T(8,128)} %get-tuple-element.108), channel_id=1, source_target_pairs={{0,10},{1,11},{2,8},{3,9},{4,14},{5,15},{6,12},{7,13},{8,2},{9,3},... | collective-permute-start | bytes 393224 | tf_op jit(solution)/shard_map/ppermute | solution.py:263
  12.6 14.5 %collective-permute-start.25 = (f32[32,8,128]{2,1,0:T(8,128)}, f32[32,8,128]{2,1,0:T(8,128)S(1)}, u32[]{:S(2)}, u32[]{:S(2)}) collective-permute-start(f32[32,8,128]{2,1,0:T(8,128)} %get-tuple-element.109), channel_id=1, source_target_pairs={{0,5},{1,4},{2,7},{3,6},{4,1},{5,0},{6,3},{7,2},{8,13},{9,12},{10,... | collective-permute-start | bytes 393224 | tf_op jit(solution)/shard_map/ppermute | solution.py:263
  17.4 13.7 %collective-permute-start.26 = (f32[32,8,128]{2,1,0:T(8,128)}, f32[32,8,128]{2,1,0:T(8,128)S(1)}, u32[]{:S(2)}, u32[]{:S(2)}) collective-permute-start(f32[32,8,128]{2,1,0:T(8,128)} %get-tuple-element.110), channel_id=1, source_target_pairs={{0,11},{1,10},{2,9},{3,8},{4,15},{5,14},{6,13},{7,12},{8,3},{9,2},... | collective-permute-start | bytes 393224 | tf_op jit(solution)/shard_map/ppermute | solution.py:263
  19.9 15.1 %collective-permute-start.27 = (f32[32,8,128]{2,1,0:T(8,128)}, f32[32,8,128]{2,1,0:T(8,128)S(1)}, u32[]{:S(2)}, u32[]{:S(2)}) collective-permute-start(f32[32,8,128]{2,1,0:T(8,128)} %get-tuple-element.111), channel_id=1, source_target_pairs={{0,4},{1,5},{2,6},{3,7},{4,0},{5,1},{6,2},{7,3},{8,12},{9,13},{10,... | collective-permute-start | bytes 393224 | tf_op jit(solution)/shard_map/ppermute | solution.py:263
  22.5 15.6 %collective-permute-start.28 = (f32[32,8,128]{2,1,0:T(8,128)}, f32[32,8,128]{2,1,0:T(8,128)S(1)}, u32[]{:S(2)}, u32[]{:S(2)}) collective-permute-start(f32[32,8,128]{2,1,0:T(8,128)} %get-tuple-element.112), channel_id=1, source_target_pairs={{0,12},{1,13},{2,14},{3,15},{4,8},{5,9},{6,10},{7,11},{8,4},{9,5},... | collective-permute-start | bytes 393224 | tf_op jit(solution)/shard_map/ppermute | solution.py:263
  24.2 14.0 %collective-permute-start.29 = (f32[32,8,128]{2,1,0:T(8,128)}, f32[32,8,128]{2,1,0:T(8,128)S(1)}, u32[]{:S(2)}, u32[]{:S(2)}) collective-permute-start(f32[32,8,128]{2,1,0:T(8,128)} %get-tuple-element.113), channel_id=1, source_target_pairs={{0,3},{1,2},{2,1},{3,0},{4,7},{5,6},{6,5},{7,4},{8,11},{9,10},{10,... | collective-permute-start | bytes 393224 | tf_op jit(solution)/shard_map/ppermute | solution.py:263
  27.1 24.9 %collective-permute-start.30 = (f32[32,8,128]{2,1,0:T(8,128)}, f32[32,8,128]{2,1,0:T(8,128)S(1)}, u32[]{:S(2)}, u32[]{:S(2)}) collective-permute-start(f32[32,8,128]{2,1,0:T(8,128)} %get-tuple-element.114), channel_id=1, source_target_pairs={{0,2},{1,3},{2,0},{3,1},{4,6},{5,7},{6,4},{7,5},{8,10},{9,11},{10,... | collective-permute-start | bytes 393224 | tf_op jit(solution)/shard_map/ppermute | solution.py:263
  31.1 20.9 %collective-permute-start.31 = (f32[32,8,128]{2,1,0:T(8,128)}, f32[32,8,128]{2,1,0:T(8,128)S(1)}, u32[]{:S(2)}, u32[]{:S(2)}) collective-permute-start(f32[32,8,128]{2,1,0:T(8,128)} %get-tuple-element.115), channel_id=1, source_target_pairs={{0,13},{1,12},{2,15},{3,14},{4,9},{5,8},{6,11},{7,10},{8,5},{9,4},... | collective-permute-start | bytes 393224 | tf_op jit(solution)/shard_map/ppermute | solution.py:263
  35.0 18.5 %collective-permute-start.32 = (f32[32,8,128]{2,1,0:T(8,128)}, f32[32,8,128]{2,1,0:T(8,128)S(1)}, u32[]{:S(2)}, u32[]{:S(2)}) collective-permute-start(f32[32,8,128]{2,1,0:T(8,128)} %get-tuple-element.116), channel_id=1, source_target_pairs={{0,1},{1,0},{2,3},{3,2},{4,5},{5,4},{6,7},{7,6},{8,9},{9,8},{10,11... | collective-permute-start | bytes 393224 | tf_op jit(solution)/shard_map/ppermute | solution.py:263
  38.1 18.2 %collective-permute-start.33 = (f32[32,8,128]{2,1,0:T(8,128)}, f32[32,8,128]{2,1,0:T(8,128)S(1)}, u32[]{:S(2)}, u32[]{:S(2)}) collective-permute-start(f32[32,8,128]{2,1,0:T(8,128)} %get-tuple-element.117), channel_id=1, source_target_pairs={{0,14},{1,15},{2,12},{3,13},{4,10},{5,11},{6,8},{7,9},{8,6},{9,7},... | collective-permute-start | bytes 393224 | tf_op jit(solution)/shard_map/ppermute | solution.py:263
  38.2 18.9 %collective-permute-start.34 = (f32[32,8,128]{2,1,0:T(8,128)}, f32[32,8,128]{2,1,0:T(8,128)S(1)}, u32[]{:S(2)}, u32[]{:S(2)}) collective-permute-start(f32[32,8,128]{2,1,0:T(8,128)} %get-tuple-element.118), channel_id=1, source_target_pairs={{0,15},{1,14},{2,13},{3,12},{4,11},{5,10},{6,9},{7,8},{8,7},{9,6},... | collective-permute-start | bytes 393224 | tf_op jit(solution)/shard_map/ppermute | solution.py:263
  52.0 13.3 %collective-permute-start = (f32[32,8,128]{2,1,0:T(8,128)S(1)}, f32[32,8,128]{2,1,0:T(8,128)S(1)}, u32[]{:S(2)}, u32[]{:S(2)}) collective-permute-start(f32[32,8,128]{2,1,0:T(8,128)S(1)} %get-tuple-element.81), channel_id=1, source_target_pairs={{0,8},{1,9},{2,10},{3,11},{4,12},{5,13},{6,14},{7,15},{8,0},{9,1},... | collective-permute-start | bytes 393224 | tf_op jit(solution)/shard_map/ppermute | solution.py:263
  52.1 15.6 %collective-permute-start.1 = (f32[32,8,128]{2,1,0:T(8,128)S(1)}, f32[32,8,128]{2,1,0:T(8,128)S(1)}, u32[]{:S(2)}, u32[]{:S(2)}) collective-permute-start(f32[32,8,128]{2,1,0:T(8,128)S(1)} %get-tuple-element.82), channel_id=1, source_target_pairs={{0,7},{1,6},{2,5},{3,4},{4,3},{5,2},{6,1},{7,0},{8,15},{9,14},{10,... | collective-permute-start | bytes 393224 | tf_op jit(solution)/shard_map/ppermute | solution.py:263
  53.5 14.4 %collective-permute-start.2 = (f32[32,8,128]{2,1,0:T(8,128)S(1)}, f32[32,8,128]{2,1,0:T(8,128)S(1)}, u32[]{:S(2)}, u32[]{:S(2)}) collective-permute-start(f32[32,8,128]{2,1,0:T(8,128)S(1)} %get-tuple-element.83), channel_id=1, source_target_pairs={{0,9},{1,8},{2,11},{3,10},{4,13},{5,12},{6,15},{7,14},{8,1},{9,0},... | collective-permute-start | bytes 393224 | tf_op jit(solution)/shard_map/ppermute | solution.py:263
  56.2 16.8 %collective-permute-start.3 = (f32[32,8,128]{2,1,0:T(8,128)S(1)}, f32[32,8,128]{2,1,0:T(8,128)S(1)}, u32[]{:S(2)}, u32[]{:S(2)}) collective-permute-start(f32[32,8,128]{2,1,0:T(8,128)S(1)} %get-tuple-element.84), channel_id=1, source_target_pairs={{0,6},{1,7},{2,4},{3,5},{4,2},{5,3},{6,0},{7,1},{8,14},{9,15},{10,... | collective-permute-start | bytes 393224 | tf_op jit(solution)/shard_map/ppermute | solution.py:263
  57.1 19.9 %collective-permute-start.4 = (f32[32,8,128]{2,1,0:T(8,128)S(1)}, f32[32,8,128]{2,1,0:T(8,128)S(1)}, u32[]{:S(2)}, u32[]{:S(2)}) collective-permute-start(f32[32,8,128]{2,1,0:T(8,128)S(1)} %get-tuple-element.85), channel_id=1, source_target_pairs={{0,10},{1,11},{2,8},{3,9},{4,14},{5,15},{6,12},{7,13},{8,2},{9,3},... | collective-permute-start | bytes 393224 | tf_op jit(solution)/shard_map/ppermute | solution.py:263
  65.3 14.1 %collective-permute-start.5 = (f32[32,8,128]{2,1,0:T(8,128)S(1)}, f32[32,8,128]{2,1,0:T(8,128)S(1)}, u32[]{:S(2)}, u32[]{:S(2)}) collective-permute-start(f32[32,8,128]{2,1,0:T(8,128)S(1)} %get-tuple-element.86), channel_id=1, source_target_pairs={{0,5},{1,4},{2,7},{3,6},{4,1},{5,0},{6,3},{7,2},{8,13},{9,12},{10,... | collective-permute-start | bytes 393224 | tf_op jit(solution)/shard_map/ppermute | solution.py:263
  67.7 12.0 %collective-permute-start.6 = (f32[32,8,128]{2,1,0:T(8,128)S(1)}, f32[32,8,128]{2,1,0:T(8,128)S(1)}, u32[]{:S(2)}, u32[]{:S(2)}) collective-permute-start(f32[32,8,128]{2,1,0:T(8,128)S(1)} %get-tuple-element.87), channel_id=1, source_target_pairs={{0,11},{1,10},{2,9},{3,8},{4,15},{5,14},{6,13},{7,12},{8,3},{9,2},... | collective-permute-start | bytes 393224 | tf_op jit(solution)/shard_map/ppermute | solution.py:263
  67.9 15.5 %collective-permute-start.7 = (f32[32,8,128]{2,1,0:T(8,128)S(1)}, f32[32,8,128]{2,1,0:T(8,128)S(1)}, u32[]{:S(2)}, u32[]{:S(2)}) collective-permute-start(f32[32,8,128]{2,1,0:T(8,128)S(1)} %get-tuple-element.88), channel_id=1, source_target_pairs={{0,4},{1,5},{2,6},{3,7},{4,0},{5,1},{6,2},{7,3},{8,12},{9,13},{10,... | collective-permute-start | bytes 393224 | tf_op jit(solution)/shard_map/ppermute | solution.py:263
  73.0 12.5 %collective-permute-start.8 = (f32[32,8,128]{2,1,0:T(8,128)S(1)}, f32[32,8,128]{2,1,0:T(8,128)S(1)}, u32[]{:S(2)}, u32[]{:S(2)}) collective-permute-start(f32[32,8,128]{2,1,0:T(8,128)S(1)} %get-tuple-element.89), channel_id=1, source_target_pairs={{0,12},{1,13},{2,14},{3,15},{4,8},{5,9},{6,10},{7,11},{8,4},{9,5},... | collective-permute-start | bytes 393224 | tf_op jit(solution)/shard_map/ppermute | solution.py:263
  79.4 16.7 %collective-permute-start.10 = (f32[32,8,128]{2,1,0:T(8,128)S(1)}, f32[32,8,128]{2,1,0:T(8,128)S(1)}, u32[]{:S(2)}, u32[]{:S(2)}) collective-permute-start(f32[32,8,128]{2,1,0:T(8,128)S(1)} %get-tuple-element.91), channel_id=1, source_target_pairs={{0,2},{1,3},{2,0},{3,1},{4,6},{5,7},{6,4},{7,5},{8,10},{9,11},{10,... | collective-permute-start | bytes 393224 | tf_op jit(solution)/shard_map/ppermute | solution.py:263
  79.7 22.3 %collective-permute-start.11 = (f32[32,8,128]{2,1,0:T(8,128)S(1)}, f32[32,8,128]{2,1,0:T(8,128)S(1)}, u32[]{:S(2)}, u32[]{:S(2)}) collective-permute-start(f32[32,8,128]{2,1,0:T(8,128)S(1)} %get-tuple-element.92), channel_id=1, source_target_pairs={{0,13},{1,12},{2,15},{3,14},{4,9},{5,8},{6,11},{7,10},{8,5},{9,4},... | collective-permute-start | bytes 393224 | tf_op jit(solution)/shard_map/ppermute | solution.py:263
  83.4 18.5 %collective-permute-start.12 = (f32[32,8,128]{2,1,0:T(8,128)S(1)}, f32[32,8,128]{2,1,0:T(8,128)S(1)}, u32[]{:S(2)}, u32[]{:S(2)}) collective-permute-start(f32[32,8,128]{2,1,0:T(8,128)S(1)} %get-tuple-element.93), channel_id=1, source_target_pairs={{0,1},{1,0},{2,3},{3,2},{4,5},{5,4},{6,7},{7,6},{8,9},{9,8},{10,11... | collective-permute-start | bytes 393224 | tf_op jit(solution)/shard_map/ppermute | solution.py:263
  85.5 16.8 %collective-permute-start.13 = (f32[32,8,128]{2,1,0:T(8,128)S(1)}, f32[32,8,128]{2,1,0:T(8,128)S(1)}, u32[]{:S(2)}, u32[]{:S(2)}) collective-permute-start(f32[32,8,128]{2,1,0:T(8,128)S(1)} %get-tuple-element.94), channel_id=1, source_target_pairs={{0,14},{1,15},{2,12},{3,13},{4,10},{5,11},{6,8},{7,9},{8,6},{9,7},... | collective-permute-start | bytes 393224 | tf_op jit(solution)/shard_map/ppermute | solution.py:263
  85.9 22.2 %collective-permute-start.14 = (f32[32,8,128]{2,1,0:T(8,128)S(1)}, f32[32,8,128]{2,1,0:T(8,128)S(1)}, u32[]{:S(2)}, u32[]{:S(2)}) collective-permute-start(f32[32,8,128]{2,1,0:T(8,128)S(1)} %get-tuple-element.95), channel_id=1, source_target_pairs={{0,15},{1,14},{2,13},{3,12},{4,11},{5,10},{6,9},{7,8},{8,7},{9,6},... | collective-permute-start | bytes 393224 | tf_op jit(solution)/shard_map/ppermute | solution.py:263
  96.1 14.9 %collective-permute-start.35 = (f32[32,8,128]{2,1,0:T(8,128)S(1)}, f32[32,8,128]{2,1,0:T(8,128)S(1)}, u32[]{:S(2)}, u32[]{:S(2)}) collective-permute-start(f32[32,8,128]{2,1,0:T(8,128)S(1)} %get-tuple-element.120), channel_id=1, source_target_pairs={{0,8},{1,9},{2,10},{3,11},{4,12},{5,13},{6,14},{7,15},{8,0},{9,1},... | collective-permute-start | bytes 393224 | tf_op jit(solution)/shard_map/ppermute | solution.py:263
  102.3 13.1 %collective-permute-start.38 = (f32[32,8,128]{2,1,0:T(8,128)S(1)}, f32[32,8,128]{2,1,0:T(8,128)S(1)}, u32[]{:S(2)}, u32[]{:S(2)}) collective-permute-start(f32[32,8,128]{2,1,0:T(8,128)S(1)} %get-tuple-element.123), channel_id=1, source_target_pairs={{0,6},{1,7},{2,4},{3,5},{4,2},{5,3},{6,0},{7,1},{8,14},{9,15},{10,... | collective-permute-start | bytes 393224 | tf_op jit(solution)/shard_map/ppermute | solution.py:263
  108.1 12.7 %collective-permute-start.39 = (f32[32,8,128]{2,1,0:T(8,128)S(1)}, f32[32,8,128]{2,1,0:T(8,128)S(1)}, u32[]{:S(2)}, u32[]{:S(2)}) collective-permute-start(f32[32,8,128]{2,1,0:T(8,128)S(1)} %get-tuple-element.124), channel_id=1, source_target_pairs={{0,10},{1,11},{2,8},{3,9},{4,14},{5,15},{6,12},{7,13},{8,2},{9,3},... | collective-permute-start | bytes 393224 | tf_op jit(solution)/shard_map/ppermute | solution.py:263
  113.3 12.1 %collective-permute-start.41 = (f32[32,8,128]{2,1,0:T(8,128)S(1)}, f32[32,8,128]{2,1,0:T(8,128)S(1)}, u32[]{:S(2)}, u32[]{:S(2)}) collective-permute-start(f32[32,8,128]{2,1,0:T(8,128)S(1)} %get-tuple-element.126), channel_id=1, source_target_pairs={{0,11},{1,10},{2,9},{3,8},{4,15},{5,14},{6,13},{7,12},{8,3},{9,2},... | collective-permute-start | bytes 393224 | tf_op jit(solution)/shard_map/ppermute | solution.py:263
  115.4 15.3 %collective-permute-start.43 = (f32[32,8,128]{2,1,0:T(8,128)S(1)}, f32[32,8,128]{2,1,0:T(8,128)S(1)}, u32[]{:S(2)}, u32[]{:S(2)}) collective-permute-start(f32[32,8,128]{2,1,0:T(8,128)S(1)} %get-tuple-element.128), channel_id=1, source_target_pairs={{0,12},{1,13},{2,14},{3,15},{4,8},{5,9},{6,10},{7,11},{8,4},{9,5},... | collective-permute-start | bytes 393224 | tf_op jit(solution)/shard_map/ppermute | solution.py:263
  120.8 23.8 %collective-permute-start.45 = (f32[32,8,128]{2,1,0:T(8,128)S(1)}, f32[32,8,128]{2,1,0:T(8,128)S(1)}, u32[]{:S(2)}, u32[]{:S(2)}) collective-permute-start(f32[32,8,128]{2,1,0:T(8,128)S(1)} %get-tuple-element.130), channel_id=1, source_target_pairs={{0,2},{1,3},{2,0},{3,1},{4,6},{5,7},{6,4},{7,5},{8,10},{9,11},{10,... | collective-permute-start | bytes 393224 | tf_op jit(solution)/shard_map/ppermute | solution.py:263
  125.4 20.0 %collective-permute-start.46 = (f32[32,8,128]{2,1,0:T(8,128)S(1)}, f32[32,8,128]{2,1,0:T(8,128)S(1)}, u32[]{:S(2)}, u32[]{:S(2)}) collective-permute-start(f32[32,8,128]{2,1,0:T(8,128)S(1)} %get-tuple-element.131), channel_id=1, source_target_pairs={{0,13},{1,12},{2,15},{3,14},{4,9},{5,8},{6,11},{7,10},{8,5},{9,4},... | collective-permute-start | bytes 393224 | tf_op jit(solution)/shard_map/ppermute | solution.py:263
  125.4 20.6 %collective-permute-start.47 = (f32[32,8,128]{2,1,0:T(8,128)S(1)}, f32[32,8,128]{2,1,0:T(8,128)S(1)}, u32[]{:S(2)}, u32[]{:S(2)}) collective-permute-start(f32[32,8,128]{2,1,0:T(8,128)S(1)} %get-tuple-element.132), channel_id=1, source_target_pairs={{0,1},{1,0},{2,3},{3,2},{4,5},{5,4},{6,7},{7,6},{8,9},{9,8},{10,11... | collective-permute-start | bytes 393224 | tf_op jit(solution)/shard_map/ppermute | solution.py:263
  130.7 17.8 %collective-permute-start.48 = (f32[32,8,128]{2,1,0:T(8,128)S(1)}, f32[32,8,128]{2,1,0:T(8,128)S(1)}, u32[]{:S(2)}, u32[]{:S(2)}) collective-permute-start(f32[32,8,128]{2,1,0:T(8,128)S(1)} %get-tuple-element.133), channel_id=1, source_target_pairs={{0,14},{1,15},{2,12},{3,13},{4,10},{5,11},{6,8},{7,9},{8,6},{9,7},... | collective-permute-start | bytes 393224 | tf_op jit(solution)/shard_map/ppermute | solution.py:263
  131.7 17.9 %collective-permute-start.49 = (f32[32,8,128]{2,1,0:T(8,128)S(1)}, f32[32,8,128]{2,1,0:T(8,128)S(1)}, u32[]{:S(2)}, u32[]{:S(2)}) collective-permute-start(f32[32,8,128]{2,1,0:T(8,128)S(1)} %get-tuple-element.134), channel_id=1, source_target_pairs={{0,15},{1,14},{2,13},{3,12},{4,11},{5,10},{6,9},{7,8},{8,7},{9,6},... | collective-permute-start | bytes 393224 | tf_op jit(solution)/shard_map/ppermute | solution.py:263
  144.5 12.7 %collective-permute-start.50 = (f32[32,8,128]{2,1,0:T(8,128)S(1)}, f32[32,8,128]{2,1,0:T(8,128)S(1)}, u32[]{:S(2)}, u32[]{:S(2)}) collective-permute-start(f32[32,8,128]{2,1,0:T(8,128)S(1)} %get-tuple-element.136), channel_id=1, source_target_pairs={{0,8},{1,9},{2,10},{3,11},{4,12},{5,13},{6,14},{7,15},{8,0},{9,1},... | collective-permute-start | bytes 393224 | tf_op jit(solution)/shard_map/ppermute | solution.py:263
  146.1 15.9 %collective-permute-start.52 = (f32[32,8,128]{2,1,0:T(8,128)S(1)}, f32[32,8,128]{2,1,0:T(8,128)S(1)}, u32[]{:S(2)}, u32[]{:S(2)}) collective-permute-start(f32[32,8,128]{2,1,0:T(8,128)S(1)} %get-tuple-element.138), channel_id=1, source_target_pairs={{0,9},{1,8},{2,11},{3,10},{4,13},{5,12},{6,15},{7,14},{8,1},{9,0},... | collective-permute-start | bytes 393224 | tf_op jit(solution)/shard_map/ppermute | solution.py:263
  148.5 13.6 %collective-permute-start.53 = (f32[32,8,128]{2,1,0:T(8,128)S(1)}, f32[32,8,128]{2,1,0:T(8,128)S(1)}, u32[]{:S(2)}, u32[]{:S(2)}) collective-permute-start(f32[32,8,128]{2,1,0:T(8,128)S(1)} %get-tuple-element.139), channel_id=1, source_target_pairs={{0,6},{1,7},{2,4},{3,5},{4,2},{5,3},{6,0},{7,1},{8,14},{9,15},{10,... | collective-permute-start | bytes 393224 | tf_op jit(solution)/shard_map/ppermute | solution.py:263
  149.6 18.2 %collective-permute-start.54 = (f32[32,8,128]{2,1,0:T(8,128)S(1)}, f32[32,8,128]{2,1,0:T(8,128)S(1)}, u32[]{:S(2)}, u32[]{:S(2)}) collective-permute-start(f32[32,8,128]{2,1,0:T(8,128)S(1)} %get-tuple-element.140), channel_id=1, source_target_pairs={{0,10},{1,11},{2,8},{3,9},{4,14},{5,15},{6,12},{7,13},{8,2},{9,3},... | collective-permute-start | bytes 393224 | tf_op jit(solution)/shard_map/ppermute | solution.py:263
  157.2 11.8 %collective-permute-start.55 = (f32[32,8,128]{2,1,0:T(8,128)S(1)}, f32[32,8,128]{2,1,0:T(8,128)S(1)}, u32[]{:S(2)}, u32[]{:S(2)}) collective-permute-start(f32[32,8,128]{2,1,0:T(8,128)S(1)} %get-tuple-element.141), channel_id=1, source_target_pairs={{0,5},{1,4},{2,7},{3,6},{4,1},{5,0},{6,3},{7,2},{8,13},{9,12},{10,... | collective-permute-start | bytes 393224 | tf_op jit(solution)/shard_map/ppermute | solution.py:263
  157.2 17.6 %collective-permute-start.56 = (f32[32,8,128]{2,1,0:T(8,128)S(1)}, f32[32,8,128]{2,1,0:T(8,128)S(1)}, u32[]{:S(2)}, u32[]{:S(2)}) collective-permute-start(f32[32,8,128]{2,1,0:T(8,128)S(1)} %get-tuple-element.142), channel_id=1, source_target_pairs={{0,11},{1,10},{2,9},{3,8},{4,15},{5,14},{6,13},{7,12},{8,3},{9,2},... | collective-permute-start | bytes 393224 | tf_op jit(solution)/shard_map/ppermute | solution.py:263
  162.0 14.7 %collective-permute-start.57 = (f32[32,8,128]{2,1,0:T(8,128)S(1)}, f32[32,8,128]{2,1,0:T(8,128)S(1)}, u32[]{:S(2)}, u32[]{:S(2)}) collective-permute-start(f32[32,8,128]{2,1,0:T(8,128)S(1)} %get-tuple-element.143), channel_id=1, source_target_pairs={{0,4},{1,5},{2,6},{3,7},{4,0},{5,1},{6,2},{7,3},{8,12},{9,13},{10,... | collective-permute-start | bytes 393224 | tf_op jit(solution)/shard_map/ppermute | solution.py:263
  162.1 14.7 %collective-permute-start.58 = (f32[32,8,128]{2,1,0:T(8,128)S(1)}, f32[32,8,128]{2,1,0:T(8,128)S(1)}, u32[]{:S(2)}, u32[]{:S(2)}) collective-permute-start(f32[32,8,128]{2,1,0:T(8,128)S(1)} %get-tuple-element.144), channel_id=1, source_target_pairs={{0,12},{1,13},{2,14},{3,15},{4,8},{5,9},{6,10},{7,11},{8,4},{9,5},... | collective-permute-start | bytes 393224 | tf_op jit(solution)/shard_map/ppermute | solution.py:263
  167.9 13.4 %collective-permute-start.59 = (f32[32,8,128]{2,1,0:T(8,128)S(1)}, f32[32,8,128]{2,1,0:T(8,128)S(1)}, u32[]{:S(2)}, u32[]{:S(2)}) collective-permute-start(f32[32,8,128]{2,1,0:T(8,128)S(1)} %get-tuple-element.145), channel_id=1, source_target_pairs={{0,3},{1,2},{2,1},{3,0},{4,7},{5,6},{6,5},{7,4},{8,11},{9,10},{10,... | collective-permute-start | bytes 393224 | tf_op jit(solution)/shard_map/ppermute | solution.py:263
  169.0 15.9 %collective-permute-start.15 = (f32[32,8,128]{2,1,0:T(8,128)S(1)}, f32[32,8,128]{2,1,0:T(8,128)S(1)}, u32[]{:S(2)}, u32[]{:S(2)}) collective-permute-start(f32[32,8,128]{2,1,0:T(8,128)S(1)} %get-tuple-element.97), channel_id=1, source_target_pairs={{0,2},{1,3},{2,0},{3,1},{4,6},{5,7},{6,4},{7,5},{8,10},{9,11},{10,... | collective-permute-start | bytes 393224 | tf_op jit(solution)/shard_map/ppermute | solution.py:263
  174.8 13.3 %collective-permute-start.16 = (f32[32,8,128]{2,1,0:T(8,128)S(1)}, f32[32,8,128]{2,1,0:T(8,128)S(1)}, u32[]{:S(2)}, u32[]{:S(2)}) collective-permute-start(f32[32,8,128]{2,1,0:T(8,128)S(1)} %get-tuple-element.98), channel_id=1, source_target_pairs={{0,13},{1,12},{2,15},{3,14},{4,9},{5,8},{6,11},{7,10},{8,5},{9,4},... | collective-permute-start | bytes 393224 | tf_op jit(solution)/shard_map/ppermute | solution.py:263
  176.7 16.4 %collective-permute-start.18 = (f32[32,8,128]{2,1,0:T(8,128)S(1)}, f32[32,8,128]{2,1,0:T(8,128)S(1)}, u32[]{:S(2)}, u32[]{:S(2)}) collective-permute-start(f32[32,8,128]{2,1,0:T(8,128)S(1)} %get-tuple-element.100), channel_id=1, source_target_pairs={{0,14},{1,15},{2,12},{3,13},{4,10},{5,11},{6,8},{7,9},{8,6},{9,7},... | collective-permute-start | bytes 393224 | tf_op jit(solution)/shard_map/ppermute | solution.py:263
  181.3 14.8 %collective-permute-start.19 = (f32[32,8,128]{2,1,0:T(8,128)S(1)}, f32[32,8,128]{2,1,0:T(8,128)S(1)}, u32[]{:S(2)}, u32[]{:S(2)}) collective-permute-start(f32[32,8,128]{2,1,0:T(8,128)S(1)} %get-tuple-element.101), channel_id=1, source_target_pairs={{0,15},{1,14},{2,13},{3,12},{4,11},{5,10},{6,9},{7,8},{8,7},{9,6},... | collective-permute-start | bytes 393224 | tf_op jit(solution)/shard_map/ppermute | solution.py:263
  (21 other events, 538.0 us)

commit v3 on v2

--- a/solution.py
+++ b/solution.py
@@ -62,7 +62,7 @@
     half = ranks // 2
     order = []
     for index in range(half):
-        order.append(half + index)
+        order.append(half + (index ^ (index >> 1) if 2 * index < half else 3 * half // 2 - 1 - index))
         order += [half - 1 - near for near in range(half - 1) if near - near // 5 == index]
     return order + [0]
 
@@ -280,7 +280,7 @@
                 pltpu.SemaphoreType.DMA((depth + 2 + len(scalar_arrays),)),
                 *[pltpu.SMEM(array.shape, array.dtype) for array in scalar_arrays],
             ],
-            compiler_params=PARAMS if chunk else pltpu.CompilerParams(vmem_limit_bytes=FIRST_LIMIT),
+            compiler_params=pltpu.CompilerParams(vmem_limit_bytes=FIRST_LIMIT),
             cost_estimate=cost(size // CHUNKS, lines, 1, 4 * (size + size // CHUNKS)),
             name=f"first_sweep_{chunk}",
         )(*scalar_arrays, explicit_line, inverse_line, concentration)

time: 199 us -> 193 us (0.970)
  starting transfers between devices: 118 us -> 93.6 us
  waiting for transfers between devices: 42.4 us -> 65.6 us
  Pallas kernels: 35.3 us -> 33 us
  local copies, waits for them, and re-layouts: 2.21 us -> 0.05 us
    ppermute x60, starting transfers between devices: 118 us -> 93.6 us  [exchange(): lax.ppermute(block, ('row', 'col'), [(i, i ^ place) for i in range(ranks)])]
    ppermute x60, waiting for transfers between devices: 42.4 us -> 65.6 us  [exchange(): lax.ppermute(block, ('row', 'col'), [(i, i ^ place) for i in range(ranks)])]
    pallas_call x2, Pallas kernels: 12.7 us -> 10.4 us  [first(): pl.pallas_call(functools.partial(first_sweep, chunk, columns), grid=(1,),...]
    unnamed x18, local copies, waits for them, and re-layouts: 2.21 us -> 0.05 us
  transfers between devices with their start and end apart: 60 -> 60, of which waited for: 19 -> 25; matrix products, arithmetic and copies ran while one was open for 0% -> 0% of each run, Pallas kernels for 14% -> 13%
where the time goes in v3:
time: 193 us
  starting transfers between devices  93.6 us (48%)
  waiting for transfers between devices  65.6 us (34%)
  Pallas kernels  33 us (17%)
    ppermute x60, starting transfers between devices, exchange(): lax.ppermute(block, ('row', 'col'), [(i, i ^ place) for i in range(ranks)])  93.6 us
    ppermute x60, waiting for transfers between devices, exchange(): lax.ppermute(block, ('row', 'col'), [(i, i ^ place) for i in range(ranks)])  65.6 us
    pallas_call x2, Pallas kernels, planes(): pl.pallas_call(functools.partial(plane_sweeps, columns, ranks), grid=(1,)...  14.7 us
    pallas_call x2, Pallas kernels, first(): pl.pallas_call(functools.partial(first_sweep, chunk, columns), grid=(1,),...  10.4 us
  transfers between devices with their start and end apart: 60, of which 25 were waited for; matrix products, arithmetic and copies ran while one was open for 0% of the time, Pallas kernels for 13%

profile of v3, /device:TPU:17, one launch (start us, length us, event | category | flops | bytes accessed | tf_op | source)
XLA Modules:
  0.0 193.3 jit_solution(3751407726990803193)
XLA Ops:
  0.7 5.3 %first_sweep_0.1 = (f32[32,8,128]{2,1,0:T(8,128)}, f32[32,8,128]{2,1,0:T(8,128)}, f32[32,8,128]{2,1,0:T(8,128)}, f32[32,8,128]{2,1,0:T(8,128)}, f32[32,8,128]{2,...) custom-call(s32[1]{0:T(128)S(6)} %copy.10.species, ...), custom_call_target="tpu_custom_call" | custom-call | flops 805306368 | bytes 6291456 | tf_op jit(solution)/shard_map/first_sweep_0/pallas_call | solution.py:271
  6.1 3.1 %collective-permute-start.21 = (f32[32,8,128]{2,1,0:T(8,128)}, f32[32,8,128]{2,1,0:T(8,128)S(1)}, u32[]{:S(2)}, u32[]{:S(2)}) collective-permute-start(f32[32,8,128]{2,1,0:T(8,128)} %get-tuple-element.105), channel_id=1, source_target_pairs={{0,7},{1,6},{2,5},{3,4},{4,3},{5,2},{6,1},{7,0},{8,15},{9,14},{10,... | collective-permute-start | bytes 393224 | tf_op jit(solution)/shard_map/ppermute | solution.py:263
  13.2 4.2 %collective-permute-start.25 = (f32[32,8,128]{2,1,0:T(8,128)}, f32[32,8,128]{2,1,0:T(8,128)S(1)}, u32[]{:S(2)}, u32[]{:S(2)}) collective-permute-start(f32[32,8,128]{2,1,0:T(8,128)} %get-tuple-element.109), channel_id=1, source_target_pairs={{0,5},{1,4},{2,7},{3,6},{4,1},{5,0},{6,3},{7,2},{8,13},{9,12},{10,... | collective-permute-start | bytes 393224 | tf_op jit(solution)/shard_map/ppermute | solution.py:263
  17.4 1.8 collective-permute-start.26
  19.3 3.3 %collective-permute-start.27 = (f32[32,8,128]{2,1,0:T(8,128)}, f32[32,8,128]{2,1,0:T(8,128)S(1)}, u32[]{:S(2)}, u32[]{:S(2)}) collective-permute-start(f32[32,8,128]{2,1,0:T(8,128)} %get-tuple-element.111), channel_id=1, source_target_pairs={{0,4},{1,5},{2,6},{3,7},{4,0},{5,1},{6,2},{7,3},{8,12},{9,13},{10,... | collective-permute-start | bytes 393224 | tf_op jit(solution)/shard_map/ppermute | solution.py:263
  22.8 2.6 %collective-permute-done.24.refs_4_ = f32[32,8,128]{2,1,0:T(8,128)S(1)} collective-permute-done((f32[32,8,128]{2,1,0:T(8,128)}, f32[32,8,128]{2,1,0:T(8,128)S(1)}, u32[]{:S(2)}, u32[]{:S(2)}) %collective-permute-start.24) | collective-permute-done | bytes 131104 | tf_op jit(solution)/shard_map/ppermute | solution.py:263
  28.1 1.8 collective-permute-done.26.refs_6_
  29.9 2.7 %collective-permute-start.31 = (f32[32,8,128]{2,1,0:T(8,128)}, f32[32,8,128]{2,1,0:T(8,128)S(1)}, u32[]{:S(2)}, u32[]{:S(2)}) collective-permute-start(f32[32,8,128]{2,1,0:T(8,128)} %get-tuple-element.115), channel_id=1, source_target_pairs={{0,14},{1,15},{2,12},{3,13},{4,10},{5,11},{6,8},{7,9},{8,6},{9,7},... | collective-permute-start | bytes 393224 | tf_op jit(solution)/shard_map/ppermute | solution.py:263
  32.7 2.4 %collective-permute-done.27.refs_7_ = f32[32,8,128]{2,1,0:T(8,128)S(1)} collective-permute-done((f32[32,8,128]{2,1,0:T(8,128)}, f32[32,8,128]{2,1,0:T(8,128)S(1)}, u32[]{:S(2)}, u32[]{:S(2)}) %collective-permute-start.27) | collective-permute-done | bytes 131104 | tf_op jit(solution)/shard_map/ppermute | solution.py:263
  35.1 3.8 %collective-permute-done.28.refs_8_ = f32[32,8,128]{2,1,0:T(8,128)S(1)} collective-permute-done((f32[32,8,128]{2,1,0:T(8,128)}, f32[32,8,128]{2,1,0:T(8,128)S(1)}, u32[]{:S(2)}, u32[]{:S(2)}) %collective-permute-start.28) | collective-permute-done | bytes 131104 | tf_op jit(solution)/shard_map/ppermute | solution.py:263
  38.9 1.8 collective-permute-start.34
  40.7 5.1 %first_sweep_1.1 = (f32[32,8,128]{2,1,0:T(8,128)}, f32[32,8,128]{2,1,0:T(8,128)}, f32[32,8,128]{2,1,0:T(8,128)}, f32[32,8,128]{2,1,0:T(8,128)}, f32[32,8,128]{2,...) custom-call(s32[1]{0:T(128)S(6)} %copy.10.species, ...), custom_call_target="tpu_custom_call" | custom-call | flops 805306368 | bytes 6291456 | tf_op jit(solution)/shard_map/first_sweep_1/pallas_call | solution.py:271
  45.8 3.0 %collective-permute-start = (f32[32,8,128]{2,1,0:T(8,128)}, f32[32,8,128]{2,1,0:T(8,128)S(1)}, u32[]{:S(2)}, u32[]{:S(2)}) collective-permute-start(f32[32,8,128]{2,1,0:T(8,128)} %get-tuple-element.81), channel_id=1, source_target_pairs={{0,8},{1,9},{2,10},{3,11},{4,12},{5,13},{6,14},{7,15},{8,0},{9,1},... | collective-permute-start | bytes 393224 | tf_op jit(solution)/shard_map/ppermute | solution.py:263
  51.0 4.2 %collective-permute-done.33.refs_13_ = f32[32,8,128]{2,1,0:T(8,128)S(1)} collective-permute-done((f32[32,8,128]{2,1,0:T(8,128)}, f32[32,8,128]{2,1,0:T(8,128)S(1)}, u32[]{:S(2)}, u32[]{:S(2)}) %collective-permute-start.33) | collective-permute-done | bytes 131104 | tf_op jit(solution)/shard_map/ppermute | solution.py:263
  55.1 5.4 %collective-permute-done.34.refs_14_ = f32[32,8,128]{2,1,0:T(8,128)S(1)} collective-permute-done((f32[32,8,128]{2,1,0:T(8,128)}, f32[32,8,128]{2,1,0:T(8,128)S(1)}, u32[]{:S(2)}, u32[]{:S(2)}) %collective-permute-start.34) | collective-permute-done | bytes 131104 | tf_op jit(solution)/shard_map/ppermute | solution.py:263
  60.6 4.5 %collective-permute-start.5 = (f32[32,8,128]{2,1,0:T(8,128)}, f32[32,8,128]{2,1,0:T(8,128)S(1)}, u32[]{:S(2)}, u32[]{:S(2)}) collective-permute-start(f32[32,8,128]{2,1,0:T(8,128)} %get-tuple-element.86), channel_id=1, source_target_pairs={{0,5},{1,4},{2,7},{3,6},{4,1},{5,0},{6,3},{7,2},{8,13},{9,12},{10,... | collective-permute-start | bytes 393224 | tf_op jit(solution)/shard_map/ppermute | solution.py:263
  65.2 5.0 %collective-permute-start.7 = (f32[32,8,128]{2,1,0:T(8,128)}, f32[32,8,128]{2,1,0:T(8,128)S(1)}, u32[]{:S(2)}, u32[]{:S(2)}) collective-permute-start(f32[32,8,128]{2,1,0:T(8,128)} %get-tuple-element.88), channel_id=1, source_target_pairs={{0,4},{1,5},{2,6},{3,7},{4,0},{5,1},{6,2},{7,3},{8,12},{9,13},{10,... | collective-permute-start | bytes 393224 | tf_op jit(solution)/shard_map/ppermute | solution.py:263
  70.2 3.9 %collective-permute-start.9 = (f32[32,8,128]{2,1,0:T(8,128)}, f32[32,8,128]{2,1,0:T(8,128)S(1)}, u32[]{:S(2)}, u32[]{:S(2)}) collective-permute-start(f32[32,8,128]{2,1,0:T(8,128)} %get-tuple-element.90), channel_id=1, source_target_pairs={{0,3},{1,2},{2,1},{3,0},{4,7},{5,6},{6,5},{7,4},{8,11},{9,10},{10,... | collective-permute-start | bytes 393224 | tf_op jit(solution)/shard_map/ppermute | solution.py:263
  74.2 2.3 %prepare.1 = (f32[2,256]{1,0:T(2,128)S(1)}, bf16[4,256,256]{2,1,0:T(8,128)(2,1)S(1)}, bf16[4,256,256]{2,1,0:T(8,128)(2,1)S(1)}, bf16[256,216]{1,0:T(8,128)(2,1)S...) custom-call(s32[1]{0:T(128)S(6)} %copy.10.species, f32[64]{0:T(128)S(1)} %copy-done.3, ...), custom_call_target="tpu_custom_call" | custom-call | flops 805306368 | bytes 2097152 | tf_op jit(solution)/shard_map/prepare/pallas_call | solution.py:337
  77.0 3.5 %collective-permute-start.11 = (f32[32,8,128]{2,1,0:T(8,128)}, f32[32,8,128]{2,1,0:T(8,128)S(1)}, u32[]{:S(2)}, u32[]{:S(2)}) collective-permute-start(f32[32,8,128]{2,1,0:T(8,128)} %get-tuple-element.92), channel_id=1, source_target_pairs={{0,14},{1,15},{2,12},{3,13},{4,10},{5,11},{6,8},{7,9},{8,6},{9,7},... | collective-permute-start | bytes 393224 | tf_op jit(solution)/shard_map/ppermute | solution.py:263
  81.3 2.6 %collective-permute-done.8.refs_8_ = f32[32,8,128]{2,1,0:T(8,128)S(1)} collective-permute-done((f32[32,8,128]{2,1,0:T(8,128)}, f32[32,8,128]{2,1,0:T(8,128)S(1)}, u32[]{:S(2)}, u32[]{:S(2)}) %collective-permute-start.8) | collective-permute-done | bytes 131104 | tf_op jit(solution)/shard_map/ppermute | solution.py:263
  84.0 1.8 collective-permute-start.14
  85.8 7.5 %plane_sweeps_0.1 = (f32[32,8,128]{2,1,0:T(8,128)S(1)}, f32[32,8,128]{2,1,0:T(8,128)S(1)}, f32[32,8,128]{2,1,0:T(8,128)S(1)}, f32[32,8,128]{2,1,0:T(8,128)S(1)},...) custom-call(f32[2,256]{1,0:T(2,128)S(1)} %get-tuple-element.76.kinet, ...), custom_call_target="tpu_custom_call" | custom-call | flops 3221225472 | bytes 4194304 | tf_op jit(solution)/shard_map/plane_sweeps_0/pallas_call | solution.py:289
  93.2 2.9 %collective-permute-start.35 = (f32[32,8,128]{2,1,0:T(8,128)S(1)}, f32[32,8,128]{2,1,0:T(8,128)S(1)}, u32[]{:S(2)}, u32[]{:S(2)}) collective-permute-start(f32[32,8,128]{2,1,0:T(8,128)S(1)} %get-tuple-element.120), channel_id=1, source_target_pairs={{0,8},{1,9},{2,10},{3,11},{4,12},{5,13},{6,14},{7,15},{8,0},{9,1},... | collective-permute-start | bytes 393224 | tf_op jit(solution)/shard_map/ppermute | solution.py:263
  96.4 2.0 %collective-permute-start.37 = (f32[32,8,128]{2,1,0:T(8,128)S(1)}, f32[32,8,128]{2,1,0:T(8,128)S(1)}, u32[]{:S(2)}, u32[]{:S(2)}) collective-permute-start(f32[32,8,128]{2,1,0:T(8,128)S(1)} %get-tuple-element.122), channel_id=1, source_target_pairs={{0,9},{1,8},{2,11},{3,10},{4,13},{5,12},{6,15},{7,14},{8,1},{9,0},... | collective-permute-start | bytes 393224 | tf_op jit(solution)/shard_map/ppermute | solution.py:263
  99.5 3.4 %collective-permute-done.14.refs_14_ = f32[32,8,128]{2,1,0:T(8,128)S(1)} collective-permute-done((f32[32,8,128]{2,1,0:T(8,128)}, f32[32,8,128]{2,1,0:T(8,128)S(1)}, u32[]{:S(2)}, u32[]{:S(2)}) %collective-permute-start.14) | collective-permute-done | bytes 131104 | tf_op jit(solution)/shard_map/ppermute | solution.py:263
  103.2 2.5 %collective-permute-done.35.refs_0_ = f32[32,8,128]{2,1,0:T(8,128)S(1)} collective-permute-done((f32[32,8,128]{2,1,0:T(8,128)S(1)}, f32[32,8,128]{2,1,0:T(8,128)S(1)}, u32[]{:S(2)}, u32[]{:S(2)}) %collective-permute-start.35) | collective-permute-done | bytes 131104 | tf_op jit(solution)/shard_map/ppermute | solution.py:263
  105.7 4.3 %collective-permute-start.40 = (f32[32,8,128]{2,1,0:T(8,128)S(1)}, f32[32,8,128]{2,1,0:T(8,128)S(1)}, u32[]{:S(2)}, u32[]{:S(2)}) collective-permute-start(f32[32,8,128]{2,1,0:T(8,128)S(1)} %get-tuple-element.125), channel_id=1, source_target_pairs={{0,5},{1,4},{2,7},{3,6},{4,1},{5,0},{6,3},{7,2},{8,13},{9,12},{10,... | collective-permute-start | bytes 393224 | tf_op jit(solution)/shard_map/ppermute | solution.py:263
  111.4 3.9 %collective-permute-start.42 = (f32[32,8,128]{2,1,0:T(8,128)S(1)}, f32[32,8,128]{2,1,0:T(8,128)S(1)}, u32[]{:S(2)}, u32[]{:S(2)}) collective-permute-start(f32[32,8,128]{2,1,0:T(8,128)S(1)} %get-tuple-element.127), channel_id=1, source_target_pairs={{0,4},{1,5},{2,6},{3,7},{4,0},{5,1},{6,2},{7,3},{8,12},{9,13},{10,... | collective-permute-start | bytes 393224 | tf_op jit(solution)/shard_map/ppermute | solution.py:263
  120.3 2.5 %collective-permute-done.41.refs_6_ = f32[32,8,128]{2,1,0:T(8,128)S(1)} collective-permute-done((f32[32,8,128]{2,1,0:T(8,128)S(1)}, f32[32,8,128]{2,1,0:T(8,128)S(1)}, u32[]{:S(2)}, u32[]{:S(2)}) %collective-permute-start.41) | collective-permute-done | bytes 131104 | tf_op jit(solution)/shard_map/ppermute | solution.py:263
  122.8 2.8 %collective-permute-start.46 = (f32[32,8,128]{2,1,0:T(8,128)S(1)}, f32[32,8,128]{2,1,0:T(8,128)S(1)}, u32[]{:S(2)}, u32[]{:S(2)}) collective-permute-start(f32[32,8,128]{2,1,0:T(8,128)S(1)} %get-tuple-element.131), channel_id=1, source_target_pairs={{0,14},{1,15},{2,12},{3,13},{4,10},{5,11},{6,8},{7,9},{8,6},{9,7},... | collective-permute-start | bytes 393224 | tf_op jit(solution)/shard_map/ppermute | solution.py:263
  129.1 1.8 collective-permute-start.49
  130.9 7.3 %plane_sweeps_1.1 = (f32[32,8,128]{2,1,0:T(8,128)S(1)}, f32[32,8,128]{2,1,0:T(8,128)S(1)}, f32[32,8,128]{2,1,0:T(8,128)S(1)}, f32[32,8,128]{2,1,0:T(8,128)S(1)},...) custom-call(f32[2,256]{1,0:T(2,128)S(1)} %get-tuple-element.76.kinet, ...), custom_call_target="tpu_custom_call" | custom-call | flops 3221225472 | bytes 4194304 | tf_op jit(solution)/shard_map/plane_sweeps_1/pallas_call | solution.py:289
  138.2 2.9 %collective-permute-start.50 = (f32[32,8,128]{2,1,0:T(8,128)S(1)}, f32[32,8,128]{2,1,0:T(8,128)S(1)}, u32[]{:S(2)}, u32[]{:S(2)}) collective-permute-start(f32[32,8,128]{2,1,0:T(8,128)S(1)} %get-tuple-element.136), channel_id=1, source_target_pairs={{0,8},{1,9},{2,10},{3,11},{4,12},{5,13},{6,14},{7,15},{8,0},{9,1},... | collective-permute-start | bytes 393224 | tf_op jit(solution)/shard_map/ppermute | solution.py:263
  141.7 1.9 collective-permute-start.52
  144.4 4.1 %collective-permute-done.49.refs_14_ = f32[32,8,128]{2,1,0:T(8,128)S(1)} collective-permute-done((f32[32,8,128]{2,1,0:T(8,128)S(1)}, f32[32,8,128]{2,1,0:T(8,128)S(1)}, u32[]{:S(2)}, u32[]{:S(2)}) %collective-permute-start.49) | collective-permute-done | bytes 131104 | tf_op jit(solution)/shard_map/ppermute | solution.py:263
  148.5 2.6 %collective-permute-done.50.refs_16_ = f32[32,8,128]{2,1,0:T(8,128)S(1)} collective-permute-done((f32[32,8,128]{2,1,0:T(8,128)S(1)}, f32[32,8,128]{2,1,0:T(8,128)S(1)}, u32[]{:S(2)}, u32[]{:S(2)}) %collective-permute-start.50) | collective-permute-done | bytes 131104 | tf_op jit(solution)/shard_map/ppermute | solution.py:263
  151.1 4.4 %collective-permute-start.55 = (f32[32,8,128]{2,1,0:T(8,128)S(1)}, f32[32,8,128]{2,1,0:T(8,128)S(1)}, u32[]{:S(2)}, u32[]{:S(2)}) collective-permute-start(f32[32,8,128]{2,1,0:T(8,128)S(1)} %get-tuple-element.141), channel_id=1, source_target_pairs={{0,5},{1,4},{2,7},{3,6},{4,1},{5,0},{6,3},{7,2},{8,13},{9,12},{10,... | collective-permute-start | bytes 393224 | tf_op jit(solution)/shard_map/ppermute | solution.py:263
  156.8 3.7 %collective-permute-start.57 = (f32[32,8,128]{2,1,0:T(8,128)S(1)}, f32[32,8,128]{2,1,0:T(8,128)S(1)}, u32[]{:S(2)}, u32[]{:S(2)}) collective-permute-start(f32[32,8,128]{2,1,0:T(8,128)S(1)} %get-tuple-element.143), channel_id=1, source_target_pairs={{0,4},{1,5},{2,6},{3,7},{4,0},{5,1},{6,2},{7,3},{8,12},{9,13},{10,... | collective-permute-start | bytes 393224 | tf_op jit(solution)/shard_map/ppermute | solution.py:263
  160.6 1.8 collective-permute-done.54.refs_20_
  165.2 2.8 %collective-permute-done.56.refs_22_ = f32[32,8,128]{2,1,0:T(8,128)S(1)} collective-permute-done((f32[32,8,128]{2,1,0:T(8,128)S(1)}, f32[32,8,128]{2,1,0:T(8,128)S(1)}, u32[]{:S(2)}, u32[]{:S(2)}) %collective-permute-start.56) | collective-permute-done | bytes 131104 | tf_op jit(solution)/shard_map/ppermute | solution.py:263
  168.0 2.5 %collective-permute-start.16 = (f32[32,8,128]{2,1,0:T(8,128)S(1)}, f32[32,8,128]{2,1,0:T(8,128)S(1)}, u32[]{:S(2)}, u32[]{:S(2)}) collective-permute-start(f32[32,8,128]{2,1,0:T(8,128)S(1)} %get-tuple-element.98), channel_id=1, source_target_pairs={{0,14},{1,15},{2,12},{3,13},{4,10},{5,11},{6,8},{7,9},{8,6},{9,7},... | collective-permute-start | bytes 393224 | tf_op jit(solution)/shard_map/ppermute | solution.py:263
  174.1 1.8 collective-permute-start.19
  175.9 2.7 %partial_sums.1.refs_5_ = f32[32,256,128]{2,1,0:T(8,128)S(1)} custom-call(f32[2,256]{1,0:T(2,128)S(1)} %get-tuple-element.76.kinetics, bf16[256,216]{1,0:T(8,128)(2,1)S(1)} %get-tuple-element.102.high, bf16[256,216]{1,0:T(8,128)(2,1)S(1)} %get-tuple-element.103.low, f32[32,8,128]{2,1,0:T(8,128)S(1)} %collective-permute-done.35.refs_0_, ...), custom_call_target="tpu_custom_call" | custom-call | flops 805306368 | bytes 6291456 | tf_op jit(solution)/shard_map/partial_sums/pallas_call | solution.py:303
  178.6 6.8 %collective-permute-done.16.refs_1_ = f32[32,8,128]{2,1,0:T(8,128)S(1)} collective-permute-done((f32[32,8,128]{2,1,0:T(8,128)S(1)}, f32[32,8,128]{2,1,0:T(8,128)S(1)}, u32[]{:S(2)}, u32[]{:S(2)}) %collective-permute-start.16) | collective-permute-done | bytes 131104 | tf_op jit(solution)/shard_map/ppermute | solution.py:263
  185.3 2.1 %collective-permute-done.18.refs_3_ = f32[32,8,128]{2,1,0:T(8,128)S(1)} collective-permute-done((f32[32,8,128]{2,1,0:T(8,128)S(1)}, f32[32,8,128]{2,1,0:T(8,128)S(1)}, u32[]{:S(2)}, u32[]{:S(2)}) %collective-permute-start.18) | collective-permute-done | bytes 131104 | tf_op jit(solution)/shard_map/ppermute | solution.py:263
  187.5 2.8 %collective-permute-done.19.refs_4_ = f32[32,8,128]{2,1,0:T(8,128)S(1)} collective-permute-done((f32[32,8,128]{2,1,0:T(8,128)S(1)}, f32[32,8,128]{2,1,0:T(8,128)S(1)}, u32[]{:S(2)}, u32[]{:S(2)}) %collective-permute-start.19) | collective-permute-done | bytes 131104 | tf_op jit(solution)/shard_map/ppermute | solution.py:263
  190.3 2.8 %last_sweep.1 = f32[256,32,128]{2,1,0:T(8,128)} custom-call(f32[2,256]{1,0:T(2,128)S(1)} %get-tuple-element.76.kinetics, bf16[256,40]{1,0:T(8,128)(2,1)S(1)} %get-tuple-element.77.high, bf16[256,40]{1,0:T(8,128)(2,1)S(1)} %get-tuple-element.78.low, f32[32,8,128]{2,1,0:T(8,128)S(1)} %collective-permute-done.15.refs_0_, ...), custom_call_target="tpu_custom_call" | custom-call | flops 805306368 | bytes 6291456 | tf_op jit(solution)/shard_map/last_sweep/pallas_call | solution.py:315
  (97 shorter events, 31.4 us)
Async XLA Ops:
  11.5 13.9 %collective-permute-start.24 = (f32[32,8,128]{2,1,0:T(8,128)}, f32[32,8,128]{2,1,0:T(8,128)S(1)}, u32[]{:S(2)}, u32[]{:S(2)}) collective-permute-start(f32[32,8,128]{2,1,0:T(8,128)} %get-tuple-element.108), channel_id=1, source_target_pairs={{0,11},{1,10},{2,9},{3,8},{4,15},{5,14},{6,13},{7,12},{8,3},{9,2},... | collective-permute-start | bytes 393224 | tf_op jit(solution)/shard_map/ppermute | solution.py:263
  13.2 13.9 %collective-permute-start.25 = (f32[32,8,128]{2,1,0:T(8,128)}, f32[32,8,128]{2,1,0:T(8,128)S(1)}, u32[]{:S(2)}, u32[]{:S(2)}) collective-permute-start(f32[32,8,128]{2,1,0:T(8,128)} %get-tuple-element.109), channel_id=1, source_target_pairs={{0,5},{1,4},{2,7},{3,6},{4,1},{5,0},{6,3},{7,2},{8,13},{9,12},{10,... | collective-permute-start | bytes 393224 | tf_op jit(solution)/shard_map/ppermute | solution.py:263
  19.3 15.8 %collective-permute-start.27 = (f32[32,8,128]{2,1,0:T(8,128)}, f32[32,8,128]{2,1,0:T(8,128)S(1)}, u32[]{:S(2)}, u32[]{:S(2)}) collective-permute-start(f32[32,8,128]{2,1,0:T(8,128)} %get-tuple-element.111), channel_id=1, source_target_pairs={{0,4},{1,5},{2,6},{3,7},{4,0},{5,1},{6,2},{7,3},{8,12},{9,13},{10,... | collective-permute-start | bytes 393224 | tf_op jit(solution)/shard_map/ppermute | solution.py:263
  22.5 16.4 %collective-permute-start.28 = (f32[32,8,128]{2,1,0:T(8,128)}, f32[32,8,128]{2,1,0:T(8,128)S(1)}, u32[]{:S(2)}, u32[]{:S(2)}) collective-permute-start(f32[32,8,128]{2,1,0:T(8,128)} %get-tuple-element.112), channel_id=1, source_target_pairs={{0,15},{1,14},{2,13},{3,12},{4,11},{5,10},{6,9},{7,8},{8,7},{9,6},... | collective-permute-start | bytes 393224 | tf_op jit(solution)/shard_map/ppermute | solution.py:263
  25.5 13.4 %collective-permute-start.29 = (f32[32,8,128]{2,1,0:T(8,128)}, f32[32,8,128]{2,1,0:T(8,128)S(1)}, u32[]{:S(2)}, u32[]{:S(2)}) collective-permute-start(f32[32,8,128]{2,1,0:T(8,128)} %get-tuple-element.113), channel_id=1, source_target_pairs={{0,3},{1,2},{2,1},{3,0},{4,7},{5,6},{6,5},{7,4},{8,11},{9,10},{10,... | collective-permute-start | bytes 393224 | tf_op jit(solution)/shard_map/ppermute | solution.py:263
  27.1 18.7 %collective-permute-start.30 = (f32[32,8,128]{2,1,0:T(8,128)}, f32[32,8,128]{2,1,0:T(8,128)S(1)}, u32[]{:S(2)}, u32[]{:S(2)}) collective-permute-start(f32[32,8,128]{2,1,0:T(8,128)} %get-tuple-element.114), channel_id=1, source_target_pairs={{0,2},{1,3},{2,0},{3,1},{4,6},{5,7},{6,4},{7,5},{8,10},{9,11},{10,... | collective-permute-start | bytes 393224 | tf_op jit(solution)/shard_map/ppermute | solution.py:263
  29.9 20.2 %collective-permute-start.31 = (f32[32,8,128]{2,1,0:T(8,128)}, f32[32,8,128]{2,1,0:T(8,128)S(1)}, u32[]{:S(2)}, u32[]{:S(2)}) collective-permute-start(f32[32,8,128]{2,1,0:T(8,128)} %get-tuple-element.115), channel_id=1, source_target_pairs={{0,14},{1,15},{2,12},{3,13},{4,10},{5,11},{6,8},{7,9},{8,6},{9,7},... | collective-permute-start | bytes 393224 | tf_op jit(solution)/shard_map/ppermute | solution.py:263
  35.0 15.1 %collective-permute-start.32 = (f32[32,8,128]{2,1,0:T(8,128)}, f32[32,8,128]{2,1,0:T(8,128)S(1)}, u32[]{:S(2)}, u32[]{:S(2)}) collective-permute-start(f32[32,8,128]{2,1,0:T(8,128)} %get-tuple-element.116), channel_id=1, source_target_pairs={{0,1},{1,0},{2,3},{3,2},{4,5},{5,4},{6,7},{7,6},{8,9},{9,8},{10,11... | collective-permute-start | bytes 393224 | tf_op jit(solution)/shard_map/ppermute | solution.py:263
  38.9 16.3 %collective-permute-start.33 = (f32[32,8,128]{2,1,0:T(8,128)}, f32[32,8,128]{2,1,0:T(8,128)S(1)}, u32[]{:S(2)}, u32[]{:S(2)}) collective-permute-start(f32[32,8,128]{2,1,0:T(8,128)} %get-tuple-element.117), channel_id=1, source_target_pairs={{0,13},{1,12},{2,15},{3,14},{4,9},{5,8},{6,11},{7,10},{8,5},{9,4},... | collective-permute-start | bytes 393224 | tf_op jit(solution)/shard_map/ppermute | solution.py:263
  38.9 21.7 %collective-permute-start.34 = (f32[32,8,128]{2,1,0:T(8,128)}, f32[32,8,128]{2,1,0:T(8,128)S(1)}, u32[]{:S(2)}, u32[]{:S(2)}) collective-permute-start(f32[32,8,128]{2,1,0:T(8,128)} %get-tuple-element.118), channel_id=1, source_target_pairs={{0,12},{1,13},{2,14},{3,15},{4,8},{5,9},{6,10},{7,11},{8,4},{9,5},... | collective-permute-start | bytes 393224 | tf_op jit(solution)/shard_map/ppermute | solution.py:263
  45.8 14.7 %collective-permute-start = (f32[32,8,128]{2,1,0:T(8,128)}, f32[32,8,128]{2,1,0:T(8,128)S(1)}, u32[]{:S(2)}, u32[]{:S(2)}) collective-permute-start(f32[32,8,128]{2,1,0:T(8,128)} %get-tuple-element.81), channel_id=1, source_target_pairs={{0,8},{1,9},{2,10},{3,11},{4,12},{5,13},{6,14},{7,15},{8,0},{9,1},... | collective-permute-start | bytes 393224 | tf_op jit(solution)/shard_map/ppermute | solution.py:263
  50.1 14.9 %collective-permute-start.1 = (f32[32,8,128]{2,1,0:T(8,128)}, f32[32,8,128]{2,1,0:T(8,128)S(1)}, u32[]{:S(2)}, u32[]{:S(2)}) collective-permute-start(f32[32,8,128]{2,1,0:T(8,128)} %get-tuple-element.82), channel_id=1, source_target_pairs={{0,7},{1,6},{2,5},{3,4},{4,3},{5,2},{6,1},{7,0},{8,15},{9,14},{10,... | collective-permute-start | bytes 393224 | tf_op jit(solution)/shard_map/ppermute | solution.py:263
  50.1 15.1 %collective-permute-start.2 = (f32[32,8,128]{2,1,0:T(8,128)}, f32[32,8,128]{2,1,0:T(8,128)S(1)}, u32[]{:S(2)}, u32[]{:S(2)}) collective-permute-start(f32[32,8,128]{2,1,0:T(8,128)} %get-tuple-element.83), channel_id=1, source_target_pairs={{0,9},{1,8},{2,11},{3,10},{4,13},{5,12},{6,15},{7,14},{8,1},{9,0},... | collective-permute-start | bytes 393224 | tf_op jit(solution)/shard_map/ppermute | solution.py:263
  55.1 15.0 %collective-permute-start.3 = (f32[32,8,128]{2,1,0:T(8,128)}, f32[32,8,128]{2,1,0:T(8,128)S(1)}, u32[]{:S(2)}, u32[]{:S(2)}) collective-permute-start(f32[32,8,128]{2,1,0:T(8,128)} %get-tuple-element.84), channel_id=1, source_target_pairs={{0,6},{1,7},{2,4},{3,5},{4,2},{5,3},{6,0},{7,1},{8,14},{9,15},{10,... | collective-permute-start | bytes 393224 | tf_op jit(solution)/shard_map/ppermute | solution.py:263
  60.6 15.9 %collective-permute-start.5 = (f32[32,8,128]{2,1,0:T(8,128)}, f32[32,8,128]{2,1,0:T(8,128)S(1)}, u32[]{:S(2)}, u32[]{:S(2)}) collective-permute-start(f32[32,8,128]{2,1,0:T(8,128)} %get-tuple-element.86), channel_id=1, source_target_pairs={{0,5},{1,4},{2,7},{3,6},{4,1},{5,0},{6,3},{7,2},{8,13},{9,12},{10,... | collective-permute-start | bytes 393224 | tf_op jit(solution)/shard_map/ppermute | solution.py:263
  65.2 15.3 %collective-permute-start.7 = (f32[32,8,128]{2,1,0:T(8,128)}, f32[32,8,128]{2,1,0:T(8,128)S(1)}, u32[]{:S(2)}, u32[]{:S(2)}) collective-permute-start(f32[32,8,128]{2,1,0:T(8,128)} %get-tuple-element.88), channel_id=1, source_target_pairs={{0,4},{1,5},{2,6},{3,7},{4,0},{5,1},{6,2},{7,3},{8,12},{9,13},{10,... | collective-permute-start | bytes 393224 | tf_op jit(solution)/shard_map/ppermute | solution.py:263
  70.2 13.8 %collective-permute-start.8 = (f32[32,8,128]{2,1,0:T(8,128)}, f32[32,8,128]{2,1,0:T(8,128)S(1)}, u32[]{:S(2)}, u32[]{:S(2)}) collective-permute-start(f32[32,8,128]{2,1,0:T(8,128)} %get-tuple-element.89), channel_id=1, source_target_pairs={{0,15},{1,14},{2,13},{3,12},{4,11},{5,10},{6,9},{7,8},{8,7},{9,6},... | collective-permute-start | bytes 393224 | tf_op jit(solution)/shard_map/ppermute | solution.py:263
  70.2 13.8 %collective-permute-start.9 = (f32[32,8,128]{2,1,0:T(8,128)}, f32[32,8,128]{2,1,0:T(8,128)S(1)}, u32[]{:S(2)}, u32[]{:S(2)}) collective-permute-start(f32[32,8,128]{2,1,0:T(8,128)} %get-tuple-element.90), channel_id=1, source_target_pairs={{0,3},{1,2},{2,1},{3,0},{4,7},{5,6},{6,5},{7,4},{8,11},{9,10},{10,... | collective-permute-start | bytes 393224 | tf_op jit(solution)/shard_map/ppermute | solution.py:263
  76.5 16.7 %collective-permute-start.10 = (f32[32,8,128]{2,1,0:T(8,128)}, f32[32,8,128]{2,1,0:T(8,128)S(1)}, u32[]{:S(2)}, u32[]{:S(2)}) collective-permute-start(f32[32,8,128]{2,1,0:T(8,128)} %get-tuple-element.91), channel_id=1, source_target_pairs={{0,2},{1,3},{2,0},{3,1},{4,6},{5,7},{6,4},{7,5},{8,10},{9,11},{10,... | collective-permute-start | bytes 393224 | tf_op jit(solution)/shard_map/ppermute | solution.py:263
  77.0 19.2 %collective-permute-start.11 = (f32[32,8,128]{2,1,0:T(8,128)}, f32[32,8,128]{2,1,0:T(8,128)S(1)}, u32[]{:S(2)}, u32[]{:S(2)}) collective-permute-start(f32[32,8,128]{2,1,0:T(8,128)} %get-tuple-element.92), channel_id=1, source_target_pairs={{0,14},{1,15},{2,12},{3,13},{4,10},{5,11},{6,8},{7,9},{8,6},{9,7},... | collective-permute-start | bytes 393224 | tf_op jit(solution)/shard_map/ppermute | solution.py:263
  80.5 15.9 %collective-permute-start.12 = (f32[32,8,128]{2,1,0:T(8,128)}, f32[32,8,128]{2,1,0:T(8,128)S(1)}, u32[]{:S(2)}, u32[]{:S(2)}) collective-permute-start(f32[32,8,128]{2,1,0:T(8,128)} %get-tuple-element.93), channel_id=1, source_target_pairs={{0,1},{1,0},{2,3},{3,2},{4,5},{5,4},{6,7},{7,6},{8,9},{9,8},{10,11... | collective-permute-start | bytes 393224 | tf_op jit(solution)/shard_map/ppermute | solution.py:263
  84.0 14.4 %collective-permute-start.13 = (f32[32,8,128]{2,1,0:T(8,128)}, f32[32,8,128]{2,1,0:T(8,128)S(1)}, u32[]{:S(2)}, u32[]{:S(2)}) collective-permute-start(f32[32,8,128]{2,1,0:T(8,128)} %get-tuple-element.94), channel_id=1, source_target_pairs={{0,13},{1,12},{2,15},{3,14},{4,9},{5,8},{6,11},{7,10},{8,5},{9,4},... | collective-permute-start | bytes 393224 | tf_op jit(solution)/shard_map/ppermute | solution.py:263
  84.0 19.0 %collective-permute-start.14 = (f32[32,8,128]{2,1,0:T(8,128)}, f32[32,8,128]{2,1,0:T(8,128)S(1)}, u32[]{:S(2)}, u32[]{:S(2)}) collective-permute-start(f32[32,8,128]{2,1,0:T(8,128)} %get-tuple-element.95), channel_id=1, source_target_pairs={{0,12},{1,13},{2,14},{3,15},{4,8},{5,9},{6,10},{7,11},{8,4},{9,5},... | collective-permute-start | bytes 393224 | tf_op jit(solution)/shard_map/ppermute | solution.py:263
  96.2 13.8 %collective-permute-start.36 = (f32[32,8,128]{2,1,0:T(8,128)S(1)}, f32[32,8,128]{2,1,0:T(8,128)S(1)}, u32[]{:S(2)}, u32[]{:S(2)}) collective-permute-start(f32[32,8,128]{2,1,0:T(8,128)S(1)} %get-tuple-element.121), channel_id=1, source_target_pairs={{0,7},{1,6},{2,5},{3,4},{4,3},{5,2},{6,1},{7,0},{8,15},{9,14},{10,... | collective-permute-start | bytes 393224 | tf_op jit(solution)/shard_map/ppermute | solution.py:263
  96.4 15.0 %collective-permute-start.37 = (f32[32,8,128]{2,1,0:T(8,128)S(1)}, f32[32,8,128]{2,1,0:T(8,128)S(1)}, u32[]{:S(2)}, u32[]{:S(2)}) collective-permute-start(f32[32,8,128]{2,1,0:T(8,128)S(1)} %get-tuple-element.122), channel_id=1, source_target_pairs={{0,9},{1,8},{2,11},{3,10},{4,13},{5,12},{6,15},{7,14},{8,1},{9,0},... | collective-permute-start | bytes 393224 | tf_op jit(solution)/shard_map/ppermute | solution.py:263
  98.4 17.0 %collective-permute-start.38 = (f32[32,8,128]{2,1,0:T(8,128)S(1)}, f32[32,8,128]{2,1,0:T(8,128)S(1)}, u32[]{:S(2)}, u32[]{:S(2)}) collective-permute-start(f32[32,8,128]{2,1,0:T(8,128)S(1)} %get-tuple-element.123), channel_id=1, source_target_pairs={{0,6},{1,7},{2,4},{3,5},{4,2},{5,3},{6,0},{7,1},{8,14},{9,15},{10,... | collective-permute-start | bytes 393224 | tf_op jit(solution)/shard_map/ppermute | solution.py:263
  102.9 14.2 %collective-permute-start.39 = (f32[32,8,128]{2,1,0:T(8,128)S(1)}, f32[32,8,128]{2,1,0:T(8,128)S(1)}, u32[]{:S(2)}, u32[]{:S(2)}) collective-permute-start(f32[32,8,128]{2,1,0:T(8,128)S(1)} %get-tuple-element.124), channel_id=1, source_target_pairs={{0,11},{1,10},{2,9},{3,8},{4,15},{5,14},{6,13},{7,12},{8,3},{9,2},... | collective-permute-start | bytes 393224 | tf_op jit(solution)/shard_map/ppermute | solution.py:263
  105.7 13.2 %collective-permute-start.40 = (f32[32,8,128]{2,1,0:T(8,128)S(1)}, f32[32,8,128]{2,1,0:T(8,128)S(1)}, u32[]{:S(2)}, u32[]{:S(2)}) collective-permute-start(f32[32,8,128]{2,1,0:T(8,128)S(1)} %get-tuple-element.125), channel_id=1, source_target_pairs={{0,5},{1,4},{2,7},{3,6},{4,1},{5,0},{6,3},{7,2},{8,13},{9,12},{10,... | collective-permute-start | bytes 393224 | tf_op jit(solution)/shard_map/ppermute | solution.py:263
  111.4 15.3 %collective-permute-start.42 = (f32[32,8,128]{2,1,0:T(8,128)S(1)}, f32[32,8,128]{2,1,0:T(8,128)S(1)}, u32[]{:S(2)}, u32[]{:S(2)}) collective-permute-start(f32[32,8,128]{2,1,0:T(8,128)S(1)} %get-tuple-element.127), channel_id=1, source_target_pairs={{0,4},{1,5},{2,6},{3,7},{4,0},{5,1},{6,2},{7,3},{8,12},{9,13},{10,... | collective-permute-start | bytes 393224 | tf_op jit(solution)/shard_map/ppermute | solution.py:263
  115.4 13.7 %collective-permute-start.43 = (f32[32,8,128]{2,1,0:T(8,128)S(1)}, f32[32,8,128]{2,1,0:T(8,128)S(1)}, u32[]{:S(2)}, u32[]{:S(2)}) collective-permute-start(f32[32,8,128]{2,1,0:T(8,128)S(1)} %get-tuple-element.128), channel_id=1, source_target_pairs={{0,15},{1,14},{2,13},{3,12},{4,11},{5,10},{6,9},{7,8},{8,7},{9,6},... | collective-permute-start | bytes 393224 | tf_op jit(solution)/shard_map/ppermute | solution.py:263
  118.9 19.3 %collective-permute-start.45 = (f32[32,8,128]{2,1,0:T(8,128)S(1)}, f32[32,8,128]{2,1,0:T(8,128)S(1)}, u32[]{:S(2)}, u32[]{:S(2)}) collective-permute-start(f32[32,8,128]{2,1,0:T(8,128)S(1)} %get-tuple-element.130), channel_id=1, source_target_pairs={{0,2},{1,3},{2,0},{3,1},{4,6},{5,7},{6,4},{7,5},{8,10},{9,11},{10,... | collective-permute-start | bytes 393224 | tf_op jit(solution)/shard_map/ppermute | solution.py:263
  122.8 18.3 %collective-permute-start.46 = (f32[32,8,128]{2,1,0:T(8,128)S(1)}, f32[32,8,128]{2,1,0:T(8,128)S(1)}, u32[]{:S(2)}, u32[]{:S(2)}) collective-permute-start(f32[32,8,128]{2,1,0:T(8,128)S(1)} %get-tuple-element.131), channel_id=1, source_target_pairs={{0,14},{1,15},{2,12},{3,13},{4,10},{5,11},{6,8},{7,9},{8,6},{9,7},... | collective-permute-start | bytes 393224 | tf_op jit(solution)/shard_map/ppermute | solution.py:263
  126.7 15.0 %collective-permute-start.47 = (f32[32,8,128]{2,1,0:T(8,128)S(1)}, f32[32,8,128]{2,1,0:T(8,128)S(1)}, u32[]{:S(2)}, u32[]{:S(2)}) collective-permute-start(f32[32,8,128]{2,1,0:T(8,128)S(1)} %get-tuple-element.132), channel_id=1, source_target_pairs={{0,1},{1,0},{2,3},{3,2},{4,5},{5,4},{6,7},{7,6},{8,9},{9,8},{10,11... | collective-permute-start | bytes 393224 | tf_op jit(solution)/shard_map/ppermute | solution.py:263
  129.1 14.5 %collective-permute-start.48 = (f32[32,8,128]{2,1,0:T(8,128)S(1)}, f32[32,8,128]{2,1,0:T(8,128)S(1)}, u32[]{:S(2)}, u32[]{:S(2)}) collective-permute-start(f32[32,8,128]{2,1,0:T(8,128)S(1)} %get-tuple-element.133), channel_id=1, source_target_pairs={{0,13},{1,12},{2,15},{3,14},{4,9},{5,8},{6,11},{7,10},{8,5},{9,4},... | collective-permute-start | bytes 393224 | tf_op jit(solution)/shard_map/ppermute | solution.py:263
  129.1 19.4 %collective-permute-start.49 = (f32[32,8,128]{2,1,0:T(8,128)S(1)}, f32[32,8,128]{2,1,0:T(8,128)S(1)}, u32[]{:S(2)}, u32[]{:S(2)}) collective-permute-start(f32[32,8,128]{2,1,0:T(8,128)S(1)} %get-tuple-element.134), channel_id=1, source_target_pairs={{0,12},{1,13},{2,14},{3,15},{4,8},{5,9},{6,10},{7,11},{8,4},{9,5},... | collective-permute-start | bytes 393224 | tf_op jit(solution)/shard_map/ppermute | solution.py:263
  138.2 12.9 %collective-permute-start.50 = (f32[32,8,128]{2,1,0:T(8,128)S(1)}, f32[32,8,128]{2,1,0:T(8,128)S(1)}, u32[]{:S(2)}, u32[]{:S(2)}) collective-permute-start(f32[32,8,128]{2,1,0:T(8,128)S(1)} %get-tuple-element.136), channel_id=1, source_target_pairs={{0,8},{1,9},{2,10},{3,11},{4,12},{5,13},{6,14},{7,15},{8,0},{9,1},... | collective-permute-start | bytes 393224 | tf_op jit(solution)/shard_map/ppermute | solution.py:263
  141.0 14.4 %collective-permute-start.51 = (f32[32,8,128]{2,1,0:T(8,128)S(1)}, f32[32,8,128]{2,1,0:T(8,128)S(1)}, u32[]{:S(2)}, u32[]{:S(2)}) collective-permute-start(f32[32,8,128]{2,1,0:T(8,128)S(1)} %get-tuple-element.137), channel_id=1, source_target_pairs={{0,7},{1,6},{2,5},{3,4},{4,3},{5,2},{6,1},{7,0},{8,15},{9,14},{10,... | collective-permute-start | bytes 393224 | tf_op jit(solution)/shard_map/ppermute | solution.py:263
  141.7 15.1 %collective-permute-start.52 = (f32[32,8,128]{2,1,0:T(8,128)S(1)}, f32[32,8,128]{2,1,0:T(8,128)S(1)}, u32[]{:S(2)}, u32[]{:S(2)}) collective-permute-start(f32[32,8,128]{2,1,0:T(8,128)S(1)} %get-tuple-element.138), channel_id=1, source_target_pairs={{0,9},{1,8},{2,11},{3,10},{4,13},{5,12},{6,15},{7,14},{8,1},{9,0},... | collective-permute-start | bytes 393224 | tf_op jit(solution)/shard_map/ppermute | solution.py:263
  143.6 16.9 %collective-permute-start.53 = (f32[32,8,128]{2,1,0:T(8,128)S(1)}, f32[32,8,128]{2,1,0:T(8,128)S(1)}, u32[]{:S(2)}, u32[]{:S(2)}) collective-permute-start(f32[32,8,128]{2,1,0:T(8,128)S(1)} %get-tuple-element.139), channel_id=1, source_target_pairs={{0,6},{1,7},{2,4},{3,5},{4,2},{5,3},{6,0},{7,1},{8,14},{9,15},{10,... | collective-permute-start | bytes 393224 | tf_op jit(solution)/shard_map/ppermute | solution.py:263
  148.4 13.9 %collective-permute-start.54 = (f32[32,8,128]{2,1,0:T(8,128)S(1)}, f32[32,8,128]{2,1,0:T(8,128)S(1)}, u32[]{:S(2)}, u32[]{:S(2)}) collective-permute-start(f32[32,8,128]{2,1,0:T(8,128)S(1)} %get-tuple-element.140), channel_id=1, source_target_pairs={{0,11},{1,10},{2,9},{3,8},{4,15},{5,14},{6,13},{7,12},{8,3},{9,2},... | collective-permute-start | bytes 393224 | tf_op jit(solution)/shard_map/ppermute | solution.py:263
  151.1 12.9 %collective-permute-start.55 = (f32[32,8,128]{2,1,0:T(8,128)S(1)}, f32[32,8,128]{2,1,0:T(8,128)S(1)}, u32[]{:S(2)}, u32[]{:S(2)}) collective-permute-start(f32[32,8,128]{2,1,0:T(8,128)S(1)} %get-tuple-element.141), channel_id=1, source_target_pairs={{0,5},{1,4},{2,7},{3,6},{4,1},{5,0},{6,3},{7,2},{8,13},{9,12},{10,... | collective-permute-start | bytes 393224 | tf_op jit(solution)/shard_map/ppermute | solution.py:263
  156.8 15.3 %collective-permute-start.57 = (f32[32,8,128]{2,1,0:T(8,128)S(1)}, f32[32,8,128]{2,1,0:T(8,128)S(1)}, u32[]{:S(2)}, u32[]{:S(2)}) collective-permute-start(f32[32,8,128]{2,1,0:T(8,128)S(1)} %get-tuple-element.143), channel_id=1, source_target_pairs={{0,4},{1,5},{2,6},{3,7},{4,0},{5,1},{6,2},{7,3},{8,12},{9,13},{10,... | collective-permute-start | bytes 393224 | tf_op jit(solution)/shard_map/ppermute | solution.py:263
  160.5 13.6 %collective-permute-start.58 = (f32[32,8,128]{2,1,0:T(8,128)S(1)}, f32[32,8,128]{2,1,0:T(8,128)S(1)}, u32[]{:S(2)}, u32[]{:S(2)}) collective-permute-start(f32[32,8,128]{2,1,0:T(8,128)S(1)} %get-tuple-element.144), channel_id=1, source_target_pairs={{0,15},{1,14},{2,13},{3,12},{4,11},{5,10},{6,9},{7,8},{8,7},{9,6},... | collective-permute-start | bytes 393224 | tf_op jit(solution)/shard_map/ppermute | solution.py:263
  164.0 14.5 %collective-permute-start.15 = (f32[32,8,128]{2,1,0:T(8,128)S(1)}, f32[32,8,128]{2,1,0:T(8,128)S(1)}, u32[]{:S(2)}, u32[]{:S(2)}) collective-permute-start(f32[32,8,128]{2,1,0:T(8,128)S(1)} %get-tuple-element.97), channel_id=1, source_target_pairs={{0,2},{1,3},{2,0},{3,1},{4,6},{5,7},{6,4},{7,5},{8,10},{9,11},{10,... | collective-permute-start | bytes 393224 | tf_op jit(solution)/shard_map/ppermute | solution.py:263
  168.0 17.3 %collective-permute-start.16 = (f32[32,8,128]{2,1,0:T(8,128)S(1)}, f32[32,8,128]{2,1,0:T(8,128)S(1)}, u32[]{:S(2)}, u32[]{:S(2)}) collective-permute-start(f32[32,8,128]{2,1,0:T(8,128)S(1)} %get-tuple-element.98), channel_id=1, source_target_pairs={{0,14},{1,15},{2,12},{3,13},{4,10},{5,11},{6,8},{7,9},{8,6},{9,7},... | collective-permute-start | bytes 393224 | tf_op jit(solution)/shard_map/ppermute | solution.py:263
  172.1 13.3 %collective-permute-start.17 = (f32[32,8,128]{2,1,0:T(8,128)S(1)}, f32[32,8,128]{2,1,0:T(8,128)S(1)}, u32[]{:S(2)}, u32[]{:S(2)}) collective-permute-start(f32[32,8,128]{2,1,0:T(8,128)S(1)} %get-tuple-element.99), channel_id=1, source_target_pairs={{0,1},{1,0},{2,3},{3,2},{4,5},{5,4},{6,7},{7,6},{8,9},{9,8},{10,11... | collective-permute-start | bytes 393224 | tf_op jit(solution)/shard_map/ppermute | solution.py:263
  174.1 13.4 %collective-permute-start.18 = (f32[32,8,128]{2,1,0:T(8,128)S(1)}, f32[32,8,128]{2,1,0:T(8,128)S(1)}, u32[]{:S(2)}, u32[]{:S(2)}) collective-permute-start(f32[32,8,128]{2,1,0:T(8,128)S(1)} %get-tuple-element.100), channel_id=1, source_target_pairs={{0,13},{1,12},{2,15},{3,14},{4,9},{5,8},{6,11},{7,10},{8,5},{9,4},... | collective-permute-start | bytes 393224 | tf_op jit(solution)/shard_map/ppermute | solution.py:263
  174.1 16.2 %collective-permute-start.19 = (f32[32,8,128]{2,1,0:T(8,128)S(1)}, f32[32,8,128]{2,1,0:T(8,128)S(1)}, u32[]{:S(2)}, u32[]{:S(2)}) collective-permute-start(f32[32,8,128]{2,1,0:T(8,128)S(1)} %get-tuple-element.101), channel_id=1, source_target_pairs={{0,12},{1,13},{2,14},{3,15},{4,8},{5,9},{6,10},{7,11},{8,4},{9,5},... | collective-permute-start | bytes 393224 | tf_op jit(solution)/shard_map/ppermute | solution.py:263
  (21 other events, 774.6 us)

commit v4 on v3

--- a/solution.py
+++ b/solution.py
@@ -14,7 +14,7 @@
 FIRST_LIMIT = 60 * 1024 * 1024
 GRAIN = 16
 OUT_GRAIN = 4
-LATE = 5
+LATE = 4
 
 
 def split(value):
@@ -24,9 +24,10 @@
 
 def product(left, right):
     dot = functools.partial(jnp.dot, preferred_element_type=F32)
-    rows = left[0].shape[0]
-    both = dot(jnp.concatenate(left, axis=0), right[0])
-    return both[:rows] + (both[rows:] + dot(left[0], right[1]))
+    return dot(
+        jnp.concatenate([left[0], left[1], left[0]], axis=1),
+        jnp.concatenate([right[0], right[0], right[1]], axis=0),
+    )
 
 
 def react(value, kinetics):
@@ -63,8 +64,8 @@
     order = []
     for index in range(half):
         order.append(half + (index ^ (index >> 1) if 2 * index < half else 3 * half // 2 - 1 - index))
-        order += [half - 1 - near for near in range(half - 1) if near - near // 5 == index]
-    return order + [0]
+        order.append(half - 1 - index)
+    return order
 
 
 def arrivals(ranks):

time: 193 us -> 193 us (level)
  waiting for transfers between devices: 65.6 us -> 51.9 us
  starting transfers between devices: 93.6 us -> 107 us
    ppermute x60, waiting for transfers between devices: 65.6 us -> 51.9 us  [exchange(): lax.ppermute(block, ('row', 'col'), [(i, i ^ place) for i in range(ranks)])]
    ppermute x60, starting transfers between devices: 93.6 us -> 107 us  [exchange(): lax.ppermute(block, ('row', 'col'), [(i, i ^ place) for i in range(ranks)])]
  transfers between devices with their start and end apart: 60 -> 60, of which waited for: 25 -> 19; matrix products, arithmetic and copies ran while one was open for 0% -> 0% of each run, Pallas kernels for 13% -> 13%
where the time goes in v4:
time: 193 us
  starting transfers between devices  107 us (55%)
  waiting for transfers between devices  51.9 us (27%)
  Pallas kernels  32.9 us (17%)
    ppermute x60, starting transfers between devices, exchange(): lax.ppermute(block, ('row', 'col'), [(i, i ^ place) for i in range(ranks)])  107 us
    ppermute x60, waiting for transfers between devices, exchange(): lax.ppermute(block, ('row', 'col'), [(i, i ^ place) for i in range(ranks)])  51.9 us
    pallas_call x2, Pallas kernels, planes(): pl.pallas_call(functools.partial(plane_sweeps, columns, ranks), grid=(1,)...  14.7 us
    pallas_call x2, Pallas kernels, first(): pl.pallas_call(functools.partial(first_sweep, chunk, columns), grid=(1,),...  10.6 us
  transfers between devices with their start and end apart: 60, of which 19 were waited for; matrix products, arithmetic and copies ran while one was open for 0% of the time, Pallas kernels for 13%

profile of v4, /device:TPU:17, one launch (start us, length us, event | category | flops | bytes accessed | tf_op | source)
XLA Modules:
  0.0 193.0 jit_solution(5361003373452332990)
XLA Ops:
  0.7 5.4 %first_sweep_0.1 = (f32[32,8,128]{2,1,0:T(8,128)}, f32[32,8,128]{2,1,0:T(8,128)}, f32[32,8,128]{2,1,0:T(8,128)}, f32[32,8,128]{2,1,0:T(8,128)}, f32[32,8,128]{2,...) custom-call(s32[1]{0:T(128)S(6)} %copy.10.species, ...), custom_call_target="tpu_custom_call" | custom-call | flops 805306368 | bytes 6291456 | tf_op jit(solution)/shard_map/first_sweep_0/pallas_call | solution.py:272
  6.2 3.1 %collective-permute-start.20 = (f32[32,8,128]{2,1,0:T(8,128)}, f32[32,8,128]{2,1,0:T(8,128)S(1)}, u32[]{:S(2)}, u32[]{:S(2)}) collective-permute-start(f32[32,8,128]{2,1,0:T(8,128)} %get-tuple-element.104), channel_id=1, source_target_pairs={{0,7},{1,6},{2,5},{3,4},{4,3},{5,2},{6,1},{7,0},{8,15},{9,14},{10,... | collective-permute-start | bytes 393224 | tf_op jit(solution)/shard_map/ppermute | solution.py:264
  9.3 1.7 collective-permute-start.21
  11.6 1.7 collective-permute-start.23
  13.3 4.2 %collective-permute-start.24 = (f32[32,8,128]{2,1,0:T(8,128)}, f32[32,8,128]{2,1,0:T(8,128)S(1)}, u32[]{:S(2)}, u32[]{:S(2)}) collective-permute-start(f32[32,8,128]{2,1,0:T(8,128)} %get-tuple-element.108), channel_id=1, source_target_pairs={{0,5},{1,4},{2,7},{3,6},{4,1},{5,0},{6,3},{7,2},{8,13},{9,12},{10,... | collective-permute-start | bytes 393224 | tf_op jit(solution)/shard_map/ppermute | solution.py:264
  17.5 1.8 collective-permute-start.25
  19.3 3.3 %collective-permute-start.26 = (f32[32,8,128]{2,1,0:T(8,128)}, f32[32,8,128]{2,1,0:T(8,128)S(1)}, u32[]{:S(2)}, u32[]{:S(2)}) collective-permute-start(f32[32,8,128]{2,1,0:T(8,128)} %get-tuple-element.110), channel_id=1, source_target_pairs={{0,4},{1,5},{2,6},{3,7},{4,0},{5,1},{6,2},{7,3},{8,12},{9,13},{10,... | collective-permute-start | bytes 393224 | tf_op jit(solution)/shard_map/ppermute | solution.py:264
  22.9 2.6 %collective-permute-done.23.refs_4_ = f32[32,8,128]{2,1,0:T(8,128)S(1)} collective-permute-done((f32[32,8,128]{2,1,0:T(8,128)}, f32[32,8,128]{2,1,0:T(8,128)S(1)}, u32[]{:S(2)}, u32[]{:S(2)}) %collective-permute-start.23) | collective-permute-done | bytes 131104 | tf_op jit(solution)/shard_map/ppermute | solution.py:264
  25.5 1.7 collective-permute-start.28
  27.2 1.7 collective-permute-start.29
  31.0 6.9 %collective-permute-done.26.refs_7_ = f32[32,8,128]{2,1,0:T(8,128)S(1)} collective-permute-done((f32[32,8,128]{2,1,0:T(8,128)}, f32[32,8,128]{2,1,0:T(8,128)S(1)}, u32[]{:S(2)}, u32[]{:S(2)}) %collective-permute-start.26) | collective-permute-done | bytes 131104 | tf_op jit(solution)/shard_map/ppermute | solution.py:264
  37.9 5.2 %collective-permute-done.27.refs_8_ = f32[32,8,128]{2,1,0:T(8,128)S(1)} collective-permute-done((f32[32,8,128]{2,1,0:T(8,128)}, f32[32,8,128]{2,1,0:T(8,128)S(1)}, u32[]{:S(2)}, u32[]{:S(2)}) %collective-permute-start.27) | collective-permute-done | bytes 131104 | tf_op jit(solution)/shard_map/ppermute | solution.py:264
  43.6 5.2 %first_sweep_1.1 = (f32[32,8,128]{2,1,0:T(8,128)}, f32[32,8,128]{2,1,0:T(8,128)}, f32[32,8,128]{2,1,0:T(8,128)}, f32[32,8,128]{2,1,0:T(8,128)}, f32[32,8,128]{2,...) custom-call(s32[1]{0:T(128)S(6)} %copy.10.species, ...), custom_call_target="tpu_custom_call" | custom-call | flops 805306368 | bytes 6291456 | tf_op jit(solution)/shard_map/first_sweep_1/pallas_call | solution.py:272
  48.8 1.4 collective-permute-done.29.refs_10_
  53.4 3.4 %collective-permute-start.3 = (f32[32,8,128]{2,1,0:T(8,128)}, f32[32,8,128]{2,1,0:T(8,128)S(1)}, u32[]{:S(2)}, u32[]{:S(2)}) collective-permute-start(f32[32,8,128]{2,1,0:T(8,128)} %get-tuple-element.84), channel_id=1, source_target_pairs={{0,6},{1,7},{2,4},{3,5},{4,2},{5,3},{6,0},{7,1},{8,14},{9,15},{10,... | collective-permute-start | bytes 393224 | tf_op jit(solution)/shard_map/ppermute | solution.py:264
  58.7 6.4 %collective-permute-start.5 = (f32[32,8,128]{2,1,0:T(8,128)}, f32[32,8,128]{2,1,0:T(8,128)S(1)}, u32[]{:S(2)}, u32[]{:S(2)}) collective-permute-start(f32[32,8,128]{2,1,0:T(8,128)} %get-tuple-element.86), channel_id=1, source_target_pairs={{0,5},{1,4},{2,7},{3,6},{4,1},{5,0},{6,3},{7,2},{8,13},{9,12},{10,... | collective-permute-start | bytes 393224 | tf_op jit(solution)/shard_map/ppermute | solution.py:264
  65.3 4.9 %collective-permute-start.7 = (f32[32,8,128]{2,1,0:T(8,128)}, f32[32,8,128]{2,1,0:T(8,128)S(1)}, u32[]{:S(2)}, u32[]{:S(2)}) collective-permute-start(f32[32,8,128]{2,1,0:T(8,128)} %get-tuple-element.88), channel_id=1, source_target_pairs={{0,4},{1,5},{2,6},{3,7},{4,0},{5,1},{6,2},{7,3},{8,12},{9,13},{10,... | collective-permute-start | bytes 393224 | tf_op jit(solution)/shard_map/ppermute | solution.py:264
  70.3 4.1 %collective-permute-start.9 = (f32[32,8,128]{2,1,0:T(8,128)}, f32[32,8,128]{2,1,0:T(8,128)S(1)}, u32[]{:S(2)}, u32[]{:S(2)}) collective-permute-start(f32[32,8,128]{2,1,0:T(8,128)} %get-tuple-element.90), channel_id=1, source_target_pairs={{0,3},{1,2},{2,1},{3,0},{4,7},{5,6},{6,5},{7,4},{8,11},{9,10},{10,... | collective-permute-start | bytes 393224 | tf_op jit(solution)/shard_map/ppermute | solution.py:264
  74.5 2.3 %prepare.1 = (f32[2,256]{1,0:T(2,128)S(1)}, bf16[4,256,256]{2,1,0:T(8,128)(2,1)S(1)}, bf16[4,256,256]{2,1,0:T(8,128)(2,1)S(1)}, bf16[256,224]{1,0:T(8,128)(2,1)S...) custom-call(s32[1]{0:T(128)S(6)} %copy.10.species, f32[64]{0:T(128)S(1)} %copy-done.3, ...), custom_call_target="tpu_custom_call" | custom-call | flops 805306368 | bytes 2097152 | tf_op jit(solution)/shard_map/prepare/pallas_call | solution.py:338
  78.0 1.4 collective-permute-start.11
  81.6 2.4 %collective-permute-done.8.refs_8_ = f32[32,8,128]{2,1,0:T(8,128)S(1)} collective-permute-done((f32[32,8,128]{2,1,0:T(8,128)}, f32[32,8,128]{2,1,0:T(8,128)S(1)}, u32[]{:S(2)}, u32[]{:S(2)}) %collective-permute-start.8) | collective-permute-done | bytes 131104 | tf_op jit(solution)/shard_map/ppermute | solution.py:264
  84.5 2.4 %collective-permute-start.14 = (f32[32,8,128]{2,1,0:T(8,128)}, f32[32,8,128]{2,1,0:T(8,128)S(1)}, u32[]{:S(2)}, u32[]{:S(2)}) collective-permute-start(f32[32,8,128]{2,1,0:T(8,128)} %get-tuple-element.95), channel_id=1, source_target_pairs={{0,12},{1,13},{2,14},{3,15},{4,8},{5,9},{6,10},{7,11},{8,4},{9,5},... | collective-permute-start | bytes 393224 | tf_op jit(solution)/shard_map/ppermute | solution.py:264
  86.9 7.4 %plane_sweeps_0.1 = (f32[32,8,128]{2,1,0:T(8,128)S(1)}, f32[32,8,128]{2,1,0:T(8,128)S(1)}, f32[32,8,128]{2,1,0:T(8,128)S(1)}, f32[32,8,128]{2,1,0:T(8,128)S(1)},...) custom-call(f32[2,256]{1,0:T(2,128)S(1)} %get-tuple-element.76.kinet, ...), custom_call_target="tpu_custom_call" | custom-call | flops 3221225472 | bytes 4194304 | tf_op jit(solution)/shard_map/plane_sweeps_0/pallas_call | solution.py:290
  95.3 1.5 collective-permute-start.35
  98.5 1.8 collective-permute-start.37
  100.3 2.5 %collective-permute-done.14.refs_14_ = f32[32,8,128]{2,1,0:T(8,128)S(1)} collective-permute-done((f32[32,8,128]{2,1,0:T(8,128)}, f32[32,8,128]{2,1,0:T(8,128)S(1)}, u32[]{:S(2)}, u32[]{:S(2)}) %collective-permute-start.14) | collective-permute-done | bytes 131104 | tf_op jit(solution)/shard_map/ppermute | solution.py:264
  102.9 7.3 %collective-permute-start.39 = (f32[32,8,128]{2,1,0:T(8,128)S(1)}, f32[32,8,128]{2,1,0:T(8,128)S(1)}, u32[]{:S(2)}, u32[]{:S(2)}) collective-permute-start(f32[32,8,128]{2,1,0:T(8,128)S(1)} %get-tuple-element.124), channel_id=1, source_target_pairs={{0,5},{1,4},{2,7},{3,6},{4,1},{5,0},{6,3},{7,2},{8,13},{9,12},{10,... | collective-permute-start | bytes 393224 | tf_op jit(solution)/shard_map/ppermute | solution.py:264
  110.3 5.0 %collective-permute-start.41 = (f32[32,8,128]{2,1,0:T(8,128)S(1)}, f32[32,8,128]{2,1,0:T(8,128)S(1)}, u32[]{:S(2)}, u32[]{:S(2)}) collective-permute-start(f32[32,8,128]{2,1,0:T(8,128)S(1)} %get-tuple-element.126), channel_id=1, source_target_pairs={{0,4},{1,5},{2,6},{3,7},{4,0},{5,1},{6,2},{7,3},{8,12},{9,13},{10,... | collective-permute-start | bytes 393224 | tf_op jit(solution)/shard_map/ppermute | solution.py:264
  115.3 4.0 %collective-permute-start.43 = (f32[32,8,128]{2,1,0:T(8,128)S(1)}, f32[32,8,128]{2,1,0:T(8,128)S(1)}, u32[]{:S(2)}, u32[]{:S(2)}) collective-permute-start(f32[32,8,128]{2,1,0:T(8,128)S(1)} %get-tuple-element.128), channel_id=1, source_target_pairs={{0,3},{1,2},{2,1},{3,0},{4,7},{5,6},{6,5},{7,4},{8,11},{9,10},{10,... | collective-permute-start | bytes 393224 | tf_op jit(solution)/shard_map/ppermute | solution.py:264
  121.8 3.1 %collective-permute-done.41.refs_7_ = f32[32,8,128]{2,1,0:T(8,128)S(1)} collective-permute-done((f32[32,8,128]{2,1,0:T(8,128)S(1)}, f32[32,8,128]{2,1,0:T(8,128)S(1)}, u32[]{:S(2)}, u32[]{:S(2)}) %collective-permute-start.41) | collective-permute-done | bytes 131104 | tf_op jit(solution)/shard_map/ppermute | solution.py:264
  125.0 1.6 collective-permute-start.46
  126.6 5.3 %collective-permute-done.42.refs_8_ = f32[32,8,128]{2,1,0:T(8,128)S(1)} collective-permute-done((f32[32,8,128]{2,1,0:T(8,128)S(1)}, f32[32,8,128]{2,1,0:T(8,128)S(1)}, u32[]{:S(2)}, u32[]{:S(2)}) %collective-permute-start.42) | collective-permute-done | bytes 131104 | tf_op jit(solution)/shard_map/ppermute | solution.py:264
  132.3 7.3 %plane_sweeps_1.1 = (f32[32,8,128]{2,1,0:T(8,128)S(1)}, f32[32,8,128]{2,1,0:T(8,128)S(1)}, f32[32,8,128]{2,1,0:T(8,128)S(1)}, f32[32,8,128]{2,1,0:T(8,128)S(1)},...) custom-call(f32[2,256]{1,0:T(2,128)S(1)} %get-tuple-element.76.kinet, ...), custom_call_target="tpu_custom_call" | custom-call | flops 3221225472 | bytes 4194304 | tf_op jit(solution)/shard_map/plane_sweeps_1/pallas_call | solution.py:290
  139.6 3.1 %collective-permute-start.49 = (f32[32,8,128]{2,1,0:T(8,128)S(1)}, f32[32,8,128]{2,1,0:T(8,128)S(1)}, u32[]{:S(2)}, u32[]{:S(2)}) collective-permute-start(f32[32,8,128]{2,1,0:T(8,128)S(1)} %get-tuple-element.135), channel_id=1, source_target_pairs={{0,8},{1,9},{2,10},{3,11},{4,12},{5,13},{6,14},{7,15},{8,0},{9,1},... | collective-permute-start | bytes 393224 | tf_op jit(solution)/shard_map/ppermute | solution.py:264
  142.7 1.4 collective-permute-start.50
  144.1 2.0 %collective-permute-start.51 = (f32[32,8,128]{2,1,0:T(8,128)S(1)}, f32[32,8,128]{2,1,0:T(8,128)S(1)}, u32[]{:S(2)}, u32[]{:S(2)}) collective-permute-start(f32[32,8,128]{2,1,0:T(8,128)S(1)} %get-tuple-element.137), channel_id=1, source_target_pairs={{0,9},{1,8},{2,11},{3,10},{4,13},{5,12},{6,15},{7,14},{8,1},{9,0},... | collective-permute-start | bytes 393224 | tf_op jit(solution)/shard_map/ppermute | solution.py:264
  148.9 6.5 %collective-permute-start.54 = (f32[32,8,128]{2,1,0:T(8,128)S(1)}, f32[32,8,128]{2,1,0:T(8,128)S(1)}, u32[]{:S(2)}, u32[]{:S(2)}) collective-permute-start(f32[32,8,128]{2,1,0:T(8,128)S(1)} %get-tuple-element.140), channel_id=1, source_target_pairs={{0,5},{1,4},{2,7},{3,6},{4,1},{5,0},{6,3},{7,2},{8,13},{9,12},{10,... | collective-permute-start | bytes 393224 | tf_op jit(solution)/shard_map/ppermute | solution.py:264
  155.4 5.1 %collective-permute-start.56 = (f32[32,8,128]{2,1,0:T(8,128)S(1)}, f32[32,8,128]{2,1,0:T(8,128)S(1)}, u32[]{:S(2)}, u32[]{:S(2)}) collective-permute-start(f32[32,8,128]{2,1,0:T(8,128)S(1)} %get-tuple-element.142), channel_id=1, source_target_pairs={{0,4},{1,5},{2,6},{3,7},{4,0},{5,1},{6,2},{7,3},{8,12},{9,13},{10,... | collective-permute-start | bytes 393224 | tf_op jit(solution)/shard_map/ppermute | solution.py:264
  160.4 1.8 collective-permute-start.58
  162.2 3.3 %collective-permute-start.59 = (f32[32,8,128]{2,1,0:T(8,128)S(1)}, f32[32,8,128]{2,1,0:T(8,128)S(1)}, u32[]{:S(2)}, u32[]{:S(2)}) collective-permute-start(f32[32,8,128]{2,1,0:T(8,128)S(1)} %get-tuple-element.145), channel_id=1, source_target_pairs={{0,14},{1,15},{2,12},{3,13},{4,10},{5,11},{6,8},{7,9},{8,6},{9,7},... | collective-permute-start | bytes 393224 | tf_op jit(solution)/shard_map/ppermute | solution.py:264
  165.5 1.3 collective-permute-start.15
  166.8 4.8 %collective-permute-start.16 = (f32[32,8,128]{2,1,0:T(8,128)S(1)}, f32[32,8,128]{2,1,0:T(8,128)S(1)}, u32[]{:S(2)}, u32[]{:S(2)}) collective-permute-start(f32[32,8,128]{2,1,0:T(8,128)S(1)} %get-tuple-element.98), channel_id=1, source_target_pairs={{0,13},{1,12},{2,15},{3,14},{4,9},{5,8},{6,11},{7,10},{8,5},{9,4},... | collective-permute-start | bytes 393224 | tf_op jit(solution)/shard_map/ppermute | solution.py:264
  171.6 5.3 %collective-permute-done.57.refs_24_ = f32[32,8,128]{2,1,0:T(8,128)S(1)} collective-permute-done((f32[32,8,128]{2,1,0:T(8,128)S(1)}, f32[32,8,128]{2,1,0:T(8,128)S(1)}, u32[]{:S(2)}, u32[]{:S(2)}) %collective-permute-start.57) | collective-permute-done | bytes 131104 | tf_op jit(solution)/shard_map/ppermute | solution.py:264
  177.3 2.4 %collective-permute-done.59.refs_26_ = f32[32,8,128]{2,1,0:T(8,128)S(1)} collective-permute-done((f32[32,8,128]{2,1,0:T(8,128)S(1)}, f32[32,8,128]{2,1,0:T(8,128)S(1)}, u32[]{:S(2)}, u32[]{:S(2)}) %collective-permute-start.59) | collective-permute-done | bytes 131104 | tf_op jit(solution)/shard_map/ppermute | solution.py:264
  179.7 2.7 %partial_sums.1.refs_4_ = f32[32,256,128]{2,1,0:T(8,128)S(1)} custom-call(f32[2,256]{1,0:T(2,128)S(1)} %get-tuple-element.76.kinetics, bf16[256,224]{1,0:T(8,128)(2,1)S(1)} %get-tuple-element.101.high, bf16[256,224]{1,0:T(8,128)(2,1)S(1)} %get-tuple-element.102.low, f32[32,8,128]{2,1,0:T(8,128)S(1)} %collective-permute-done.34.refs_0_, ...), custom_call_target="tpu_custom_call" | custom-call | flops 805306368 | bytes 6291456 | tf_op jit(solution)/shard_map/partial_sums/pallas_call | solution.py:304
  182.4 5.0 %collective-permute-done.16.refs_1_ = f32[32,8,128]{2,1,0:T(8,128)S(1)} collective-permute-done((f32[32,8,128]{2,1,0:T(8,128)S(1)}, f32[32,8,128]{2,1,0:T(8,128)S(1)}, u32[]{:S(2)}, u32[]{:S(2)}) %collective-permute-start.16) | collective-permute-done | bytes 131104 | tf_op jit(solution)/shard_map/ppermute | solution.py:264
  187.5 2.8 %collective-permute-done.18.refs_3_ = f32[32,8,128]{2,1,0:T(8,128)S(1)} collective-permute-done((f32[32,8,128]{2,1,0:T(8,128)S(1)}, f32[32,8,128]{2,1,0:T(8,128)S(1)}, u32[]{:S(2)}, u32[]{:S(2)}) %collective-permute-start.18) | collective-permute-done | bytes 131104 | tf_op jit(solution)/shard_map/ppermute | solution.py:264
  190.3 2.5 %last_sweep.1 = f32[256,32,128]{2,1,0:T(8,128)} custom-call(f32[2,256]{1,0:T(2,128)S(1)} %get-tuple-element.76.kinetics, bf16[256,32]{1,0:T(8,128)(2,1)S(1)} %get-tuple-element.77.high, bf16[256,32]{1,0:T(8,128)(2,1)S(1)} %get-tuple-element.78.low, f32[32,8,128]{2,1,0:T(8,128)S(1)} %collective-permute-done.15.refs_0_, ...), custom_call_target="tpu_custom_call" | custom-call | flops 805306368 | bytes 6291456 | tf_op jit(solution)/shard_map/last_sweep/pallas_call | solution.py:316
  (97 shorter events, 21.7 us)
Async XLA Ops:
  11.0 11.6 %collective-permute-start.22 = (f32[32,8,128]{2,1,0:T(8,128)}, f32[32,8,128]{2,1,0:T(8,128)S(1)}, u32[]{:S(2)}, u32[]{:S(2)}) collective-permute-start(f32[32,8,128]{2,1,0:T(8,128)} %get-tuple-element.106), channel_id=1, source_target_pairs={{0,6},{1,7},{2,4},{3,5},{4,2},{5,3},{6,0},{7,1},{8,14},{9,15},{10,... | collective-permute-start | bytes 393224 | tf_op jit(solution)/shard_map/ppermute | solution.py:264
  11.6 13.9 %collective-permute-start.23 = (f32[32,8,128]{2,1,0:T(8,128)}, f32[32,8,128]{2,1,0:T(8,128)S(1)}, u32[]{:S(2)}, u32[]{:S(2)}) collective-permute-start(f32[32,8,128]{2,1,0:T(8,128)} %get-tuple-element.107), channel_id=1, source_target_pairs={{0,11},{1,10},{2,9},{3,8},{4,15},{5,14},{6,13},{7,12},{8,3},{9,2},... | collective-permute-start | bytes 393224 | tf_op jit(solution)/shard_map/ppermute | solution.py:264
  13.3 13.9 %collective-permute-start.24 = (f32[32,8,128]{2,1,0:T(8,128)}, f32[32,8,128]{2,1,0:T(8,128)S(1)}, u32[]{:S(2)}, u32[]{:S(2)}) collective-permute-start(f32[32,8,128]{2,1,0:T(8,128)} %get-tuple-element.108), channel_id=1, source_target_pairs={{0,5},{1,4},{2,7},{3,6},{4,1},{5,0},{6,3},{7,2},{8,13},{9,12},{10,... | collective-permute-start | bytes 393224 | tf_op jit(solution)/shard_map/ppermute | solution.py:264
  17.5 12.5 %collective-permute-start.25 = (f32[32,8,128]{2,1,0:T(8,128)}, f32[32,8,128]{2,1,0:T(8,128)S(1)}, u32[]{:S(2)}, u32[]{:S(2)}) collective-permute-start(f32[32,8,128]{2,1,0:T(8,128)} %get-tuple-element.109), channel_id=1, source_target_pairs={{0,10},{1,11},{2,8},{3,9},{4,14},{5,15},{6,12},{7,13},{8,2},{9,3},... | collective-permute-start | bytes 393224 | tf_op jit(solution)/shard_map/ppermute | solution.py:264
  19.3 18.6 %collective-permute-start.26 = (f32[32,8,128]{2,1,0:T(8,128)}, f32[32,8,128]{2,1,0:T(8,128)S(1)}, u32[]{:S(2)}, u32[]{:S(2)}) collective-permute-start(f32[32,8,128]{2,1,0:T(8,128)} %get-tuple-element.110), channel_id=1, source_target_pairs={{0,4},{1,5},{2,6},{3,7},{4,0},{5,1},{6,2},{7,3},{8,12},{9,13},{10,... | collective-permute-start | bytes 393224 | tf_op jit(solution)/shard_map/ppermute | solution.py:264
  22.6 20.6 %collective-permute-start.27 = (f32[32,8,128]{2,1,0:T(8,128)}, f32[32,8,128]{2,1,0:T(8,128)S(1)}, u32[]{:S(2)}, u32[]{:S(2)}) collective-permute-start(f32[32,8,128]{2,1,0:T(8,128)} %get-tuple-element.111), channel_id=1, source_target_pairs={{0,15},{1,14},{2,13},{3,12},{4,11},{5,10},{6,9},{7,8},{8,7},{9,6},... | collective-permute-start | bytes 393224 | tf_op jit(solution)/shard_map/ppermute | solution.py:264
  25.5 18.0 %collective-permute-start.28 = (f32[32,8,128]{2,1,0:T(8,128)}, f32[32,8,128]{2,1,0:T(8,128)S(1)}, u32[]{:S(2)}, u32[]{:S(2)}) collective-permute-start(f32[32,8,128]{2,1,0:T(8,128)} %get-tuple-element.112), channel_id=1, source_target_pairs={{0,3},{1,2},{2,1},{3,0},{4,7},{5,6},{6,5},{7,4},{8,11},{9,10},{10,... | collective-permute-start | bytes 393224 | tf_op jit(solution)/shard_map/ppermute | solution.py:264
  27.2 23.0 %collective-permute-start.29 = (f32[32,8,128]{2,1,0:T(8,128)}, f32[32,8,128]{2,1,0:T(8,128)S(1)}, u32[]{:S(2)}, u32[]{:S(2)}) collective-permute-start(f32[32,8,128]{2,1,0:T(8,128)} %get-tuple-element.113), channel_id=1, source_target_pairs={{0,14},{1,15},{2,12},{3,13},{4,10},{5,11},{6,8},{7,9},{8,6},{9,7},... | collective-permute-start | bytes 393224 | tf_op jit(solution)/shard_map/ppermute | solution.py:264
  30.0 20.3 %collective-permute-start.30 = (f32[32,8,128]{2,1,0:T(8,128)}, f32[32,8,128]{2,1,0:T(8,128)S(1)}, u32[]{:S(2)}, u32[]{:S(2)}) collective-permute-start(f32[32,8,128]{2,1,0:T(8,128)} %get-tuple-element.114), channel_id=1, source_target_pairs={{0,2},{1,3},{2,0},{3,1},{4,6},{5,7},{6,4},{7,5},{8,10},{9,11},{10,... | collective-permute-start | bytes 393224 | tf_op jit(solution)/shard_map/ppermute | solution.py:264
  37.9 14.3 %collective-permute-start.31 = (f32[32,8,128]{2,1,0:T(8,128)}, f32[32,8,128]{2,1,0:T(8,128)S(1)}, u32[]{:S(2)}, u32[]{:S(2)}) collective-permute-start(f32[32,8,128]{2,1,0:T(8,128)} %get-tuple-element.115), channel_id=1, source_target_pairs={{0,13},{1,12},{2,15},{3,14},{4,9},{5,8},{6,11},{7,10},{8,5},{9,4},... | collective-permute-start | bytes 393224 | tf_op jit(solution)/shard_map/ppermute | solution.py:264
  43.6 14.2 %collective-permute-start.33 = (f32[32,8,128]{2,1,0:T(8,128)}, f32[32,8,128]{2,1,0:T(8,128)S(1)}, u32[]{:S(2)}, u32[]{:S(2)}) collective-permute-start(f32[32,8,128]{2,1,0:T(8,128)} %get-tuple-element.117), channel_id=1, source_target_pairs={{0,12},{1,13},{2,14},{3,15},{4,8},{5,9},{6,10},{7,11},{8,4},{9,5},... | collective-permute-start | bytes 393224 | tf_op jit(solution)/shard_map/ppermute | solution.py:264
  50.3 14.8 %collective-permute-start.1 = (f32[32,8,128]{2,1,0:T(8,128)}, f32[32,8,128]{2,1,0:T(8,128)S(1)}, u32[]{:S(2)}, u32[]{:S(2)}) collective-permute-start(f32[32,8,128]{2,1,0:T(8,128)} %get-tuple-element.82), channel_id=1, source_target_pairs={{0,7},{1,6},{2,5},{3,4},{4,3},{5,2},{6,1},{7,0},{8,15},{9,14},{10,... | collective-permute-start | bytes 393224 | tf_op jit(solution)/shard_map/ppermute | solution.py:264
  52.2 13.1 %collective-permute-start.2 = (f32[32,8,128]{2,1,0:T(8,128)}, f32[32,8,128]{2,1,0:T(8,128)S(1)}, u32[]{:S(2)}, u32[]{:S(2)}) collective-permute-start(f32[32,8,128]{2,1,0:T(8,128)} %get-tuple-element.83), channel_id=1, source_target_pairs={{0,9},{1,8},{2,11},{3,10},{4,13},{5,12},{6,15},{7,14},{8,1},{9,0},... | collective-permute-start | bytes 393224 | tf_op jit(solution)/shard_map/ppermute | solution.py:264
  53.4 16.9 %collective-permute-start.3 = (f32[32,8,128]{2,1,0:T(8,128)}, f32[32,8,128]{2,1,0:T(8,128)S(1)}, u32[]{:S(2)}, u32[]{:S(2)}) collective-permute-start(f32[32,8,128]{2,1,0:T(8,128)} %get-tuple-element.84), channel_id=1, source_target_pairs={{0,6},{1,7},{2,4},{3,5},{4,2},{5,3},{6,0},{7,1},{8,14},{9,15},{10,... | collective-permute-start | bytes 393224 | tf_op jit(solution)/shard_map/ppermute | solution.py:264
  57.8 12.5 %collective-permute-start.4 = (f32[32,8,128]{2,1,0:T(8,128)}, f32[32,8,128]{2,1,0:T(8,128)S(1)}, u32[]{:S(2)}, u32[]{:S(2)}) collective-permute-start(f32[32,8,128]{2,1,0:T(8,128)} %get-tuple-element.85), channel_id=1, source_target_pairs={{0,11},{1,10},{2,9},{3,8},{4,15},{5,14},{6,13},{7,12},{8,3},{9,2},... | collective-permute-start | bytes 393224 | tf_op jit(solution)/shard_map/ppermute | solution.py:264
  58.7 18.1 %collective-permute-start.5 = (f32[32,8,128]{2,1,0:T(8,128)}, f32[32,8,128]{2,1,0:T(8,128)S(1)}, u32[]{:S(2)}, u32[]{:S(2)}) collective-permute-start(f32[32,8,128]{2,1,0:T(8,128)} %get-tuple-element.86), channel_id=1, source_target_pairs={{0,5},{1,4},{2,7},{3,6},{4,1},{5,0},{6,3},{7,2},{8,13},{9,12},{10,... | collective-permute-start | bytes 393224 | tf_op jit(solution)/shard_map/ppermute | solution.py:264
  65.1 12.9 %collective-permute-start.6 = (f32[32,8,128]{2,1,0:T(8,128)}, f32[32,8,128]{2,1,0:T(8,128)S(1)}, u32[]{:S(2)}, u32[]{:S(2)}) collective-permute-start(f32[32,8,128]{2,1,0:T(8,128)} %get-tuple-element.87), channel_id=1, source_target_pairs={{0,10},{1,11},{2,8},{3,9},{4,14},{5,15},{6,12},{7,13},{8,2},{9,3},... | collective-permute-start | bytes 393224 | tf_op jit(solution)/shard_map/ppermute | solution.py:264
  65.3 15.2 %collective-permute-start.7 = (f32[32,8,128]{2,1,0:T(8,128)}, f32[32,8,128]{2,1,0:T(8,128)S(1)}, u32[]{:S(2)}, u32[]{:S(2)}) collective-permute-start(f32[32,8,128]{2,1,0:T(8,128)} %get-tuple-element.88), channel_id=1, source_target_pairs={{0,4},{1,5},{2,6},{3,7},{4,0},{5,1},{6,2},{7,3},{8,12},{9,13},{10,... | collective-permute-start | bytes 393224 | tf_op jit(solution)/shard_map/ppermute | solution.py:264
  70.3 13.8 %collective-permute-start.8 = (f32[32,8,128]{2,1,0:T(8,128)}, f32[32,8,128]{2,1,0:T(8,128)S(1)}, u32[]{:S(2)}, u32[]{:S(2)}) collective-permute-start(f32[32,8,128]{2,1,0:T(8,128)} %get-tuple-element.89), channel_id=1, source_target_pairs={{0,15},{1,14},{2,13},{3,12},{4,11},{5,10},{6,9},{7,8},{8,7},{9,6},... | collective-permute-start | bytes 393224 | tf_op jit(solution)/shard_map/ppermute | solution.py:264
  70.3 14.3 %collective-permute-start.9 = (f32[32,8,128]{2,1,0:T(8,128)}, f32[32,8,128]{2,1,0:T(8,128)S(1)}, u32[]{:S(2)}, u32[]{:S(2)}) collective-permute-start(f32[32,8,128]{2,1,0:T(8,128)} %get-tuple-element.90), channel_id=1, source_target_pairs={{0,3},{1,2},{2,1},{3,0},{4,7},{5,6},{6,5},{7,4},{8,11},{9,10},{10,... | collective-permute-start | bytes 393224 | tf_op jit(solution)/shard_map/ppermute | solution.py:264
  76.8 18.5 %collective-permute-start.10 = (f32[32,8,128]{2,1,0:T(8,128)}, f32[32,8,128]{2,1,0:T(8,128)S(1)}, u32[]{:S(2)}, u32[]{:S(2)}) collective-permute-start(f32[32,8,128]{2,1,0:T(8,128)} %get-tuple-element.91), channel_id=1, source_target_pairs={{0,14},{1,15},{2,12},{3,13},{4,10},{5,11},{6,8},{7,9},{8,6},{9,7},... | collective-permute-start | bytes 393224 | tf_op jit(solution)/shard_map/ppermute | solution.py:264
  78.0 17.3 %collective-permute-start.11 = (f32[32,8,128]{2,1,0:T(8,128)}, f32[32,8,128]{2,1,0:T(8,128)S(1)}, u32[]{:S(2)}, u32[]{:S(2)}) collective-permute-start(f32[32,8,128]{2,1,0:T(8,128)} %get-tuple-element.92), channel_id=1, source_target_pairs={{0,2},{1,3},{2,0},{3,1},{4,6},{5,7},{6,4},{7,5},{8,10},{9,11},{10,... | collective-permute-start | bytes 393224 | tf_op jit(solution)/shard_map/ppermute | solution.py:264
  80.5 16.7 %collective-permute-start.12 = (f32[32,8,128]{2,1,0:T(8,128)}, f32[32,8,128]{2,1,0:T(8,128)S(1)}, u32[]{:S(2)}, u32[]{:S(2)}) collective-permute-start(f32[32,8,128]{2,1,0:T(8,128)} %get-tuple-element.93), channel_id=1, source_target_pairs={{0,13},{1,12},{2,15},{3,14},{4,9},{5,8},{6,11},{7,10},{8,5},{9,4},... | collective-permute-start | bytes 393224 | tf_op jit(solution)/shard_map/ppermute | solution.py:264
  84.1 14.4 %collective-permute-start.13 = (f32[32,8,128]{2,1,0:T(8,128)}, f32[32,8,128]{2,1,0:T(8,128)S(1)}, u32[]{:S(2)}, u32[]{:S(2)}) collective-permute-start(f32[32,8,128]{2,1,0:T(8,128)} %get-tuple-element.94), channel_id=1, source_target_pairs={{0,1},{1,0},{2,3},{3,2},{4,5},{5,4},{6,7},{7,6},{8,9},{9,8},{10,11... | collective-permute-start | bytes 393224 | tf_op jit(solution)/shard_map/ppermute | solution.py:264
  84.5 18.3 %collective-permute-start.14 = (f32[32,8,128]{2,1,0:T(8,128)}, f32[32,8,128]{2,1,0:T(8,128)S(1)}, u32[]{:S(2)}, u32[]{:S(2)}) collective-permute-start(f32[32,8,128]{2,1,0:T(8,128)} %get-tuple-element.95), channel_id=1, source_target_pairs={{0,12},{1,13},{2,14},{3,15},{4,8},{5,9},{6,10},{7,11},{8,4},{9,5},... | collective-permute-start | bytes 393224 | tf_op jit(solution)/shard_map/ppermute | solution.py:264
  95.3 14.8 %collective-permute-start.35 = (f32[32,8,128]{2,1,0:T(8,128)S(1)}, f32[32,8,128]{2,1,0:T(8,128)S(1)}, u32[]{:S(2)}, u32[]{:S(2)}) collective-permute-start(f32[32,8,128]{2,1,0:T(8,128)S(1)} %get-tuple-element.120), channel_id=1, source_target_pairs={{0,7},{1,6},{2,5},{3,4},{4,3},{5,2},{6,1},{7,0},{8,15},{9,14},{10,... | collective-permute-start | bytes 393224 | tf_op jit(solution)/shard_map/ppermute | solution.py:264
  97.3 13.0 %collective-permute-start.36 = (f32[32,8,128]{2,1,0:T(8,128)S(1)}, f32[32,8,128]{2,1,0:T(8,128)S(1)}, u32[]{:S(2)}, u32[]{:S(2)}) collective-permute-start(f32[32,8,128]{2,1,0:T(8,128)S(1)} %get-tuple-element.121), channel_id=1, source_target_pairs={{0,9},{1,8},{2,11},{3,10},{4,13},{5,12},{6,15},{7,14},{8,1},{9,0},... | collective-permute-start | bytes 393224 | tf_op jit(solution)/shard_map/ppermute | solution.py:264
  98.5 16.8 %collective-permute-start.37 = (f32[32,8,128]{2,1,0:T(8,128)S(1)}, f32[32,8,128]{2,1,0:T(8,128)S(1)}, u32[]{:S(2)}, u32[]{:S(2)}) collective-permute-start(f32[32,8,128]{2,1,0:T(8,128)S(1)} %get-tuple-element.122), channel_id=1, source_target_pairs={{0,6},{1,7},{2,4},{3,5},{4,2},{5,3},{6,0},{7,1},{8,14},{9,15},{10,... | collective-permute-start | bytes 393224 | tf_op jit(solution)/shard_map/ppermute | solution.py:264
  102.9 12.4 %collective-permute-start.38 = (f32[32,8,128]{2,1,0:T(8,128)S(1)}, f32[32,8,128]{2,1,0:T(8,128)S(1)}, u32[]{:S(2)}, u32[]{:S(2)}) collective-permute-start(f32[32,8,128]{2,1,0:T(8,128)S(1)} %get-tuple-element.123), channel_id=1, source_target_pairs={{0,11},{1,10},{2,9},{3,8},{4,15},{5,14},{6,13},{7,12},{8,3},{9,2},... | collective-permute-start | bytes 393224 | tf_op jit(solution)/shard_map/ppermute | solution.py:264
  102.9 16.4 %collective-permute-start.39 = (f32[32,8,128]{2,1,0:T(8,128)S(1)}, f32[32,8,128]{2,1,0:T(8,128)S(1)}, u32[]{:S(2)}, u32[]{:S(2)}) collective-permute-start(f32[32,8,128]{2,1,0:T(8,128)S(1)} %get-tuple-element.124), channel_id=1, source_target_pairs={{0,5},{1,4},{2,7},{3,6},{4,1},{5,0},{6,3},{7,2},{8,13},{9,12},{10,... | collective-permute-start | bytes 393224 | tf_op jit(solution)/shard_map/ppermute | solution.py:264
  110.3 14.7 %collective-permute-start.41 = (f32[32,8,128]{2,1,0:T(8,128)S(1)}, f32[32,8,128]{2,1,0:T(8,128)S(1)}, u32[]{:S(2)}, u32[]{:S(2)}) collective-permute-start(f32[32,8,128]{2,1,0:T(8,128)S(1)} %get-tuple-element.126), channel_id=1, source_target_pairs={{0,4},{1,5},{2,6},{3,7},{4,0},{5,1},{6,2},{7,3},{8,12},{9,13},{10,... | collective-permute-start | bytes 393224 | tf_op jit(solution)/shard_map/ppermute | solution.py:264
  115.3 16.6 %collective-permute-start.42 = (f32[32,8,128]{2,1,0:T(8,128)S(1)}, f32[32,8,128]{2,1,0:T(8,128)S(1)}, u32[]{:S(2)}, u32[]{:S(2)}) collective-permute-start(f32[32,8,128]{2,1,0:T(8,128)S(1)} %get-tuple-element.127), channel_id=1, source_target_pairs={{0,15},{1,14},{2,13},{3,12},{4,11},{5,10},{6,9},{7,8},{8,7},{9,6},... | collective-permute-start | bytes 393224 | tf_op jit(solution)/shard_map/ppermute | solution.py:264
  115.3 17.0 %collective-permute-start.43 = (f32[32,8,128]{2,1,0:T(8,128)S(1)}, f32[32,8,128]{2,1,0:T(8,128)S(1)}, u32[]{:S(2)}, u32[]{:S(2)}) collective-permute-start(f32[32,8,128]{2,1,0:T(8,128)S(1)} %get-tuple-element.128), channel_id=1, source_target_pairs={{0,3},{1,2},{2,1},{3,0},{4,7},{5,6},{6,5},{7,4},{8,11},{9,10},{10,... | collective-permute-start | bytes 393224 | tf_op jit(solution)/shard_map/ppermute | solution.py:264
  119.3 20.3 %collective-permute-start.44 = (f32[32,8,128]{2,1,0:T(8,128)S(1)}, f32[32,8,128]{2,1,0:T(8,128)S(1)}, u32[]{:S(2)}, u32[]{:S(2)}) collective-permute-start(f32[32,8,128]{2,1,0:T(8,128)S(1)} %get-tuple-element.129), channel_id=1, source_target_pairs={{0,14},{1,15},{2,12},{3,13},{4,10},{5,11},{6,8},{7,9},{8,6},{9,7},... | collective-permute-start | bytes 393224 | tf_op jit(solution)/shard_map/ppermute | solution.py:264
  120.5 22.1 %collective-permute-start.45 = (f32[32,8,128]{2,1,0:T(8,128)S(1)}, f32[32,8,128]{2,1,0:T(8,128)S(1)}, u32[]{:S(2)}, u32[]{:S(2)}) collective-permute-start(f32[32,8,128]{2,1,0:T(8,128)S(1)} %get-tuple-element.130), channel_id=1, source_target_pairs={{0,2},{1,3},{2,0},{3,1},{4,6},{5,7},{6,4},{7,5},{8,10},{9,11},{10,... | collective-permute-start | bytes 393224 | tf_op jit(solution)/shard_map/ppermute | solution.py:264
  125.0 19.2 %collective-permute-start.46 = (f32[32,8,128]{2,1,0:T(8,128)S(1)}, f32[32,8,128]{2,1,0:T(8,128)S(1)}, u32[]{:S(2)}, u32[]{:S(2)}) collective-permute-start(f32[32,8,128]{2,1,0:T(8,128)S(1)} %get-tuple-element.131), channel_id=1, source_target_pairs={{0,13},{1,12},{2,15},{3,14},{4,9},{5,8},{6,11},{7,10},{8,5},{9,4},... | collective-permute-start | bytes 393224 | tf_op jit(solution)/shard_map/ppermute | solution.py:264
  131.9 14.2 %collective-permute-start.47 = (f32[32,8,128]{2,1,0:T(8,128)S(1)}, f32[32,8,128]{2,1,0:T(8,128)S(1)}, u32[]{:S(2)}, u32[]{:S(2)}) collective-permute-start(f32[32,8,128]{2,1,0:T(8,128)S(1)} %get-tuple-element.132), channel_id=1, source_target_pairs={{0,1},{1,0},{2,3},{3,2},{4,5},{5,4},{6,7},{7,6},{8,9},{9,8},{10,11... | collective-permute-start | bytes 393224 | tf_op jit(solution)/shard_map/ppermute | solution.py:264
  132.3 15.6 %collective-permute-start.48 = (f32[32,8,128]{2,1,0:T(8,128)S(1)}, f32[32,8,128]{2,1,0:T(8,128)S(1)}, u32[]{:S(2)}, u32[]{:S(2)}) collective-permute-start(f32[32,8,128]{2,1,0:T(8,128)S(1)} %get-tuple-element.133), channel_id=1, source_target_pairs={{0,12},{1,13},{2,14},{3,15},{4,8},{5,9},{6,10},{7,11},{8,4},{9,5},... | collective-permute-start | bytes 393224 | tf_op jit(solution)/shard_map/ppermute | solution.py:264
  142.7 12.6 %collective-permute-start.50 = (f32[32,8,128]{2,1,0:T(8,128)S(1)}, f32[32,8,128]{2,1,0:T(8,128)S(1)}, u32[]{:S(2)}, u32[]{:S(2)}) collective-permute-start(f32[32,8,128]{2,1,0:T(8,128)S(1)} %get-tuple-element.136), channel_id=1, source_target_pairs={{0,7},{1,6},{2,5},{3,4},{4,3},{5,2},{6,1},{7,0},{8,15},{9,14},{10,... | collective-permute-start | bytes 393224 | tf_op jit(solution)/shard_map/ppermute | solution.py:264
  146.1 14.3 %collective-permute-start.52 = (f32[32,8,128]{2,1,0:T(8,128)S(1)}, f32[32,8,128]{2,1,0:T(8,128)S(1)}, u32[]{:S(2)}, u32[]{:S(2)}) collective-permute-start(f32[32,8,128]{2,1,0:T(8,128)S(1)} %get-tuple-element.138), channel_id=1, source_target_pairs={{0,6},{1,7},{2,4},{3,5},{4,2},{5,3},{6,0},{7,1},{8,14},{9,15},{10,... | collective-permute-start | bytes 393224 | tf_op jit(solution)/shard_map/ppermute | solution.py:264
  147.9 12.5 %collective-permute-start.53 = (f32[32,8,128]{2,1,0:T(8,128)S(1)}, f32[32,8,128]{2,1,0:T(8,128)S(1)}, u32[]{:S(2)}, u32[]{:S(2)}) collective-permute-start(f32[32,8,128]{2,1,0:T(8,128)S(1)} %get-tuple-element.139), channel_id=1, source_target_pairs={{0,11},{1,10},{2,9},{3,8},{4,15},{5,14},{6,13},{7,12},{8,3},{9,2},... | collective-permute-start | bytes 393224 | tf_op jit(solution)/shard_map/ppermute | solution.py:264
  148.9 13.3 %collective-permute-start.54 = (f32[32,8,128]{2,1,0:T(8,128)S(1)}, f32[32,8,128]{2,1,0:T(8,128)S(1)}, u32[]{:S(2)}, u32[]{:S(2)}) collective-permute-start(f32[32,8,128]{2,1,0:T(8,128)S(1)} %get-tuple-element.140), channel_id=1, source_target_pairs={{0,5},{1,4},{2,7},{3,6},{4,1},{5,0},{6,3},{7,2},{8,13},{9,12},{10,... | collective-permute-start | bytes 393224 | tf_op jit(solution)/shard_map/ppermute | solution.py:264
  160.4 16.5 %collective-permute-start.57 = (f32[32,8,128]{2,1,0:T(8,128)S(1)}, f32[32,8,128]{2,1,0:T(8,128)S(1)}, u32[]{:S(2)}, u32[]{:S(2)}) collective-permute-start(f32[32,8,128]{2,1,0:T(8,128)S(1)} %get-tuple-element.143), channel_id=1, source_target_pairs={{0,15},{1,14},{2,13},{3,12},{4,11},{5,10},{6,9},{7,8},{8,7},{9,6},... | collective-permute-start | bytes 393224 | tf_op jit(solution)/shard_map/ppermute | solution.py:264
  160.4 16.9 %collective-permute-start.58 = (f32[32,8,128]{2,1,0:T(8,128)S(1)}, f32[32,8,128]{2,1,0:T(8,128)S(1)}, u32[]{:S(2)}, u32[]{:S(2)}) collective-permute-start(f32[32,8,128]{2,1,0:T(8,128)S(1)} %get-tuple-element.144), channel_id=1, source_target_pairs={{0,3},{1,2},{2,1},{3,0},{4,7},{5,6},{6,5},{7,4},{8,11},{9,10},{10,... | collective-permute-start | bytes 393224 | tf_op jit(solution)/shard_map/ppermute | solution.py:264
  162.2 17.5 %collective-permute-start.59 = (f32[32,8,128]{2,1,0:T(8,128)S(1)}, f32[32,8,128]{2,1,0:T(8,128)S(1)}, u32[]{:S(2)}, u32[]{:S(2)}) collective-permute-start(f32[32,8,128]{2,1,0:T(8,128)S(1)} %get-tuple-element.145), channel_id=1, source_target_pairs={{0,14},{1,15},{2,12},{3,13},{4,10},{5,11},{6,8},{7,9},{8,6},{9,7},... | collective-permute-start | bytes 393224 | tf_op jit(solution)/shard_map/ppermute | solution.py:264
  165.5 16.9 %collective-permute-start.15 = (f32[32,8,128]{2,1,0:T(8,128)S(1)}, f32[32,8,128]{2,1,0:T(8,128)S(1)}, u32[]{:S(2)}, u32[]{:S(2)}) collective-permute-start(f32[32,8,128]{2,1,0:T(8,128)S(1)} %get-tuple-element.97), channel_id=1, source_target_pairs={{0,2},{1,3},{2,0},{3,1},{4,6},{5,7},{6,4},{7,5},{8,10},{9,11},{10,... | collective-permute-start | bytes 393224 | tf_op jit(solution)/shard_map/ppermute | solution.py:264
  166.8 20.6 %collective-permute-start.16 = (f32[32,8,128]{2,1,0:T(8,128)S(1)}, f32[32,8,128]{2,1,0:T(8,128)S(1)}, u32[]{:S(2)}, u32[]{:S(2)}) collective-permute-start(f32[32,8,128]{2,1,0:T(8,128)S(1)} %get-tuple-element.98), channel_id=1, source_target_pairs={{0,13},{1,12},{2,15},{3,14},{4,9},{5,8},{6,11},{7,10},{8,5},{9,4},... | collective-permute-start | bytes 393224 | tf_op jit(solution)/shard_map/ppermute | solution.py:264
  177.3 13.0 %collective-permute-start.18 = (f32[32,8,128]{2,1,0:T(8,128)S(1)}, f32[32,8,128]{2,1,0:T(8,128)S(1)}, u32[]{:S(2)}, u32[]{:S(2)}) collective-permute-start(f32[32,8,128]{2,1,0:T(8,128)S(1)} %get-tuple-element.100), channel_id=1, source_target_pairs={{0,12},{1,13},{2,14},{3,15},{4,8},{5,9},{6,10},{7,11},{8,4},{9,5},... | collective-permute-start | bytes 393224 | tf_op jit(solution)/shard_map/ppermute | solution.py:264
  (21 other events, 760.3 us)

commit v5 on v4

--- a/solution.py
+++ b/solution.py
@@ -13,7 +13,7 @@
 VMEM_LIMIT = 24 * 1024 * 1024
 FIRST_LIMIT = 60 * 1024 * 1024
 GRAIN = 16
-OUT_GRAIN = 4
+OUT_GRAIN = 2
 LATE = 4
 
 

time: 193 us -> 193 us (level)
  no operation moved by 1% of the time
where the time goes in v5:
time: 193 us
  starting transfers between devices  107 us (55%)
  waiting for transfers between devices  51.9 us (27%)
  Pallas kernels  32.9 us (17%)
    ppermute x60, starting transfers between devices, exchange(): lax.ppermute(block, ('row', 'col'), [(i, i ^ place) for i in range(ranks)])  107 us
    ppermute x60, waiting for transfers between devices, exchange(): lax.ppermute(block, ('row', 'col'), [(i, i ^ place) for i in range(ranks)])  51.9 us
    pallas_call x2, Pallas kernels, planes(): pl.pallas_call(functools.partial(plane_sweeps, columns, ranks), grid=(1,)...  14.7 us
    pallas_call x2, Pallas kernels, first(): pl.pallas_call(functools.partial(first_sweep, chunk, columns), grid=(1,),...  10.6 us
  transfers between devices with their start and end apart: 60, of which 19 were waited for; matrix products, arithmetic and copies ran while one was open for 0% of the time, Pallas kernels for 13%

profile of v5, /device:TPU:17, one launch (start us, length us, event | category | flops | bytes accessed | tf_op | source)
XLA Modules:
  0.0 193.0 jit_solution(13794442082587368162)
XLA Ops:
  0.7 5.4 %first_sweep_0.1 = (f32[32,8,128]{2,1,0:T(8,128)}, f32[32,8,128]{2,1,0:T(8,128)}, f32[32,8,128]{2,1,0:T(8,128)}, f32[32,8,128]{2,1,0:T(8,128)}, f32[32,8,128]{2,...) custom-call(s32[1]{0:T(128)S(6)} %copy.10.species, ...), custom_call_target="tpu_custom_call" | custom-call | flops 805306368 | bytes 6291456 | tf_op jit(solution)/shard_map/first_sweep_0/pallas_call | solution.py:272
  6.2 3.1 %collective-permute-start.20 = (f32[32,8,128]{2,1,0:T(8,128)}, f32[32,8,128]{2,1,0:T(8,128)S(1)}, u32[]{:S(2)}, u32[]{:S(2)}) collective-permute-start(f32[32,8,128]{2,1,0:T(8,128)} %get-tuple-element.104), channel_id=1, source_target_pairs={{0,7},{1,6},{2,5},{3,4},{4,3},{5,2},{6,1},{7,0},{8,15},{9,14},{10,... | collective-permute-start | bytes 393224 | tf_op jit(solution)/shard_map/ppermute | solution.py:264
  9.3 1.7 collective-permute-start.21
  11.6 1.7 collective-permute-start.23
  13.3 4.2 %collective-permute-start.24 = (f32[32,8,128]{2,1,0:T(8,128)}, f32[32,8,128]{2,1,0:T(8,128)S(1)}, u32[]{:S(2)}, u32[]{:S(2)}) collective-permute-start(f32[32,8,128]{2,1,0:T(8,128)} %get-tuple-element.108), channel_id=1, source_target_pairs={{0,5},{1,4},{2,7},{3,6},{4,1},{5,0},{6,3},{7,2},{8,13},{9,12},{10,... | collective-permute-start | bytes 393224 | tf_op jit(solution)/shard_map/ppermute | solution.py:264
  17.5 1.8 collective-permute-start.25
  19.3 3.3 %collective-permute-start.26 = (f32[32,8,128]{2,1,0:T(8,128)}, f32[32,8,128]{2,1,0:T(8,128)S(1)}, u32[]{:S(2)}, u32[]{:S(2)}) collective-permute-start(f32[32,8,128]{2,1,0:T(8,128)} %get-tuple-element.110), channel_id=1, source_target_pairs={{0,4},{1,5},{2,6},{3,7},{4,0},{5,1},{6,2},{7,3},{8,12},{9,13},{10,... | collective-permute-start | bytes 393224 | tf_op jit(solution)/shard_map/ppermute | solution.py:264
  22.9 2.6 %collective-permute-done.23.refs_4_ = f32[32,8,128]{2,1,0:T(8,128)S(1)} collective-permute-done((f32[32,8,128]{2,1,0:T(8,128)}, f32[32,8,128]{2,1,0:T(8,128)S(1)}, u32[]{:S(2)}, u32[]{:S(2)}) %collective-permute-start.23) | collective-permute-done | bytes 131104 | tf_op jit(solution)/shard_map/ppermute | solution.py:264
  25.5 1.7 collective-permute-start.28
  27.2 1.7 collective-permute-start.29
  31.0 6.9 %collective-permute-done.26.refs_7_ = f32[32,8,128]{2,1,0:T(8,128)S(1)} collective-permute-done((f32[32,8,128]{2,1,0:T(8,128)}, f32[32,8,128]{2,1,0:T(8,128)S(1)}, u32[]{:S(2)}, u32[]{:S(2)}) %collective-permute-start.26) | collective-permute-done | bytes 131104 | tf_op jit(solution)/shard_map/ppermute | solution.py:264
  37.9 5.2 %collective-permute-done.27.refs_8_ = f32[32,8,128]{2,1,0:T(8,128)S(1)} collective-permute-done((f32[32,8,128]{2,1,0:T(8,128)}, f32[32,8,128]{2,1,0:T(8,128)S(1)}, u32[]{:S(2)}, u32[]{:S(2)}) %collective-permute-start.27) | collective-permute-done | bytes 131104 | tf_op jit(solution)/shard_map/ppermute | solution.py:264
  43.6 5.2 %first_sweep_1.1 = (f32[32,8,128]{2,1,0:T(8,128)}, f32[32,8,128]{2,1,0:T(8,128)}, f32[32,8,128]{2,1,0:T(8,128)}, f32[32,8,128]{2,1,0:T(8,128)}, f32[32,8,128]{2,...) custom-call(s32[1]{0:T(128)S(6)} %copy.10.species, ...), custom_call_target="tpu_custom_call" | custom-call | flops 805306368 | bytes 6291456 | tf_op jit(solution)/shard_map/first_sweep_1/pallas_call | solution.py:272
  48.8 1.4 collective-permute-done.29.refs_10_
  53.4 3.4 %collective-permute-start.3 = (f32[32,8,128]{2,1,0:T(8,128)}, f32[32,8,128]{2,1,0:T(8,128)S(1)}, u32[]{:S(2)}, u32[]{:S(2)}) collective-permute-start(f32[32,8,128]{2,1,0:T(8,128)} %get-tuple-element.84), channel_id=1, source_target_pairs={{0,6},{1,7},{2,4},{3,5},{4,2},{5,3},{6,0},{7,1},{8,14},{9,15},{10,... | collective-permute-start | bytes 393224 | tf_op jit(solution)/shard_map/ppermute | solution.py:264
  58.7 6.4 %collective-permute-start.5 = (f32[32,8,128]{2,1,0:T(8,128)}, f32[32,8,128]{2,1,0:T(8,128)S(1)}, u32[]{:S(2)}, u32[]{:S(2)}) collective-permute-start(f32[32,8,128]{2,1,0:T(8,128)} %get-tuple-element.86), channel_id=1, source_target_pairs={{0,5},{1,4},{2,7},{3,6},{4,1},{5,0},{6,3},{7,2},{8,13},{9,12},{10,... | collective-permute-start | bytes 393224 | tf_op jit(solution)/shard_map/ppermute | solution.py:264
  65.3 4.9 %collective-permute-start.7 = (f32[32,8,128]{2,1,0:T(8,128)}, f32[32,8,128]{2,1,0:T(8,128)S(1)}, u32[]{:S(2)}, u32[]{:S(2)}) collective-permute-start(f32[32,8,128]{2,1,0:T(8,128)} %get-tuple-element.88), channel_id=1, source_target_pairs={{0,4},{1,5},{2,6},{3,7},{4,0},{5,1},{6,2},{7,3},{8,12},{9,13},{10,... | collective-permute-start | bytes 393224 | tf_op jit(solution)/shard_map/ppermute | solution.py:264
  70.3 4.1 %collective-permute-start.9 = (f32[32,8,128]{2,1,0:T(8,128)}, f32[32,8,128]{2,1,0:T(8,128)S(1)}, u32[]{:S(2)}, u32[]{:S(2)}) collective-permute-start(f32[32,8,128]{2,1,0:T(8,128)} %get-tuple-element.90), channel_id=1, source_target_pairs={{0,3},{1,2},{2,1},{3,0},{4,7},{5,6},{6,5},{7,4},{8,11},{9,10},{10,... | collective-permute-start | bytes 393224 | tf_op jit(solution)/shard_map/ppermute | solution.py:264
  74.5 2.3 %prepare.1 = (f32[2,256]{1,0:T(2,128)S(1)}, bf16[4,256,256]{2,1,0:T(8,128)(2,1)S(1)}, bf16[4,256,256]{2,1,0:T(8,128)(2,1)S(1)}, bf16[256,224]{1,0:T(8,128)(2,1)S...) custom-call(s32[1]{0:T(128)S(6)} %copy.10.species, f32[64]{0:T(128)S(1)} %copy-done.3, ...), custom_call_target="tpu_custom_call" | custom-call | flops 805306368 | bytes 2097152 | tf_op jit(solution)/shard_map/prepare/pallas_call | solution.py:338
  78.0 1.4 collective-permute-start.11
  81.6 2.4 %collective-permute-done.8.refs_8_ = f32[32,8,128]{2,1,0:T(8,128)S(1)} collective-permute-done((f32[32,8,128]{2,1,0:T(8,128)}, f32[32,8,128]{2,1,0:T(8,128)S(1)}, u32[]{:S(2)}, u32[]{:S(2)}) %collective-permute-start.8) | collective-permute-done | bytes 131104 | tf_op jit(solution)/shard_map/ppermute | solution.py:264
  84.5 2.4 %collective-permute-start.14 = (f32[32,8,128]{2,1,0:T(8,128)}, f32[32,8,128]{2,1,0:T(8,128)S(1)}, u32[]{:S(2)}, u32[]{:S(2)}) collective-permute-start(f32[32,8,128]{2,1,0:T(8,128)} %get-tuple-element.95), channel_id=1, source_target_pairs={{0,12},{1,13},{2,14},{3,15},{4,8},{5,9},{6,10},{7,11},{8,4},{9,5},... | collective-permute-start | bytes 393224 | tf_op jit(solution)/shard_map/ppermute | solution.py:264
  86.9 7.4 %plane_sweeps_0.1 = (f32[32,8,128]{2,1,0:T(8,128)S(1)}, f32[32,8,128]{2,1,0:T(8,128)S(1)}, f32[32,8,128]{2,1,0:T(8,128)S(1)}, f32[32,8,128]{2,1,0:T(8,128)S(1)},...) custom-call(f32[2,256]{1,0:T(2,128)S(1)} %get-tuple-element.76.kinet, ...), custom_call_target="tpu_custom_call" | custom-call | flops 3221225472 | bytes 4194304 | tf_op jit(solution)/shard_map/plane_sweeps_0/pallas_call | solution.py:290
  95.3 1.5 collective-permute-start.35
  98.5 1.8 collective-permute-start.37
  100.3 2.5 %collective-permute-done.14.refs_14_ = f32[32,8,128]{2,1,0:T(8,128)S(1)} collective-permute-done((f32[32,8,128]{2,1,0:T(8,128)}, f32[32,8,128]{2,1,0:T(8,128)S(1)}, u32[]{:S(2)}, u32[]{:S(2)}) %collective-permute-start.14) | collective-permute-done | bytes 131104 | tf_op jit(solution)/shard_map/ppermute | solution.py:264
  102.9 7.3 %collective-permute-start.39 = (f32[32,8,128]{2,1,0:T(8,128)S(1)}, f32[32,8,128]{2,1,0:T(8,128)S(1)}, u32[]{:S(2)}, u32[]{:S(2)}) collective-permute-start(f32[32,8,128]{2,1,0:T(8,128)S(1)} %get-tuple-element.124), channel_id=1, source_target_pairs={{0,5},{1,4},{2,7},{3,6},{4,1},{5,0},{6,3},{7,2},{8,13},{9,12},{10,... | collective-permute-start | bytes 393224 | tf_op jit(solution)/shard_map/ppermute | solution.py:264
  110.3 5.0 %collective-permute-start.41 = (f32[32,8,128]{2,1,0:T(8,128)S(1)}, f32[32,8,128]{2,1,0:T(8,128)S(1)}, u32[]{:S(2)}, u32[]{:S(2)}) collective-permute-start(f32[32,8,128]{2,1,0:T(8,128)S(1)} %get-tuple-element.126), channel_id=1, source_target_pairs={{0,4},{1,5},{2,6},{3,7},{4,0},{5,1},{6,2},{7,3},{8,12},{9,13},{10,... | collective-permute-start | bytes 393224 | tf_op jit(solution)/shard_map/ppermute | solution.py:264
  115.3 4.0 %collective-permute-start.43 = (f32[32,8,128]{2,1,0:T(8,128)S(1)}, f32[32,8,128]{2,1,0:T(8,128)S(1)}, u32[]{:S(2)}, u32[]{:S(2)}) collective-permute-start(f32[32,8,128]{2,1,0:T(8,128)S(1)} %get-tuple-element.128), channel_id=1, source_target_pairs={{0,3},{1,2},{2,1},{3,0},{4,7},{5,6},{6,5},{7,4},{8,11},{9,10},{10,... | collective-permute-start | bytes 393224 | tf_op jit(solution)/shard_map/ppermute | solution.py:264
  121.8 3.1 %collective-permute-done.41.refs_7_ = f32[32,8,128]{2,1,0:T(8,128)S(1)} collective-permute-done((f32[32,8,128]{2,1,0:T(8,128)S(1)}, f32[32,8,128]{2,1,0:T(8,128)S(1)}, u32[]{:S(2)}, u32[]{:S(2)}) %collective-permute-start.41) | collective-permute-done | bytes 131104 | tf_op jit(solution)/shard_map/ppermute | solution.py:264
  125.0 1.6 collective-permute-start.46
  126.6 5.3 %collective-permute-done.42.refs_8_ = f32[32,8,128]{2,1,0:T(8,128)S(1)} collective-permute-done((f32[32,8,128]{2,1,0:T(8,128)S(1)}, f32[32,8,128]{2,1,0:T(8,128)S(1)}, u32[]{:S(2)}, u32[]{:S(2)}) %collective-permute-start.42) | collective-permute-done | bytes 131104 | tf_op jit(solution)/shard_map/ppermute | solution.py:264
  132.3 7.3 %plane_sweeps_1.1 = (f32[32,8,128]{2,1,0:T(8,128)S(1)}, f32[32,8,128]{2,1,0:T(8,128)S(1)}, f32[32,8,128]{2,1,0:T(8,128)S(1)}, f32[32,8,128]{2,1,0:T(8,128)S(1)},...) custom-call(f32[2,256]{1,0:T(2,128)S(1)} %get-tuple-element.76.kinet, ...), custom_call_target="tpu_custom_call" | custom-call | flops 3221225472 | bytes 4194304 | tf_op jit(solution)/shard_map/plane_sweeps_1/pallas_call | solution.py:290
  139.6 3.1 %collective-permute-start.49 = (f32[32,8,128]{2,1,0:T(8,128)S(1)}, f32[32,8,128]{2,1,0:T(8,128)S(1)}, u32[]{:S(2)}, u32[]{:S(2)}) collective-permute-start(f32[32,8,128]{2,1,0:T(8,128)S(1)} %get-tuple-element.135), channel_id=1, source_target_pairs={{0,8},{1,9},{2,10},{3,11},{4,12},{5,13},{6,14},{7,15},{8,0},{9,1},... | collective-permute-start | bytes 393224 | tf_op jit(solution)/shard_map/ppermute | solution.py:264
  142.7 1.4 collective-permute-start.50
  144.1 2.0 %collective-permute-start.51 = (f32[32,8,128]{2,1,0:T(8,128)S(1)}, f32[32,8,128]{2,1,0:T(8,128)S(1)}, u32[]{:S(2)}, u32[]{:S(2)}) collective-permute-start(f32[32,8,128]{2,1,0:T(8,128)S(1)} %get-tuple-element.137), channel_id=1, source_target_pairs={{0,9},{1,8},{2,11},{3,10},{4,13},{5,12},{6,15},{7,14},{8,1},{9,0},... | collective-permute-start | bytes 393224 | tf_op jit(solution)/shard_map/ppermute | solution.py:264
  148.9 6.5 %collective-permute-start.54 = (f32[32,8,128]{2,1,0:T(8,128)S(1)}, f32[32,8,128]{2,1,0:T(8,128)S(1)}, u32[]{:S(2)}, u32[]{:S(2)}) collective-permute-start(f32[32,8,128]{2,1,0:T(8,128)S(1)} %get-tuple-element.140), channel_id=1, source_target_pairs={{0,5},{1,4},{2,7},{3,6},{4,1},{5,0},{6,3},{7,2},{8,13},{9,12},{10,... | collective-permute-start | bytes 393224 | tf_op jit(solution)/shard_map/ppermute | solution.py:264
  155.4 5.1 %collective-permute-start.56 = (f32[32,8,128]{2,1,0:T(8,128)S(1)}, f32[32,8,128]{2,1,0:T(8,128)S(1)}, u32[]{:S(2)}, u32[]{:S(2)}) collective-permute-start(f32[32,8,128]{2,1,0:T(8,128)S(1)} %get-tuple-element.142), channel_id=1, source_target_pairs={{0,4},{1,5},{2,6},{3,7},{4,0},{5,1},{6,2},{7,3},{8,12},{9,13},{10,... | collective-permute-start | bytes 393224 | tf_op jit(solution)/shard_map/ppermute | solution.py:264
  160.4 1.8 collective-permute-start.58
  162.2 3.3 %collective-permute-start.59 = (f32[32,8,128]{2,1,0:T(8,128)S(1)}, f32[32,8,128]{2,1,0:T(8,128)S(1)}, u32[]{:S(2)}, u32[]{:S(2)}) collective-permute-start(f32[32,8,128]{2,1,0:T(8,128)S(1)} %get-tuple-element.145), channel_id=1, source_target_pairs={{0,14},{1,15},{2,12},{3,13},{4,10},{5,11},{6,8},{7,9},{8,6},{9,7},... | collective-permute-start | bytes 393224 | tf_op jit(solution)/shard_map/ppermute | solution.py:264
  165.5 1.3 collective-permute-start.15
  166.8 4.8 %collective-permute-start.16 = (f32[32,8,128]{2,1,0:T(8,128)S(1)}, f32[32,8,128]{2,1,0:T(8,128)S(1)}, u32[]{:S(2)}, u32[]{:S(2)}) collective-permute-start(f32[32,8,128]{2,1,0:T(8,128)S(1)} %get-tuple-element.98), channel_id=1, source_target_pairs={{0,13},{1,12},{2,15},{3,14},{4,9},{5,8},{6,11},{7,10},{8,5},{9,4},... | collective-permute-start | bytes 393224 | tf_op jit(solution)/shard_map/ppermute | solution.py:264
  171.6 5.3 %collective-permute-done.57.refs_24_ = f32[32,8,128]{2,1,0:T(8,128)S(1)} collective-permute-done((f32[32,8,128]{2,1,0:T(8,128)S(1)}, f32[32,8,128]{2,1,0:T(8,128)S(1)}, u32[]{:S(2)}, u32[]{:S(2)}) %collective-permute-start.57) | collective-permute-done | bytes 131104 | tf_op jit(solution)/shard_map/ppermute | solution.py:264
  177.3 2.4 %collective-permute-done.59.refs_26_ = f32[32,8,128]{2,1,0:T(8,128)S(1)} collective-permute-done((f32[32,8,128]{2,1,0:T(8,128)S(1)}, f32[32,8,128]{2,1,0:T(8,128)S(1)}, u32[]{:S(2)}, u32[]{:S(2)}) %collective-permute-start.59) | collective-permute-done | bytes 131104 | tf_op jit(solution)/shard_map/ppermute | solution.py:264
  179.7 2.7 %partial_sums.1.refs_4_ = f32[32,256,128]{2,1,0:T(8,128)S(1)} custom-call(f32[2,256]{1,0:T(2,128)S(1)} %get-tuple-element.76.kinetics, bf16[256,224]{1,0:T(8,128)(2,1)S(1)} %get-tuple-element.101.high, bf16[256,224]{1,0:T(8,128)(2,1)S(1)} %get-tuple-element.102.low, f32[32,8,128]{2,1,0:T(8,128)S(1)} %collective-permute-done.34.refs_0_, ...), custom_call_target="tpu_custom_call" | custom-call | flops 805306368 | bytes 6291456 | tf_op jit(solution)/shard_map/partial_sums/pallas_call | solution.py:304
  182.4 5.0 %collective-permute-done.16.refs_1_ = f32[32,8,128]{2,1,0:T(8,128)S(1)} collective-permute-done((f32[32,8,128]{2,1,0:T(8,128)S(1)}, f32[32,8,128]{2,1,0:T(8,128)S(1)}, u32[]{:S(2)}, u32[]{:S(2)}) %collective-permute-start.16) | collective-permute-done | bytes 131104 | tf_op jit(solution)/shard_map/ppermute | solution.py:264
  187.5 2.8 %collective-permute-done.18.refs_3_ = f32[32,8,128]{2,1,0:T(8,128)S(1)} collective-permute-done((f32[32,8,128]{2,1,0:T(8,128)S(1)}, f32[32,8,128]{2,1,0:T(8,128)S(1)}, u32[]{:S(2)}, u32[]{:S(2)}) %collective-permute-start.18) | collective-permute-done | bytes 131104 | tf_op jit(solution)/shard_map/ppermute | solution.py:264
  190.3 2.5 %last_sweep.1 = f32[256,32,128]{2,1,0:T(8,128)} custom-call(f32[2,256]{1,0:T(2,128)S(1)} %get-tuple-element.76.kinetics, bf16[256,32]{1,0:T(8,128)(2,1)S(1)} %get-tuple-element.77.high, bf16[256,32]{1,0:T(8,128)(2,1)S(1)} %get-tuple-element.78.low, f32[32,8,128]{2,1,0:T(8,128)S(1)} %collective-permute-done.15.refs_0_, ...), custom_call_target="tpu_custom_call" | custom-call | flops 805306368 | bytes 6291456 | tf_op jit(solution)/shard_map/last_sweep/pallas_call | solution.py:316
  (97 shorter events, 21.7 us)
Async XLA Ops:
  11.0 11.6 %collective-permute-start.22 = (f32[32,8,128]{2,1,0:T(8,128)}, f32[32,8,128]{2,1,0:T(8,128)S(1)}, u32[]{:S(2)}, u32[]{:S(2)}) collective-permute-start(f32[32,8,128]{2,1,0:T(8,128)} %get-tuple-element.106), channel_id=1, source_target_pairs={{0,6},{1,7},{2,4},{3,5},{4,2},{5,3},{6,0},{7,1},{8,14},{9,15},{10,... | collective-permute-start | bytes 393224 | tf_op jit(solution)/shard_map/ppermute | solution.py:264
  11.6 13.9 %collective-permute-start.23 = (f32[32,8,128]{2,1,0:T(8,128)}, f32[32,8,128]{2,1,0:T(8,128)S(1)}, u32[]{:S(2)}, u32[]{:S(2)}) collective-permute-start(f32[32,8,128]{2,1,0:T(8,128)} %get-tuple-element.107), channel_id=1, source_target_pairs={{0,11},{1,10},{2,9},{3,8},{4,15},{5,14},{6,13},{7,12},{8,3},{9,2},... | collective-permute-start | bytes 393224 | tf_op jit(solution)/shard_map/ppermute | solution.py:264
  13.3 13.9 %collective-permute-start.24 = (f32[32,8,128]{2,1,0:T(8,128)}, f32[32,8,128]{2,1,0:T(8,128)S(1)}, u32[]{:S(2)}, u32[]{:S(2)}) collective-permute-start(f32[32,8,128]{2,1,0:T(8,128)} %get-tuple-element.108), channel_id=1, source_target_pairs={{0,5},{1,4},{2,7},{3,6},{4,1},{5,0},{6,3},{7,2},{8,13},{9,12},{10,... | collective-permute-start | bytes 393224 | tf_op jit(solution)/shard_map/ppermute | solution.py:264
  17.5 12.5 %collective-permute-start.25 = (f32[32,8,128]{2,1,0:T(8,128)}, f32[32,8,128]{2,1,0:T(8,128)S(1)}, u32[]{:S(2)}, u32[]{:S(2)}) collective-permute-start(f32[32,8,128]{2,1,0:T(8,128)} %get-tuple-element.109), channel_id=1, source_target_pairs={{0,10},{1,11},{2,8},{3,9},{4,14},{5,15},{6,12},{7,13},{8,2},{9,3},... | collective-permute-start | bytes 393224 | tf_op jit(solution)/shard_map/ppermute | solution.py:264
  19.3 18.6 %collective-permute-start.26 = (f32[32,8,128]{2,1,0:T(8,128)}, f32[32,8,128]{2,1,0:T(8,128)S(1)}, u32[]{:S(2)}, u32[]{:S(2)}) collective-permute-start(f32[32,8,128]{2,1,0:T(8,128)} %get-tuple-element.110), channel_id=1, source_target_pairs={{0,4},{1,5},{2,6},{3,7},{4,0},{5,1},{6,2},{7,3},{8,12},{9,13},{10,... | collective-permute-start | bytes 393224 | tf_op jit(solution)/shard_map/ppermute | solution.py:264
  22.6 20.6 %collective-permute-start.27 = (f32[32,8,128]{2,1,0:T(8,128)}, f32[32,8,128]{2,1,0:T(8,128)S(1)}, u32[]{:S(2)}, u32[]{:S(2)}) collective-permute-start(f32[32,8,128]{2,1,0:T(8,128)} %get-tuple-element.111), channel_id=1, source_target_pairs={{0,15},{1,14},{2,13},{3,12},{4,11},{5,10},{6,9},{7,8},{8,7},{9,6},... | collective-permute-start | bytes 393224 | tf_op jit(solution)/shard_map/ppermute | solution.py:264
  25.5 18.0 %collective-permute-start.28 = (f32[32,8,128]{2,1,0:T(8,128)}, f32[32,8,128]{2,1,0:T(8,128)S(1)}, u32[]{:S(2)}, u32[]{:S(2)}) collective-permute-start(f32[32,8,128]{2,1,0:T(8,128)} %get-tuple-element.112), channel_id=1, source_target_pairs={{0,3},{1,2},{2,1},{3,0},{4,7},{5,6},{6,5},{7,4},{8,11},{9,10},{10,... | collective-permute-start | bytes 393224 | tf_op jit(solution)/shard_map/ppermute | solution.py:264
  27.2 23.0 %collective-permute-start.29 = (f32[32,8,128]{2,1,0:T(8,128)}, f32[32,8,128]{2,1,0:T(8,128)S(1)}, u32[]{:S(2)}, u32[]{:S(2)}) collective-permute-start(f32[32,8,128]{2,1,0:T(8,128)} %get-tuple-element.113), channel_id=1, source_target_pairs={{0,14},{1,15},{2,12},{3,13},{4,10},{5,11},{6,8},{7,9},{8,6},{9,7},... | collective-permute-start | bytes 393224 | tf_op jit(solution)/shard_map/ppermute | solution.py:264
  30.0 20.3 %collective-permute-start.30 = (f32[32,8,128]{2,1,0:T(8,128)}, f32[32,8,128]{2,1,0:T(8,128)S(1)}, u32[]{:S(2)}, u32[]{:S(2)}) collective-permute-start(f32[32,8,128]{2,1,0:T(8,128)} %get-tuple-element.114), channel_id=1, source_target_pairs={{0,2},{1,3},{2,0},{3,1},{4,6},{5,7},{6,4},{7,5},{8,10},{9,11},{10,... | collective-permute-start | bytes 393224 | tf_op jit(solution)/shard_map/ppermute | solution.py:264
  37.9 14.3 %collective-permute-start.31 = (f32[32,8,128]{2,1,0:T(8,128)}, f32[32,8,128]{2,1,0:T(8,128)S(1)}, u32[]{:S(2)}, u32[]{:S(2)}) collective-permute-start(f32[32,8,128]{2,1,0:T(8,128)} %get-tuple-element.115), channel_id=1, source_target_pairs={{0,13},{1,12},{2,15},{3,14},{4,9},{5,8},{6,11},{7,10},{8,5},{9,4},... | collective-permute-start | bytes 393224 | tf_op jit(solution)/shard_map/ppermute | solution.py:264
  43.6 14.2 %collective-permute-start.33 = (f32[32,8,128]{2,1,0:T(8,128)}, f32[32,8,128]{2,1,0:T(8,128)S(1)}, u32[]{:S(2)}, u32[]{:S(2)}) collective-permute-start(f32[32,8,128]{2,1,0:T(8,128)} %get-tuple-element.117), channel_id=1, source_target_pairs={{0,12},{1,13},{2,14},{3,15},{4,8},{5,9},{6,10},{7,11},{8,4},{9,5},... | collective-permute-start | bytes 393224 | tf_op jit(solution)/shard_map/ppermute | solution.py:264
  50.3 14.8 %collective-permute-start.1 = (f32[32,8,128]{2,1,0:T(8,128)}, f32[32,8,128]{2,1,0:T(8,128)S(1)}, u32[]{:S(2)}, u32[]{:S(2)}) collective-permute-start(f32[32,8,128]{2,1,0:T(8,128)} %get-tuple-element.82), channel_id=1, source_target_pairs={{0,7},{1,6},{2,5},{3,4},{4,3},{5,2},{6,1},{7,0},{8,15},{9,14},{10,... | collective-permute-start | bytes 393224 | tf_op jit(solution)/shard_map/ppermute | solution.py:264
  52.2 13.1 %collective-permute-start.2 = (f32[32,8,128]{2,1,0:T(8,128)}, f32[32,8,128]{2,1,0:T(8,128)S(1)}, u32[]{:S(2)}, u32[]{:S(2)}) collective-permute-start(f32[32,8,128]{2,1,0:T(8,128)} %get-tuple-element.83), channel_id=1, source_target_pairs={{0,9},{1,8},{2,11},{3,10},{4,13},{5,12},{6,15},{7,14},{8,1},{9,0},... | collective-permute-start | bytes 393224 | tf_op jit(solution)/shard_map/ppermute | solution.py:264
  53.4 16.9 %collective-permute-start.3 = (f32[32,8,128]{2,1,0:T(8,128)}, f32[32,8,128]{2,1,0:T(8,128)S(1)}, u32[]{:S(2)}, u32[]{:S(2)}) collective-permute-start(f32[32,8,128]{2,1,0:T(8,128)} %get-tuple-element.84), channel_id=1, source_target_pairs={{0,6},{1,7},{2,4},{3,5},{4,2},{5,3},{6,0},{7,1},{8,14},{9,15},{10,... | collective-permute-start | bytes 393224 | tf_op jit(solution)/shard_map/ppermute | solution.py:264
  57.8 12.5 %collective-permute-start.4 = (f32[32,8,128]{2,1,0:T(8,128)}, f32[32,8,128]{2,1,0:T(8,128)S(1)}, u32[]{:S(2)}, u32[]{:S(2)}) collective-permute-start(f32[32,8,128]{2,1,0:T(8,128)} %get-tuple-element.85), channel_id=1, source_target_pairs={{0,11},{1,10},{2,9},{3,8},{4,15},{5,14},{6,13},{7,12},{8,3},{9,2},... | collective-permute-start | bytes 393224 | tf_op jit(solution)/shard_map/ppermute | solution.py:264
  58.7 18.1 %collective-permute-start.5 = (f32[32,8,128]{2,1,0:T(8,128)}, f32[32,8,128]{2,1,0:T(8,128)S(1)}, u32[]{:S(2)}, u32[]{:S(2)}) collective-permute-start(f32[32,8,128]{2,1,0:T(8,128)} %get-tuple-element.86), channel_id=1, source_target_pairs={{0,5},{1,4},{2,7},{3,6},{4,1},{5,0},{6,3},{7,2},{8,13},{9,12},{10,... | collective-permute-start | bytes 393224 | tf_op jit(solution)/shard_map/ppermute | solution.py:264
  65.1 12.9 %collective-permute-start.6 = (f32[32,8,128]{2,1,0:T(8,128)}, f32[32,8,128]{2,1,0:T(8,128)S(1)}, u32[]{:S(2)}, u32[]{:S(2)}) collective-permute-start(f32[32,8,128]{2,1,0:T(8,128)} %get-tuple-element.87), channel_id=1, source_target_pairs={{0,10},{1,11},{2,8},{3,9},{4,14},{5,15},{6,12},{7,13},{8,2},{9,3},... | collective-permute-start | bytes 393224 | tf_op jit(solution)/shard_map/ppermute | solution.py:264
  65.3 15.2 %collective-permute-start.7 = (f32[32,8,128]{2,1,0:T(8,128)}, f32[32,8,128]{2,1,0:T(8,128)S(1)}, u32[]{:S(2)}, u32[]{:S(2)}) collective-permute-start(f32[32,8,128]{2,1,0:T(8,128)} %get-tuple-element.88), channel_id=1, source_target_pairs={{0,4},{1,5},{2,6},{3,7},{4,0},{5,1},{6,2},{7,3},{8,12},{9,13},{10,... | collective-permute-start | bytes 393224 | tf_op jit(solution)/shard_map/ppermute | solution.py:264
  70.3 13.8 %collective-permute-start.8 = (f32[32,8,128]{2,1,0:T(8,128)}, f32[32,8,128]{2,1,0:T(8,128)S(1)}, u32[]{:S(2)}, u32[]{:S(2)}) collective-permute-start(f32[32,8,128]{2,1,0:T(8,128)} %get-tuple-element.89), channel_id=1, source_target_pairs={{0,15},{1,14},{2,13},{3,12},{4,11},{5,10},{6,9},{7,8},{8,7},{9,6},... | collective-permute-start | bytes 393224 | tf_op jit(solution)/shard_map/ppermute | solution.py:264
  70.3 14.3 %collective-permute-start.9 = (f32[32,8,128]{2,1,0:T(8,128)}, f32[32,8,128]{2,1,0:T(8,128)S(1)}, u32[]{:S(2)}, u32[]{:S(2)}) collective-permute-start(f32[32,8,128]{2,1,0:T(8,128)} %get-tuple-element.90), channel_id=1, source_target_pairs={{0,3},{1,2},{2,1},{3,0},{4,7},{5,6},{6,5},{7,4},{8,11},{9,10},{10,... | collective-permute-start | bytes 393224 | tf_op jit(solution)/shard_map/ppermute | solution.py:264
  76.8 18.5 %collective-permute-start.10 = (f32[32,8,128]{2,1,0:T(8,128)}, f32[32,8,128]{2,1,0:T(8,128)S(1)}, u32[]{:S(2)}, u32[]{:S(2)}) collective-permute-start(f32[32,8,128]{2,1,0:T(8,128)} %get-tuple-element.91), channel_id=1, source_target_pairs={{0,14},{1,15},{2,12},{3,13},{4,10},{5,11},{6,8},{7,9},{8,6},{9,7},... | collective-permute-start | bytes 393224 | tf_op jit(solution)/shard_map/ppermute | solution.py:264
  78.0 17.3 %collective-permute-start.11 = (f32[32,8,128]{2,1,0:T(8,128)}, f32[32,8,128]{2,1,0:T(8,128)S(1)}, u32[]{:S(2)}, u32[]{:S(2)}) collective-permute-start(f32[32,8,128]{2,1,0:T(8,128)} %get-tuple-element.92), channel_id=1, source_target_pairs={{0,2},{1,3},{2,0},{3,1},{4,6},{5,7},{6,4},{7,5},{8,10},{9,11},{10,... | collective-permute-start | bytes 393224 | tf_op jit(solution)/shard_map/ppermute | solution.py:264
  80.5 16.7 %collective-permute-start.12 = (f32[32,8,128]{2,1,0:T(8,128)}, f32[32,8,128]{2,1,0:T(8,128)S(1)}, u32[]{:S(2)}, u32[]{:S(2)}) collective-permute-start(f32[32,8,128]{2,1,0:T(8,128)} %get-tuple-element.93), channel_id=1, source_target_pairs={{0,13},{1,12},{2,15},{3,14},{4,9},{5,8},{6,11},{7,10},{8,5},{9,4},... | collective-permute-start | bytes 393224 | tf_op jit(solution)/shard_map/ppermute | solution.py:264
  84.1 14.4 %collective-permute-start.13 = (f32[32,8,128]{2,1,0:T(8,128)}, f32[32,8,128]{2,1,0:T(8,128)S(1)}, u32[]{:S(2)}, u32[]{:S(2)}) collective-permute-start(f32[32,8,128]{2,1,0:T(8,128)} %get-tuple-element.94), channel_id=1, source_target_pairs={{0,1},{1,0},{2,3},{3,2},{4,5},{5,4},{6,7},{7,6},{8,9},{9,8},{10,11... | collective-permute-start | bytes 393224 | tf_op jit(solution)/shard_map/ppermute | solution.py:264
  84.5 18.3 %collective-permute-start.14 = (f32[32,8,128]{2,1,0:T(8,128)}, f32[32,8,128]{2,1,0:T(8,128)S(1)}, u32[]{:S(2)}, u32[]{:S(2)}) collective-permute-start(f32[32,8,128]{2,1,0:T(8,128)} %get-tuple-element.95), channel_id=1, source_target_pairs={{0,12},{1,13},{2,14},{3,15},{4,8},{5,9},{6,10},{7,11},{8,4},{9,5},... | collective-permute-start | bytes 393224 | tf_op jit(solution)/shard_map/ppermute | solution.py:264
  95.3 14.8 %collective-permute-start.35 = (f32[32,8,128]{2,1,0:T(8,128)S(1)}, f32[32,8,128]{2,1,0:T(8,128)S(1)}, u32[]{:S(2)}, u32[]{:S(2)}) collective-permute-start(f32[32,8,128]{2,1,0:T(8,128)S(1)} %get-tuple-element.120), channel_id=1, source_target_pairs={{0,7},{1,6},{2,5},{3,4},{4,3},{5,2},{6,1},{7,0},{8,15},{9,14},{10,... | collective-permute-start | bytes 393224 | tf_op jit(solution)/shard_map/ppermute | solution.py:264
  97.3 13.0 %collective-permute-start.36 = (f32[32,8,128]{2,1,0:T(8,128)S(1)}, f32[32,8,128]{2,1,0:T(8,128)S(1)}, u32[]{:S(2)}, u32[]{:S(2)}) collective-permute-start(f32[32,8,128]{2,1,0:T(8,128)S(1)} %get-tuple-element.121), channel_id=1, source_target_pairs={{0,9},{1,8},{2,11},{3,10},{4,13},{5,12},{6,15},{7,14},{8,1},{9,0},... | collective-permute-start | bytes 393224 | tf_op jit(solution)/shard_map/ppermute | solution.py:264
  98.5 16.8 %collective-permute-start.37 = (f32[32,8,128]{2,1,0:T(8,128)S(1)}, f32[32,8,128]{2,1,0:T(8,128)S(1)}, u32[]{:S(2)}, u32[]{:S(2)}) collective-permute-start(f32[32,8,128]{2,1,0:T(8,128)S(1)} %get-tuple-element.122), channel_id=1, source_target_pairs={{0,6},{1,7},{2,4},{3,5},{4,2},{5,3},{6,0},{7,1},{8,14},{9,15},{10,... | collective-permute-start | bytes 393224 | tf_op jit(solution)/shard_map/ppermute | solution.py:264
  102.9 12.4 %collective-permute-start.38 = (f32[32,8,128]{2,1,0:T(8,128)S(1)}, f32[32,8,128]{2,1,0:T(8,128)S(1)}, u32[]{:S(2)}, u32[]{:S(2)}) collective-permute-start(f32[32,8,128]{2,1,0:T(8,128)S(1)} %get-tuple-element.123), channel_id=1, source_target_pairs={{0,11},{1,10},{2,9},{3,8},{4,15},{5,14},{6,13},{7,12},{8,3},{9,2},... | collective-permute-start | bytes 393224 | tf_op jit(solution)/shard_map/ppermute | solution.py:264
  102.9 16.4 %collective-permute-start.39 = (f32[32,8,128]{2,1,0:T(8,128)S(1)}, f32[32,8,128]{2,1,0:T(8,128)S(1)}, u32[]{:S(2)}, u32[]{:S(2)}) collective-permute-start(f32[32,8,128]{2,1,0:T(8,128)S(1)} %get-tuple-element.124), channel_id=1, source_target_pairs={{0,5},{1,4},{2,7},{3,6},{4,1},{5,0},{6,3},{7,2},{8,13},{9,12},{10,... | collective-permute-start | bytes 393224 | tf_op jit(solution)/shard_map/ppermute | solution.py:264
  110.3 14.7 %collective-permute-start.41 = (f32[32,8,128]{2,1,0:T(8,128)S(1)}, f32[32,8,128]{2,1,0:T(8,128)S(1)}, u32[]{:S(2)}, u32[]{:S(2)}) collective-permute-start(f32[32,8,128]{2,1,0:T(8,128)S(1)} %get-tuple-element.126), channel_id=1, source_target_pairs={{0,4},{1,5},{2,6},{3,7},{4,0},{5,1},{6,2},{7,3},{8,12},{9,13},{10,... | collective-permute-start | bytes 393224 | tf_op jit(solution)/shard_map/ppermute | solution.py:264
  115.3 16.6 %collective-permute-start.42 = (f32[32,8,128]{2,1,0:T(8,128)S(1)}, f32[32,8,128]{2,1,0:T(8,128)S(1)}, u32[]{:S(2)}, u32[]{:S(2)}) collective-permute-start(f32[32,8,128]{2,1,0:T(8,128)S(1)} %get-tuple-element.127), channel_id=1, source_target_pairs={{0,15},{1,14},{2,13},{3,12},{4,11},{5,10},{6,9},{7,8},{8,7},{9,6},... | collective-permute-start | bytes 393224 | tf_op jit(solution)/shard_map/ppermute | solution.py:264
  115.3 17.0 %collective-permute-start.43 = (f32[32,8,128]{2,1,0:T(8,128)S(1)}, f32[32,8,128]{2,1,0:T(8,128)S(1)}, u32[]{:S(2)}, u32[]{:S(2)}) collective-permute-start(f32[32,8,128]{2,1,0:T(8,128)S(1)} %get-tuple-element.128), channel_id=1, source_target_pairs={{0,3},{1,2},{2,1},{3,0},{4,7},{5,6},{6,5},{7,4},{8,11},{9,10},{10,... | collective-permute-start | bytes 393224 | tf_op jit(solution)/shard_map/ppermute | solution.py:264
  119.3 20.3 %collective-permute-start.44 = (f32[32,8,128]{2,1,0:T(8,128)S(1)}, f32[32,8,128]{2,1,0:T(8,128)S(1)}, u32[]{:S(2)}, u32[]{:S(2)}) collective-permute-start(f32[32,8,128]{2,1,0:T(8,128)S(1)} %get-tuple-element.129), channel_id=1, source_target_pairs={{0,14},{1,15},{2,12},{3,13},{4,10},{5,11},{6,8},{7,9},{8,6},{9,7},... | collective-permute-start | bytes 393224 | tf_op jit(solution)/shard_map/ppermute | solution.py:264
  120.5 22.1 %collective-permute-start.45 = (f32[32,8,128]{2,1,0:T(8,128)S(1)}, f32[32,8,128]{2,1,0:T(8,128)S(1)}, u32[]{:S(2)}, u32[]{:S(2)}) collective-permute-start(f32[32,8,128]{2,1,0:T(8,128)S(1)} %get-tuple-element.130), channel_id=1, source_target_pairs={{0,2},{1,3},{2,0},{3,1},{4,6},{5,7},{6,4},{7,5},{8,10},{9,11},{10,... | collective-permute-start | bytes 393224 | tf_op jit(solution)/shard_map/ppermute | solution.py:264
  125.0 19.2 %collective-permute-start.46 = (f32[32,8,128]{2,1,0:T(8,128)S(1)}, f32[32,8,128]{2,1,0:T(8,128)S(1)}, u32[]{:S(2)}, u32[]{:S(2)}) collective-permute-start(f32[32,8,128]{2,1,0:T(8,128)S(1)} %get-tuple-element.131), channel_id=1, source_target_pairs={{0,13},{1,12},{2,15},{3,14},{4,9},{5,8},{6,11},{7,10},{8,5},{9,4},... | collective-permute-start | bytes 393224 | tf_op jit(solution)/shard_map/ppermute | solution.py:264
  131.9 14.2 %collective-permute-start.47 = (f32[32,8,128]{2,1,0:T(8,128)S(1)}, f32[32,8,128]{2,1,0:T(8,128)S(1)}, u32[]{:S(2)}, u32[]{:S(2)}) collective-permute-start(f32[32,8,128]{2,1,0:T(8,128)S(1)} %get-tuple-element.132), channel_id=1, source_target_pairs={{0,1},{1,0},{2,3},{3,2},{4,5},{5,4},{6,7},{7,6},{8,9},{9,8},{10,11... | collective-permute-start | bytes 393224 | tf_op jit(solution)/shard_map/ppermute | solution.py:264
  132.3 15.6 %collective-permute-start.48 = (f32[32,8,128]{2,1,0:T(8,128)S(1)}, f32[32,8,128]{2,1,0:T(8,128)S(1)}, u32[]{:S(2)}, u32[]{:S(2)}) collective-permute-start(f32[32,8,128]{2,1,0:T(8,128)S(1)} %get-tuple-element.133), channel_id=1, source_target_pairs={{0,12},{1,13},{2,14},{3,15},{4,8},{5,9},{6,10},{7,11},{8,4},{9,5},... | collective-permute-start | bytes 393224 | tf_op jit(solution)/shard_map/ppermute | solution.py:264
  142.7 12.6 %collective-permute-start.50 = (f32[32,8,128]{2,1,0:T(8,128)S(1)}, f32[32,8,128]{2,1,0:T(8,128)S(1)}, u32[]{:S(2)}, u32[]{:S(2)}) collective-permute-start(f32[32,8,128]{2,1,0:T(8,128)S(1)} %get-tuple-element.136), channel_id=1, source_target_pairs={{0,7},{1,6},{2,5},{3,4},{4,3},{5,2},{6,1},{7,0},{8,15},{9,14},{10,... | collective-permute-start | bytes 393224 | tf_op jit(solution)/shard_map/ppermute | solution.py:264
  146.1 14.3 %collective-permute-start.52 = (f32[32,8,128]{2,1,0:T(8,128)S(1)}, f32[32,8,128]{2,1,0:T(8,128)S(1)}, u32[]{:S(2)}, u32[]{:S(2)}) collective-permute-start(f32[32,8,128]{2,1,0:T(8,128)S(1)} %get-tuple-element.138), channel_id=1, source_target_pairs={{0,6},{1,7},{2,4},{3,5},{4,2},{5,3},{6,0},{7,1},{8,14},{9,15},{10,... | collective-permute-start | bytes 393224 | tf_op jit(solution)/shard_map/ppermute | solution.py:264
  147.9 12.5 %collective-permute-start.53 = (f32[32,8,128]{2,1,0:T(8,128)S(1)}, f32[32,8,128]{2,1,0:T(8,128)S(1)}, u32[]{:S(2)}, u32[]{:S(2)}) collective-permute-start(f32[32,8,128]{2,1,0:T(8,128)S(1)} %get-tuple-element.139), channel_id=1, source_target_pairs={{0,11},{1,10},{2,9},{3,8},{4,15},{5,14},{6,13},{7,12},{8,3},{9,2},... | collective-permute-start | bytes 393224 | tf_op jit(solution)/shard_map/ppermute | solution.py:264
  148.9 13.3 %collective-permute-start.54 = (f32[32,8,128]{2,1,0:T(8,128)S(1)}, f32[32,8,128]{2,1,0:T(8,128)S(1)}, u32[]{:S(2)}, u32[]{:S(2)}) collective-permute-start(f32[32,8,128]{2,1,0:T(8,128)S(1)} %get-tuple-element.140), channel_id=1, source_target_pairs={{0,5},{1,4},{2,7},{3,6},{4,1},{5,0},{6,3},{7,2},{8,13},{9,12},{10,... | collective-permute-start | bytes 393224 | tf_op jit(solution)/shard_map/ppermute | solution.py:264
  160.4 16.5 %collective-permute-start.57 = (f32[32,8,128]{2,1,0:T(8,128)S(1)}, f32[32,8,128]{2,1,0:T(8,128)S(1)}, u32[]{:S(2)}, u32[]{:S(2)}) collective-permute-start(f32[32,8,128]{2,1,0:T(8,128)S(1)} %get-tuple-element.143), channel_id=1, source_target_pairs={{0,15},{1,14},{2,13},{3,12},{4,11},{5,10},{6,9},{7,8},{8,7},{9,6},... | collective-permute-start | bytes 393224 | tf_op jit(solution)/shard_map/ppermute | solution.py:264
  160.4 16.9 %collective-permute-start.58 = (f32[32,8,128]{2,1,0:T(8,128)S(1)}, f32[32,8,128]{2,1,0:T(8,128)S(1)}, u32[]{:S(2)}, u32[]{:S(2)}) collective-permute-start(f32[32,8,128]{2,1,0:T(8,128)S(1)} %get-tuple-element.144), channel_id=1, source_target_pairs={{0,3},{1,2},{2,1},{3,0},{4,7},{5,6},{6,5},{7,4},{8,11},{9,10},{10,... | collective-permute-start | bytes 393224 | tf_op jit(solution)/shard_map/ppermute | solution.py:264
  162.2 17.5 %collective-permute-start.59 = (f32[32,8,128]{2,1,0:T(8,128)S(1)}, f32[32,8,128]{2,1,0:T(8,128)S(1)}, u32[]{:S(2)}, u32[]{:S(2)}) collective-permute-start(f32[32,8,128]{2,1,0:T(8,128)S(1)} %get-tuple-element.145), channel_id=1, source_target_pairs={{0,14},{1,15},{2,12},{3,13},{4,10},{5,11},{6,8},{7,9},{8,6},{9,7},... | collective-permute-start | bytes 393224 | tf_op jit(solution)/shard_map/ppermute | solution.py:264
  165.5 16.9 %collective-permute-start.15 = (f32[32,8,128]{2,1,0:T(8,128)S(1)}, f32[32,8,128]{2,1,0:T(8,128)S(1)}, u32[]{:S(2)}, u32[]{:S(2)}) collective-permute-start(f32[32,8,128]{2,1,0:T(8,128)S(1)} %get-tuple-element.97), channel_id=1, source_target_pairs={{0,2},{1,3},{2,0},{3,1},{4,6},{5,7},{6,4},{7,5},{8,10},{9,11},{10,... | collective-permute-start | bytes 393224 | tf_op jit(solution)/shard_map/ppermute | solution.py:264
  166.8 20.6 %collective-permute-start.16 = (f32[32,8,128]{2,1,0:T(8,128)S(1)}, f32[32,8,128]{2,1,0:T(8,128)S(1)}, u32[]{:S(2)}, u32[]{:S(2)}) collective-permute-start(f32[32,8,128]{2,1,0:T(8,128)S(1)} %get-tuple-element.98), channel_id=1, source_target_pairs={{0,13},{1,12},{2,15},{3,14},{4,9},{5,8},{6,11},{7,10},{8,5},{9,4},... | collective-permute-start | bytes 393224 | tf_op jit(solution)/shard_map/ppermute | solution.py:264
  177.3 13.0 %collective-permute-start.18 = (f32[32,8,128]{2,1,0:T(8,128)S(1)}, f32[32,8,128]{2,1,0:T(8,128)S(1)}, u32[]{:S(2)}, u32[]{:S(2)}) collective-permute-start(f32[32,8,128]{2,1,0:T(8,128)S(1)} %get-tuple-element.100), channel_id=1, source_target_pairs={{0,12},{1,13},{2,14},{3,15},{4,8},{5,9},{6,10},{7,11},{8,4},{9,5},... | collective-permute-start | bytes 393224 | tf_op jit(solution)/shard_map/ppermute | solution.py:264
  (21 other events, 760.3 us)
